TPU v7x, 32 devices: a whole 2x2x4 slice. The times are simulated.
32 devices in a mesh: row: 2 (over x), col: 16 (over z, y, core).
Axes of the slice: x: 2, y: 2, z: 4, core: 2. Of those that a mesh axis runs over, the one named last changes fastest.
Arguments:
- features: float32 [16, 1024, 128], P('col'), may hold values from -6 to 6
- self_weight: float32 [128, 256], replicated, may hold values from -0.5 to 0.5
- neigh_weight: float32 [128, 256], replicated, may hold values from -0.5 to 0.5
- bias: float32 [256], replicated, may hold values from -4 to 4
- edge_tiles: bfloat16 [2, 16, 96, 128, 128], P('row', 'col'), may hold values from -0.15625 to 0.15625
- tile_rows: int32 [2, 16, 96], P('row', 'col'), may hold values from 0 to 7
- tile_cols: int32 [2, 16, 96], P('row', 'col'), may hold values from 0 to 7
- tile_count: int32 [2, 16, 8], P('row', 'col'), may hold values from 1 to 12, as said below
- cotangent: float32 [16, 1024, 256], P('col', 'row'), may hold values from -6 to 6
Outputs:
- output: float32 [16, 1024, 256], P('col', 'row')
- grad_self: float32 [128, 256], replicated
- grad_neigh: float32 [128, 256], replicated
- grad_bias: float32 [256], replicated
Inputs may be any that keep to these rules, and one draw needn't show every extreme that they name: tile_count reaches 12 in every draw.
All inputs are finite; a program needn't handle non-finite values.
Results may differ from a plain program's by a relative error of at most 0.0003.
Values sent between devices are 32-bit elements; how exact they have to be, the bound alone decides.
No kernel may reach another device: no remote copies, remote signals or barrier semaphores. Data moves between devices by JAX's collectives and lax.ppermute only.
A program may use at most 64 MiB of HBM per device.

v0:
```python
import jax
import jax.numpy as jnp
from jax import lax
from jax.sharding import PartitionSpec as P


def shifted(value, axis, steps):
    count = lax.axis_size(axis)
    pairs = [(source, (source + steps) % count) for source in range(count)]
    return lax.ppermute(value, axis, pairs)


def layer(params, own, agg):
    self_weight, neigh_weight, bias = params
    pre = (
        jnp.dot(own, self_weight, precision=lax.Precision.HIGHEST)
        + jnp.dot(agg, neigh_weight, precision=lax.Precision.HIGHEST)
        + bias
    )
    hidden = jax.nn.gelu(pre, approximate=True)
    scale = lax.rsqrt(jnp.mean(hidden * hidden, axis=-1, keepdims=True) + 1e-06)
    return hidden * scale


def stop_product(block, tiles, rows_idx, cols_idx, count):
    slots = tiles.shape[0]
    side = tiles.shape[-1]
    width = block.shape[1]
    across = block.shape[0] // side
    pieces = block.reshape(across, side, width)
    positions = jnp.arange(across, dtype=jnp.int32)
    col_hot = (cols_idx[:, None] == positions[None, :]).astype(jnp.float32)
    chosen = jnp.einsum("tk,kjd->tjd", col_hot, pieces, precision=lax.Precision.HIGHEST)
    live = (jnp.arange(slots, dtype=jnp.int32) < count).astype(jnp.float32)
    weights = tiles.astype(jnp.float32) * live[:, None, None]
    prod = jnp.einsum("tij,tjd->tid", weights, chosen, precision=lax.Precision.HIGHEST)
    row_hot = (rows_idx[:, None] == positions[None, :]).astype(jnp.float32)
    summed = jnp.einsum("tk,tid->kid", row_hot, prod, precision=lax.Precision.HIGHEST)
    return summed.reshape(across * side, width)


def on_device(
    features,
    self_weight,
    neigh_weight,
    bias,
    edge_tiles,
    tile_rows,
    tile_cols,
    tile_count,
    cotangent,
):
    row_count = lax.axis_size("row")
    col_count = lax.axis_size("col")
    stops = col_count // row_count
    row_index = lax.axis_index("row")
    block = features[0]
    walking = block
    current = block
    for step in range(1, row_count):
        walking = shifted(walking, "col", stops)
        current = jnp.where(row_index == step, walking, current)
    tiles = edge_tiles[0, 0].reshape(stops, -1, edge_tiles.shape[3], edge_tiles.shape[4])
    rows_all = tile_rows[0, 0].reshape(stops, -1)
    cols_all = tile_cols[0, 0].reshape(stops, -1)
    counts = tile_count[0, 0]
    total = stop_product(current, tiles[0], rows_all[0], cols_all[0], counts[0])

    def visit(carry, stop_data):
        held, running = carry
        tiles_s, rows_s, cols_s, count_s = stop_data
        held = shifted(held, "col", 1)
        running = running + stop_product(held, tiles_s, rows_s, cols_s, count_s)
        return ((held, running), None)

    (current, total), _ = lax.scan(
        visit, (current, total), (tiles[1:], rows_all[1:], cols_all[1:], counts[1:])
    )
    params = (self_weight, neigh_weight, bias)
    share = cotangent.shape[1]
    aggregate = lax.psum_scatter(total, "row", scatter_dimension=0, tiled=True)
    own = lax.dynamic_slice_in_dim(block, row_index * share, share, 0)
    output, pullback = jax.vjp(lambda p: layer(p, own, aggregate), params)
    grads = pullback(cotangent[0])[0]
    grad_s, grad_n, grad_b = lax.psum((grads[0], grads[1], grads[2]), ("row", "col"))
    return (output[None], grad_s, grad_n, grad_b)


def solution(mesh):
    in_specs = (
        P("col", None, None),
        P(),
        P(),
        P(),
        P("row", "col", None, None, None),
        P("row", "col", None),
        P("row", "col", None),
        P("row", "col", None),
        P("col", "row", None),
    )
    out_specs = (P("col", "row", None), P(), P(), P())
    return jax.shard_map(
        on_device, mesh=mesh, in_specs=in_specs, out_specs=out_specs, check_vma=False
    )
```

profile of v0, /device:TPU:0, one launch (start us, length us, event | category | flops | bytes accessed | tf_op | source)
XLA Modules:
  0.0 302.0 jit_solution(3939419926362653314)
XLA Ops:
  7.3 4.1 %collective-permute-start.1 = (f32[1024,128]{1,0:T(8,128)}, f32[1024,128]{1,0:T(8,128)S(1)}, u32[]{:S(2)}, u32[]{:S(2)}) collective-permute-start(f32[1024,128]{1,0:T(8,128)} %bitcast.85), channel_id=1, source_target_pairs={{0,8},{1,9},{2,10},{3,11},{4,12},{5,13},{6,14},{7,15},{8,0},{9,1},... | collective-permute-start | bytes 1572872 | tf_op jit(solution)/shard_map/ppermute | solution.py:10
  12.9 3.7 %slice.46 = bf16[1,1,84,128,128]{4,3,2,1,0:T(8,128)(2,1)} slice(bf16[1,1,96,128,128]{4,3,2,1,0:T(8,128)(2,1)} %param.15), slice={[0:1], [0:1], [12:96], [0:128], [0:128]} | slice | bytes 5505024 | tf_op jit(solution)/shard_map/slice | solution.py:77
  16.8 18.0 %collective-permute-done.1 = f32[1024,128]{1,0:T(8,128)S(1)} collective-permute-done((f32[1024,128]{1,0:T(8,128)}, f32[1024,128]{1,0:T(8,128)S(1)}, u32[]{:S(2)}, u32[]{:S(2)}) %collective-permute-start.1) | collective-permute-done | bytes 524320 | tf_op jit(solution)/shard_map/ppermute | solution.py:10
  35.6 2.1 fusion.21
  38.7 107.9 %while.12 = (s32[]{:T(128)}, f32[1024,128]{1,0:T(8,128)S(1)}, f32[1024,128]{1,0:T(8,128)S(1)}, s32[7,12]{1,0:T(8,128)S(1)}, bf16[7,12,128,128]{3,2,1,0:T(8,128)(...) while((s32[]{:T(128)}, f32[1024,128]{1,0:T(8,128)S(1)}, f32[1024,128]{1,0:T(8,128)S(1)}, ...), condition=%wide.region_1.2_spmd, body=%wide.region_0.1_spmd.sunk | while | flops 340263136 | bytes 10355229 | solution.py:76
  40.1 10.0 %collective-permute-done = f32[1024,128]{1,0:T(8,128)S(1)} collective-permute-done((f32[1024,128]{1,0:T(8,128)S(1)}, f32[1024,128]{1,0:T(8,128)S(1)}, u32[]{:S(2)}, u32[]{:S(2)}) %collective-permute-start) | collective-permute-done | bytes 524320 | tf_op jit(solution)/shard_map/while/body/eval_jaxpr/ppermute | solution.py:10
  50.9 2.1 fusion.75
  55.5 10.0 %collective-permute-done = f32[1024,128]{1,0:T(8,128)S(1)} collective-permute-done((f32[1024,128]{1,0:T(8,128)S(1)}, f32[1024,128]{1,0:T(8,128)S(1)}, u32[]{:S(2)}, u32[]{:S(2)}) %collective-permute-start) | collective-permute-done | bytes 524320 | tf_op jit(solution)/shard_map/while/body/eval_jaxpr/ppermute | solution.py:10
  66.3 2.1 fusion.75
  70.9 10.0 %collective-permute-done = f32[1024,128]{1,0:T(8,128)S(1)} collective-permute-done((f32[1024,128]{1,0:T(8,128)S(1)}, f32[1024,128]{1,0:T(8,128)S(1)}, u32[]{:S(2)}, u32[]{:S(2)}) %collective-permute-start) | collective-permute-done | bytes 524320 | tf_op jit(solution)/shard_map/while/body/eval_jaxpr/ppermute | solution.py:10
  81.8 2.1 fusion.75
  86.3 10.0 %collective-permute-done = f32[1024,128]{1,0:T(8,128)S(1)} collective-permute-done((f32[1024,128]{1,0:T(8,128)S(1)}, f32[1024,128]{1,0:T(8,128)S(1)}, u32[]{:S(2)}, u32[]{:S(2)}) %collective-permute-start) | collective-permute-done | bytes 524320 | tf_op jit(solution)/shard_map/while/body/eval_jaxpr/ppermute | solution.py:10
  97.2 2.1 fusion.75
  101.8 10.0 %collective-permute-done = f32[1024,128]{1,0:T(8,128)S(1)} collective-permute-done((f32[1024,128]{1,0:T(8,128)S(1)}, f32[1024,128]{1,0:T(8,128)S(1)}, u32[]{:S(2)}, u32[]{:S(2)}) %collective-permute-start) | collective-permute-done | bytes 524320 | tf_op jit(solution)/shard_map/while/body/eval_jaxpr/ppermute | solution.py:10
  112.6 2.1 fusion.75
  117.2 10.0 %collective-permute-done = f32[1024,128]{1,0:T(8,128)S(1)} collective-permute-done((f32[1024,128]{1,0:T(8,128)S(1)}, f32[1024,128]{1,0:T(8,128)S(1)}, u32[]{:S(2)}, u32[]{:S(2)}) %collective-permute-start) | collective-permute-done | bytes 524320 | tf_op jit(solution)/shard_map/while/body/eval_jaxpr/ppermute | solution.py:10
  128.0 2.1 fusion.75
  132.6 10.0 %collective-permute-done = f32[1024,128]{1,0:T(8,128)S(1)} collective-permute-done((f32[1024,128]{1,0:T(8,128)S(1)}, f32[1024,128]{1,0:T(8,128)S(1)}, u32[]{:S(2)}, u32[]{:S(2)}) %collective-permute-start) | collective-permute-done | bytes 524320 | tf_op jit(solution)/shard_map/while/body/eval_jaxpr/ppermute | solution.py:10
  143.4 2.1 fusion.75
  148.4 11.1 %reduce-scatter.2.cloned.1.call-done = f32[512,128]{1,0:T(8,128)} async-done(((f32[1024,128]{1,0:T(8,128)}), f32[512,128]{1,0:T(8,128)}) %reduce-scatter.2.cloned.1.call-update) | async-done | bytes 262160 | tf_op jit(solution)/shard_map/reduce_scatter | solution.py:81
  159.5 1.9 fusion.29
  165.5 39.4 %psum.23 = f32[256]{0:T(256)} all-reduce(f32[256]{0:T(256)S(1)} %get-tuple-element.68), channel_id=1, replica_groups=mesh['row'=2,'col'=16] {'row','col'}, use_global_device_ids=true, to_apply=%region_8.9 | all-reduce | flops 256 | bytes 2048 | tf_op jit(solution)/shard_map/psum | solution.py:85
  204.9 87.2 %all-reduce.3.cloned.1.call-done = (f32[128,256]{1,0:T(8,128)}, f32[128,256]{1,0:T(8,128)}) async-done(((f32[128,256]{1,0:T(8,128)}, f32[128,256]{1,0:T(8,128)}), (f32[128,256]{1,0:T(8,128)}, f32[128,256]{1,0:T(8,128)})) %all-reduce.3.cloned.1.call-update) | async-done | bytes 262160 | tf_op jit(solution)/shard_map/psum | solution.py:85
  292.0 1.6 copy.56
  (104 shorter events, 33.4 us)
Async XLA Ops:
  7.2 152.4 %copy-start = (f32[128,256]{1,0:T(8,128)S(1)}, f32[128,256]{1,0:T(8,128)}, u32[]{:S(2)}) copy-start(f32[128,256]{1,0:T(8,128)} %param.13) | copy-start | bytes 393220
  7.2 27.6 %copy-start.2 = (f32[1,1024,128]{2,1,0:T(8,128)S(1)}, f32[1,1024,128]{2,1,0:T(8,128)}, u32[]{:S(2)}) copy-start(f32[1,1024,128]{2,1,0:T(8,128)} %param.11) | copy-start | bytes 1572868
  7.2 9.5 %copy-start.6 = (s32[1,1,96]{2,1,0:T(1,128)S(1)}, s32[1,1,96]{2,1,0:T(1,128)}, u32[]{:S(2)}) copy-start(s32[1,1,96]{2,1,0:T(1,128)} %param.16) | copy-start | bytes 1156
  7.2 9.4 %copy-start.8 = (s32[1,1,8]{2,1,0:T(1,128)S(1)}, s32[1,1,8]{2,1,0:T(1,128)}, u32[]{:S(2)}) copy-start(s32[1,1,8]{2,1,0:T(1,128)} %param.18) | copy-start | bytes 100
  7.2 152.3 %reduce-scatter.2.cloned.1.call-start = ((), (), s32[]{:S(2)}) async-start(), calls=%async_computation.1 | async-start | bytes 786432 | tf_op jit(solution)/shard_map/reduce_scatter | solution.py:81
  7.3 27.5 %collective-permute-start.1 = (f32[1024,128]{1,0:T(8,128)}, f32[1024,128]{1,0:T(8,128)S(1)}, u32[]{:S(2)}, u32[]{:S(2)}) collective-permute-start(f32[1024,128]{1,0:T(8,128)} %bitcast.85), channel_id=1, source_target_pairs={{0,8},{1,9},{2,10},{3,11},{4,12},{5,13},{6,14},{7,15},{8,0},{9,1},... | collective-permute-start | bytes 1572872 | tf_op jit(solution)/shard_map/ppermute | solution.py:10
  38.7 108.9 %copy-start.3 = (f32[1,512,256]{2,1,0:T(8,128)S(1)}, f32[1,512,256]{2,1,0:T(8,128)}, u32[]{:S(2)}) copy-start(f32[1,512,256]{2,1,0:T(8,128)} %param.19) | copy-start | bytes 1572868
  38.7 109.1 %copy-start.5 = (f32[128,256]{1,0:T(8,128)S(1)}, f32[128,256]{1,0:T(8,128)}, u32[]{:S(2)}) copy-start(f32[128,256]{1,0:T(8,128)} %param.12) | copy-start | bytes 393220
  38.7 120.8 %copy-start.7 = (f32[256]{0:T(256)S(1)}, f32[256]{0:T(256)}, u32[]{:S(2)}) copy-start(f32[256]{0:T(256)} %param.14) | copy-start | bytes 3076
  38.8 11.4 %collective-permute-start = (f32[1024,128]{1,0:T(8,128)S(1)}, f32[1024,128]{1,0:T(8,128)S(1)}, u32[]{:S(2)}, u32[]{:S(2)}) collective-permute-start(f32[1024,128]{1,0:T(8,128)S(1)} %get-tuple-element.134), channel_id=1, source_target_pairs={{0,1},{1,2},{2,3},{3,4},{4,5},{5,6},{6,7},{7,8},{8,9},{9,10},{10,1... | collective-permute-start | bytes 1572872 | tf_op jit(solution)/shard_map/while/body/eval_jaxpr/ppermute | solution.py:10
  54.2 11.4 %collective-permute-start = (f32[1024,128]{1,0:T(8,128)S(1)}, f32[1024,128]{1,0:T(8,128)S(1)}, u32[]{:S(2)}, u32[]{:S(2)}) collective-permute-start(f32[1024,128]{1,0:T(8,128)S(1)} %get-tuple-element.134), channel_id=1, source_target_pairs={{0,1},{1,2},{2,3},{3,4},{4,5},{5,6},{6,7},{7,8},{8,9},{9,10},{10,1... | collective-permute-start | bytes 1572872 | tf_op jit(solution)/shard_map/while/body/eval_jaxpr/ppermute | solution.py:10
  69.6 11.4 %collective-permute-start = (f32[1024,128]{1,0:T(8,128)S(1)}, f32[1024,128]{1,0:T(8,128)S(1)}, u32[]{:S(2)}, u32[]{:S(2)}) collective-permute-start(f32[1024,128]{1,0:T(8,128)S(1)} %get-tuple-element.134), channel_id=1, source_target_pairs={{0,1},{1,2},{2,3},{3,4},{4,5},{5,6},{6,7},{7,8},{8,9},{9,10},{10,1... | collective-permute-start | bytes 1572872 | tf_op jit(solution)/shard_map/while/body/eval_jaxpr/ppermute | solution.py:10
  85.0 11.4 %collective-permute-start = (f32[1024,128]{1,0:T(8,128)S(1)}, f32[1024,128]{1,0:T(8,128)S(1)}, u32[]{:S(2)}, u32[]{:S(2)}) collective-permute-start(f32[1024,128]{1,0:T(8,128)S(1)} %get-tuple-element.134), channel_id=1, source_target_pairs={{0,1},{1,2},{2,3},{3,4},{4,5},{5,6},{6,7},{7,8},{8,9},{9,10},{10,1... | collective-permute-start | bytes 1572872 | tf_op jit(solution)/shard_map/while/body/eval_jaxpr/ppermute | solution.py:10
  100.4 11.4 %collective-permute-start = (f32[1024,128]{1,0:T(8,128)S(1)}, f32[1024,128]{1,0:T(8,128)S(1)}, u32[]{:S(2)}, u32[]{:S(2)}) collective-permute-start(f32[1024,128]{1,0:T(8,128)S(1)} %get-tuple-element.134), channel_id=1, source_target_pairs={{0,1},{1,2},{2,3},{3,4},{4,5},{5,6},{6,7},{7,8},{8,9},{9,10},{10,1... | collective-permute-start | bytes 1572872 | tf_op jit(solution)/shard_map/while/body/eval_jaxpr/ppermute | solution.py:10
  115.9 11.4 %collective-permute-start = (f32[1024,128]{1,0:T(8,128)S(1)}, f32[1024,128]{1,0:T(8,128)S(1)}, u32[]{:S(2)}, u32[]{:S(2)}) collective-permute-start(f32[1024,128]{1,0:T(8,128)S(1)} %get-tuple-element.134), channel_id=1, source_target_pairs={{0,1},{1,2},{2,3},{3,4},{4,5},{5,6},{6,7},{7,8},{8,9},{9,10},{10,1... | collective-permute-start | bytes 1572872 | tf_op jit(solution)/shard_map/while/body/eval_jaxpr/ppermute | solution.py:10
  131.3 11.4 %collective-permute-start = (f32[1024,128]{1,0:T(8,128)S(1)}, f32[1024,128]{1,0:T(8,128)S(1)}, u32[]{:S(2)}, u32[]{:S(2)}) collective-permute-start(f32[1024,128]{1,0:T(8,128)S(1)} %get-tuple-element.134), channel_id=1, source_target_pairs={{0,1},{1,2},{2,3},{3,4},{4,5},{5,6},{6,7},{7,8},{8,9},{9,10},{10,1... | collective-permute-start | bytes 1572872 | tf_op jit(solution)/shard_map/while/body/eval_jaxpr/ppermute | solution.py:10
  146.7 0.8 copy-start.1
  147.5 144.5 %all-reduce.3.cloned.1.call-start = ((), (), s32[]{:S(2)}) async-start(), calls=%async_computation.2 | async-start | bytes 524288 | tf_op jit(solution)/shard_map/psum | solution.py:85
  159.5 3.7 %copy-start.4 = (f32[512,128]{1,0:T(8,128)S(1)}, f32[512,128]{1,0:T(8,128)}, u32[]{:S(2)}) copy-start(f32[512,128]{1,0:T(8,128)} %reduce-scatter.2.cloned.1.call-done) | copy-start | bytes 786436
Sparse Core Ops, SparseCore 0:
  147.6 11.8 reduce-scatter.1
  166.7 125.2 all-reduce.2
where the time goes:
time: 303 us; the launch traced here: 302 us
  waiting for transfers between devices  186 us (61%)
  blocking collectives  39.4 us (13%)
  matrix products  35.3 us (12%)
  local copies, waits for them, and re-layouts  15.8 us (5%)
  between operations  14.2 us (5%)
  other arithmetic  5.71 us (2%)
  starting transfers between devices  4.59 us (2%)
    ppermute x8, waiting for transfers between devices, shifted(): return lax.ppermute(value, axis, pairs)  88.2 us
    psum x1, waiting for transfers between devices, on_device(): lax.psum((grads[0], grads[1], grads[2]), ('row', 'col'))  87.2 us
    psum x1, blocking collectives, on_device(): lax.psum((grads[0], grads[1], grads[2]), ('row', 'col'))  39.4 us
    dot_general x8, matrix products, stop_product(): jnp.einsum('tij,tjd->tid', weights, chosen, precision=lax.Precision.HIGHEST)  16.7 us
    reduce_scatter x1, waiting for transfers between devices, on_device(): aggregate = lax.psum_scatter(total, 'row', scatter_dimension=0, tiled=True)  11.1 us
    dot_general x8, matrix products, stop_product(): jnp.einsum('tk,tid->kid', row_hot, prod, precision=lax.Precision.HIGHEST)  7.22 us
    dot_general x8, matrix products, stop_product(): jnp.einsum('tk,kjd->tjd', col_hot, pieces, precision=lax.Precision.HIGHEST)  6.36 us
  transfers between devices with their start and end apart: 10, of which 10 were waited for; matrix products, arithmetic and copies ran while one was open for 5% of the time, Pallas kernels for 0%

commit v1 on v0

v1 whole, which is shorter than its diff:
```python
import functools

import jax
import jax.numpy as jnp
from jax import lax
from jax.experimental import pallas as pl
from jax.experimental.pallas import tpu as pltpu
from jax.sharding import PartitionSpec as P

VMEM = pltpu.VMEM
SMEM = pltpu.SMEM
F32 = jnp.float32
BF16 = jnp.bfloat16
LIMIT = 48 * 1024 * 1024
GROUP = 4


def split(value):
    high = value.astype(BF16)
    low = (value - high.astype(F32)).astype(BF16)
    return high, low


def dot3(left, right, dims):
    lh, ll = left
    rh, rl = right
    mul = functools.partial(
        lax.dot_general, dimension_numbers=(dims, ((), ())), preferred_element_type=F32
    )
    return mul(lh, rh) + (mul(lh, rl) + mul(ll, rh))


def spec(space):
    return pl.BlockSpec(memory_space=space)


def tiles_kernel(
    parts, halved, has_acc, n_half, slots, side,
    meta, rows, cols, counts, *refs,
):
    n_in = sum(2 if h else 1 for h in halved)
    blocks, refs = refs[:n_in], refs[n_in:]
    tiles, refs = refs[0], refs[1:]
    if has_acc:
        acc_in, refs = refs[0], refs[1:]
    if n_half:
        keep, send, acc, pair, buf, sems = refs
    else:
        acc, pair, buf, sems = refs

    def copy(b):
        stop = jnp.maximum(meta[b], 0)
        return pltpu.make_async_copy(
            tiles.at[pl.ds(stop * slots, slots)], buf.at[b], sems.at[b]
        )

    for b in range(parts):
        copy(b).start()
    if has_acc:
        acc[...] = acc_in[...]
    else:
        acc[...] = jnp.zeros_like(acc)
    width = acc.shape[1]
    at = 0
    for b in range(parts):
        stop = meta[b]
        slot = b % 2
        if halved[b]:
            mine, other = blocks[at], blocks[at + 1]
            at += 2
            half = mine.shape[0]
            core = meta[parts]
            for ref, place in ((mine, core), (other, 1 - core)):
                high, low = split(ref[...])
                start = pl.multiple_of(place * half, half)
                pair[slot, pl.ds(start, half), :width] = high
                pair[slot, pl.ds(start, half), width:] = low
        else:
            high, low = split(blocks[at][...])
            at += 1
            pair[slot, :, :width] = high
            pair[slot, :, width:] = low
        copy(b).wait()
        safe = jnp.maximum(stop, 0)
        count = jnp.where(stop >= 0, counts[safe], 0)
        base = safe * slots
        for first in range(0, slots, GROUP):
            here = range(first, min(first + GROUP, slots))

            @pl.when(first < count)
            def _(b=b, slot=slot, here=here, base=base, count=count):
                prods = []
                for t in here:
                    col = pl.multiple_of(cols[base + t] * side, side)
                    both = jnp.dot(
                        buf[b, t], pair[slot, pl.ds(col, side), :],
                        preferred_element_type=F32,
                    )
                    prods.append(both[:, :width] + both[:, width:])
                for t, prod in zip(here, prods):
                    row = pl.multiple_of(rows[base + t] * side, side)
                    acc[pl.ds(row, side), :] += jnp.where(t < count, prod, 0.0)

    if n_half:
        half = keep.shape[0]
        row = meta[parts + 1]
        for out, place in zip((keep, *(send,)), (row, 1 - row)):
            out[...] = acc[pl.ds(pl.multiple_of(place * half, half), half), :]


def add_products(blocks, stops, core, row, index, tiles, acc, finish):
    rows, cols, counts = index
    halved = tuple(isinstance(b, tuple) for b in blocks)
    flat = [a for b in blocks for a in (b if isinstance(b, tuple) else (b,))]
    n = len(blocks)
    nodes = 2 * flat[0].shape[0] if halved[0] else flat[0].shape[0]
    width = flat[0].shape[1]
    slots = tiles.shape[0] // counts.shape[0]
    side = tiles.shape[1]
    meta = jnp.stack([*stops, core, row]).astype(jnp.int32)
    whole = jax.ShapeDtypeStruct((nodes, width), F32)
    part = jax.ShapeDtypeStruct((nodes // 2, width), F32)
    body = functools.partial(
        tiles_kernel, n, halved, acc is not None, int(finish), slots, side
    )
    scratch = [
        VMEM((2, nodes, 2 * width), BF16),
        VMEM((n, slots, side, side), BF16),
        pltpu.SemaphoreType.DMA((n,)),
    ]
    if finish:
        scratch = [VMEM((nodes, width), F32)] + scratch
    return pl.pallas_call(
        body,
        out_shape=(part, part) if finish else whole,
        in_specs=[spec(SMEM)] * 4
        + [spec(VMEM)] * len(flat)
        + [spec(pl.ANY)]
        + ([spec(VMEM)] if acc is not None else []),
        out_specs=(spec(VMEM),) * 2 if finish else spec(VMEM),
        scratch_shapes=scratch,
        compiler_params=pltpu.CompilerParams(vmem_limit_bytes=LIMIT),
        cost_estimate=pl.CostEstimate(
            flops=n * slots * side * side * width * 40,
            bytes_accessed=n * slots * side * side * 2,
            transcendentals=0,
        ),
    )(meta, rows, cols, counts, *flat, tiles, *(() if acc is None else (acc,)))


def layer_kernel(
    core, own, kept, got, self_weight, neigh_weight, bias, cotangent,
    output, keep, send,
):
    depth = self_weight.shape[0]
    units = self_weight.shape[1]
    both = jnp.concatenate([own[...], kept[...] + got[...]], axis=1)
    inputs = split(both)
    weights = split(jnp.concatenate([self_weight[...], neigh_weight[...]], axis=0))
    pre = dot3(inputs, weights, ((1,), (0,))) + bias[...]
    root = 0.7978845608028654
    square = pre * pre
    bend = jnp.tanh(root * (pre + 0.044715 * (square * pre)))
    rise = 0.5 * (1.0 + bend)
    hidden = pre * rise
    scale = lax.rsqrt(jnp.mean(hidden * hidden, axis=-1, keepdims=True) + 1e-06)
    out = hidden * scale
    output[...] = out
    weight = cotangent[...]
    along = jnp.mean(weight * out, axis=-1, keepdims=True)
    slope = rise + (0.5 * root) * pre * (1.0 - bend * bend) * (
        1.0 + (3 * 0.044715) * square
    )
    back = scale * (weight - out * along) * slope
    grads = dot3(inputs, split(back), ((0,), (0,)))
    grad_bias = jnp.sum(back, axis=0, keepdims=True)
    first = core[0] == 0
    tail = jnp.broadcast_to(grad_bias, (8, units))
    keep[:depth, :] = jnp.where(first, grads[:depth], grads[depth:])
    send[:depth, :] = jnp.where(first, grads[depth:], grads[:depth])
    keep[depth:, :] = tail
    send[depth:, :] = tail


def run_layer(core, own, kept, got, self_weight, neigh_weight, bias, cotangent):
    nodes, depth = own.shape
    units = self_weight.shape[1]
    part = jax.ShapeDtypeStruct((depth + 8, units), F32)
    return pl.pallas_call(
        layer_kernel,
        out_shape=(jax.ShapeDtypeStruct((nodes, units), F32), part, part),
        in_specs=[spec(SMEM)] + [spec(VMEM)] * 7,
        out_specs=(spec(VMEM),) * 3,
        compiler_params=pltpu.CompilerParams(vmem_limit_bytes=LIMIT),
        cost_estimate=pl.CostEstimate(
            flops=12 * nodes * 2 * depth * units,
            bytes_accessed=nodes * units * 12,
            transcendentals=nodes * units,
        ),
    )(jnp.reshape(core, (1,)), own, kept, got, self_weight, neigh_weight,
      bias.reshape(1, units), cotangent)


def gather_small(block, row, col, send):
    core = col % 2
    y = (col // 2) % 2
    z = col // 4
    half = block.shape[0] // 2
    swap = lambda value: send(value, lambda r, c: (r, c ^ 1))
    beside = swap(block)
    yield [block, beside], [col, col ^ 1]

    near = send(block, lambda r, c: (r, (c + (4 if r == 0 else 12)) % 16))
    near_col = (col + jnp.where(row == 0, 12, 4)) % 16

    mine = jnp.where(core == 1 - row, block, beside)
    mine = lax.dynamic_slice_in_dim(mine, core * half, half, 0)
    far = send(mine, lambda r, c: (r, c ^ 8))

    level = send(
        block, lambda r, c: (r, c ^ 2) if (c // 2) % 2 == r else None
    )
    level_beside = swap(level)
    yield [level, level_beside], [col ^ 2, col ^ 3]

    near_beside = swap(near)
    yield [near, near_beside], [near_col, near_col ^ 1]
    cross = send(near, lambda r, c: (r, c ^ 2))
    cross_beside = swap(cross)
    yield [cross, cross_beside], [near_col ^ 2, near_col ^ 3]

    place = lambda r, c: (r, (c // 2) % 2)
    over_y = send(far, lambda r, c: (r, c ^ 2) if place(r, c) in ((0, 1), (1, 0)) else None)
    over_x = send(far, lambda r, c: (1, c) if r == 0 else None)
    over_d = send(far, lambda r, c: (1 - r, c ^ 2) if place(r, c) in ((0, 0), (1, 1)) else None)
    base = 4 * ((z + 2) % 4)
    here = 2 * row + y
    far_cols = [
        base + 2 * y + 1 - row,
        jnp.where(here == 0, base + 3, jnp.where(here == 3, base, -1)),
        jnp.where(here == 2, base + 1, jnp.where(here == 3, base + 3, -1)),
        jnp.where(here == 0, base + 2, jnp.where(here == 3, base + 1, -1)),
    ]
    halves = [far, over_y, over_x, over_d]
    yield [(h, swap(h)) for h in halves], far_cols


def gather_ring(block, row, col, send, rows, cols, stops):
    held = send(block, lambda r, c: (r, (c + stops * r) % cols))
    held = jnp.where(row == 0, block, held)
    at = (col - stops * row) % cols
    for stop in range(stops):
        if stop:
            held = send(held, lambda r, c: (r, (c + 1) % cols))
            at = (at - 1) % cols
        yield [held], [at]


def on_device(
    features, self_weight, neigh_weight, bias, edge_tiles, tile_rows, tile_cols,
    tile_count, cotangent,
):
    rows = lax.axis_size("row")
    cols = lax.axis_size("col")
    row = lax.axis_index("row")
    col = lax.axis_index("col")
    stops = tile_count.shape[2]
    block = features[0]
    tiles = edge_tiles[0, 0]
    index = (tile_rows[0, 0], tile_cols[0, 0], tile_count[0, 0])
    small = rows == 2 and cols == 16 and stops == 8

    def send(value, to):
        pairs = []
        for r in range(rows):
            for c in range(cols):
                goal = to(r, c)
                if goal is not None and goal != (r, c):
                    pairs.append((r * cols + c, goal[0] * cols + goal[1]))
        return lax.ppermute(value, ("row", "col"), pairs)

    if small:
        groups = list(gather_small(block, row, col, send))
    else:
        groups = list(gather_ring(block, row, col, send, rows, cols, stops))
    core = col % 2
    acc = None
    for g, (blocks, at) in enumerate(groups):
        which = []
        for column in at:
            stop = (col - stops * row - column) % cols
            which.append(jnp.where((column >= 0) & (stop < stops), stop, -1))
        last = small and g == len(groups) - 1
        acc = add_products(blocks, which, core, row, index, tiles, acc, last)

    share = cotangent.shape[1]
    own = lax.dynamic_slice_in_dim(block, row * share, share, 0)
    if small:
        kept, away = acc
        got = send(away, lambda r, c: (1 - r, c))
    else:
        kept = lax.psum_scatter(acc, "row", scatter_dimension=0, tiled=True)
        got = jnp.zeros_like(kept)
    output, keep, away = run_layer(
        core, own, kept, got, self_weight, neigh_weight, bias, cotangent[0]
    )
    swap = lambda value: send(value, lambda r, c: (r, c ^ 1))
    total = keep + swap(away)
    if small:
        total = total + send(total, lambda r, c: (1 - r, c))
        for bit in (2, 4, 8):
            total = total + send(total, lambda r, c: (r, c ^ bit))
    else:
        total = lax.psum(total, "row")
        bit = 2
        while bit < cols:
            total = total + send(total, lambda r, c: (r, c ^ bit))
            bit *= 2
    other = swap(total)
    depth = self_weight.shape[0]
    first = core == 0
    grad_self = jnp.where(first, total[:depth], other[:depth])
    grad_neigh = jnp.where(first, other[:depth], total[:depth])
    return (output[None], grad_self, grad_neigh, total[depth])


def solution(mesh):
    in_specs = (
        P("col", None, None),
        P(),
        P(),
        P(),
        P("row", "col", None, None, None),
        P("row", "col", None),
        P("row", "col", None),
        P("row", "col", None),
        P("col", "row", None),
    )
    out_specs = (P("col", "row", None), P(), P(), P())
    return jax.shard_map(
        on_device, mesh=mesh, in_specs=in_specs, out_specs=out_specs, check_vma=False
    )
```

time: 303 us -> 100 us (0.33)
  waiting for transfers between devices: 186 us -> 53.5 us
  blocking collectives: 39.4 us -> 0 us
  matrix products: 35.3 us -> 0 us
  starting transfers between devices: 4.59 us -> 23.4 us
  between operations: 14.2 us -> 1.09 us
  Pallas kernels: 0 us -> 13 us
  local copies, waits for them, and re-layouts: 15.8 us -> 5.6 us
    psum x1 -> x0, waiting for transfers between devices: 87.2 us -> none  [on_device(): lax.psum((grads[0], grads[1], grads[2]), ('row', 'col'))]
    psum x1 -> x0, blocking collectives: 39.4 us -> none  [on_device(): lax.psum((grads[0], grads[1], grads[2]), ('row', 'col'))]
    dot_general x28 -> x0, matrix products: 35.3 us -> none  [the longest x8 16.7 us: stop_product(): jnp.einsum('tij,tjd->tid', weights, chosen, precision=lax.Precision.HIGHEST)]
    ppermute x8 -> x22, waiting for transfers between devices: 88.2 us -> 53.5 us  [send(): return lax.ppermute(value, ('row', 'col'), pairs)]
    ppermute x8 -> x22, starting transfers between devices: 4.51 us -> 23.4 us  [send(): return lax.ppermute(value, ('row', 'col'), pairs)]
    pallas_call x0 -> x6, Pallas kernels: none -> 13 us  [the longest x5 11.3 us: add_products(): pl.pallas_call(body, out_shape=(part, part) if finish else whole, in_spec...]
    reduce_scatter x1 -> x0, waiting for transfers between devices: 11.1 us -> none  [on_device(): aggregate = lax.psum_scatter(total, 'row', scatter_dimension=0, tiled=True)]
    convert_element_type x8 -> x0, other arithmetic: 4.56 us -> none  [stop_product(): live = (jnp.arange(slots, dtype=jnp.int32) < count).astype(jnp.float32)]
  transfers between devices with their start and end apart: 10 -> 22, of which waited for: 10 -> 10; matrix products, arithmetic and copies ran while one was open for 5% -> 3% of each run, Pallas kernels for 0% -> 8%
where the time goes in v1:
time: 100 us; the launch traced here: 99.5 us
  waiting for transfers between devices  53.5 us (54%)
  starting transfers between devices  23.4 us (23%)
  Pallas kernels  13 us (13%)
  local copies, waits for them, and re-layouts  5.6 us (6%)
  other arithmetic  2.82 us (3%)
  between operations  1.09 us (1%)
    ppermute x22, waiting for transfers between devices, send(): return lax.ppermute(value, ('row', 'col'), pairs)  53.5 us
    ppermute x22, starting transfers between devices, send(): return lax.ppermute(value, ('row', 'col'), pairs)  23.4 us
    pallas_call x5, Pallas kernels, add_products(): pl.pallas_call(body, out_shape=(part, part) if finish else whole, in_spec...  11.3 us
    unnamed x22, local copies, waits for them, and re-layouts  4.93 us
  transfers between devices with their start and end apart: 22, of which 10 were waited for; matrix products, arithmetic and copies ran while one was open for 3% of the time, Pallas kernels for 8%

profile of v1, /device:TPU:0, one launch (start us, length us, event | category | flops | bytes accessed | tf_op | source)
XLA Modules:
  0.0 99.5 jit_solution(4305090204640385103)
XLA Ops:
  0.6 4.9 %collective-permute-start.13 = (f32[1024,128]{1,0:T(8,128)}, f32[1024,128]{1,0:T(8,128)S(1)}, u32[]{:S(2)}, u32[]{:S(2)}) collective-permute-start(f32[1024,128]{1,0:T(8,128)} %bitcast.26), channel_id=1, source_target_pairs={{0,2},{1,3},{4,6},{5,7},{8,10},{9,11},{12,14},{13,15},{18,16},{19,... | collective-permute-start | bytes 1572872 | tf_op jit(solution)/shard_map/ppermute | solution.py:280
  5.5 1.6 %collective-permute-start.9 = (f32[1024,128]{1,0:T(8,128)}, f32[1024,128]{1,0:T(8,128)S(1)}, u32[]{:S(2)}, u32[]{:S(2)}) collective-permute-start(f32[1024,128]{1,0:T(8,128)} %bitcast.27), channel_id=1, source_target_pairs={{0,4},{1,5},{2,6},{3,7},{4,8},{5,9},{6,10},{7,11},{8,12},{9,13},{1... | collective-permute-start | bytes 1572872 | tf_op jit(solution)/shard_map/ppermute | solution.py:280
  7.2 9.8 %collective-permute-done.13.refs_0_ = f32[1024,128]{1,0:T(8,128)S(1)} collective-permute-done((f32[1024,128]{1,0:T(8,128)}, f32[1024,128]{1,0:T(8,128)S(1)}, u32[]{:S(2)}, u32[]{:S(2)}) %collective-permute-start.13) | collective-permute-done | bytes 524320 | tf_op jit(solution)/shard_map/ppermute | solution.py:280
  17.0 4.1 %collective-permute-done.9.refs_0_ = f32[1024,128]{1,0:T(8,128)S(1)} collective-permute-done((f32[1024,128]{1,0:T(8,128)}, f32[1024,128]{1,0:T(8,128)S(1)}, u32[]{:S(2)}, u32[]{:S(2)}) %collective-permute-start.9) | collective-permute-done | bytes 524320 | tf_op jit(solution)/shard_map/ppermute | solution.py:280
  21.1 1.7 %dynamic-slice_select_fusion = f32[512,128]{1,0:T(8,128)} fusion(f32[1024,128]{1,0:T(8,128)S(1)} %collective-permute-done.refs_1_, s32[]{:T(128)S(6)} %select_n.183, f32[1024,128]{1,0:T(8,128)} %bitcast.29, pred[]{:T(512)S(6)} %eq.42), kind=kLoop, calls=%fused_computation | loop fusion | flops 65536 | bytes 786437 | tf_op jit(solution)/shard_map/jit(_where)/select_n | solution.py:216
  24.3 12.3 %collective-permute-done.1.refs_0_ = f32[512,128]{1,0:T(8,128)} collective-permute-done((f32[512,128]{1,0:T(8,128)}, f32[512,128]{1,0:T(8,128)}, u32[]{:S(2)}, u32[]{:S(2)}) %collective-permute-start.1) | collective-permute-done | bytes 262176 | tf_op jit(solution)/shard_map/ppermute | solution.py:280
  36.6 1.3 %collective-permute-start.3 = (f32[512,128]{1,0:T(8,128)}, f32[512,128]{1,0:T(8,128)S(1)}, u32[]{:S(2)}, u32[]{:S(2)}) collective-permute-start(f32[512,128]{1,0:T(8,128)} %collective-permute-done.1.refs_0_), channel_id=1, source_target_pairs={{2,0},{3,1},{6,4},{7,5},{10,8},{11,9},{14,12},{15,13},{16,18},{17,... | collective-permute-start | bytes 786440 | tf_op jit(solution)/shard_map/ppermute | solution.py:280
  37.9 4.4 %collective-permute-start.5 = (f32[512,128]{1,0:T(8,128)}, f32[512,128]{1,0:T(8,128)S(1)}, u32[]{:S(2)}, u32[]{:S(2)}) collective-permute-start(f32[512,128]{1,0:T(8,128)} %collective-permute-done.1.refs_0_), channel_id=1, source_target_pairs={{0,16},{1,17},{2,18},{3,19},{4,20},{5,21},{6,22},{7,23},{8,24},{9,... | collective-permute-start | bytes 786440 | tf_op jit(solution)/shard_map/ppermute | solution.py:280
  42.3 1.9 %collective-permute-start.7 = (f32[512,128]{1,0:T(8,128)}, f32[512,128]{1,0:T(8,128)S(1)}, u32[]{:S(2)}, u32[]{:S(2)}) collective-permute-start(f32[512,128]{1,0:T(8,128)} %collective-permute-done.1.refs_0_), channel_id=1, source_target_pairs={{0,18},{1,19},{4,22},{5,23},{8,26},{9,27},{12,30},{13,31},{18,0},{... | collective-permute-start | bytes 786440 | tf_op jit(solution)/shard_map/ppermute | solution.py:280
  45.3 1.9 %copy-done.6 = bf16[1,1,96,128,128]{4,3,2,1,0:T(8,128)(2,1)S(1)} copy-done((bf16[1,1,96,128,128]{4,3,2,1,0:T(8,128)(2,1)S(1)}, bf16[1,1,96,128,128]{4,3,2,1,0:T(8,128)(2,1)}, u32[]{:S(2)}) %copy-start.6) | copy-done | bytes 3145752
  49.2 1.9 %shard_map.120.refs_3_ = f32[1024,128]{1,0:T(8,128)S(1)} custom-call(s32[4]{0:T(128)S(1)} %add_add_fusion.3.meta, s32[96]{0:T(128)S(1)} %bitcast.37, s32[96]{0:T(128)S(1)} %bitcast.42, s32[8]{0:T(128)S(1)} %bitcast.47, f32[1024,128]{1,0:T(8,128)S(1)} %bitcast.30, f32[1024,128]{1,0:T(8,128)S(1)} %collective-permute-done.refs_1_, ...), custom_call_target="tpu_custom_call" | custom-call | flops 2013265920 | bytes 786432 | tf_op jit(solution)/shard_map/pallas_call | solution.py:133
  54.0 2.2 %shard_map.122.refs_3_ = f32[1024,128]{1,0:T(8,128)S(1)} custom-call(s32[4]{0:T(128)S(1)} %add_add_fusion.1.meta, s32[96]{0:T(128)S(1)} %bitcast.39, s32[96]{0:T(128)S(1)} %bitcast.44, s32[8]{0:T(128)S(1)} %bitcast.49, f32[1024,128]{1,0:T(8,128)S(1)} %collective-permute-done.9.refs_0_, f32[1024,128]{1,0:T(8,128)S(1)} %collective-permute-done.12.refs_1_, ...), custom_call_target="tpu_custom_call" | custom-call | flops 2013265920 | bytes 786432 | tf_op jit(solution)/shard_map/pallas_call | solution.py:133
  56.2 2.4 %shard_map.123.refs_9_ = f32[1024,128]{1,0:T(8,128)S(1)} custom-call(s32[4]{0:T(128)S(1)} %add_add_fusion.meta, s32[96]{0:T(128)S(1)} %bitcast.40, s32[96]{0:T(128)S(1)} %bitcast.45, s32[8]{0:T(128)S(1)} %bitcast.50, f32[1024,128]{1,0:T(8,128)S(1)} %collective-permute-done.10.refs_0_, f32[1024,128]{1,0:T(8,128)S(1)} %collective-permute-done.11.refs_1_, ...), custom_call_target="tpu_custom_call" | custom-call | flops 2013265920 | bytes 786432 | tf_op jit(solution)/shard_map/pallas_call | solution.py:133
  58.7 3.6 %shard_map.124 = (f32[512,128]{1,0:T(8,128)S(1)}, f32[512,128]{1,0:T(8,128)S(1)}) custom-call(s32[6]{0:T(128)S(1)} %stack.68.meta, s32[96]{0:T(128)S(1)} %bitcast.41, s32[96]{0:T(128)S(1)} %bitcast.46, s32[8]{0:T(128)S(1)} %bitcast.51, f32[512,128]{1,0:T(8,128)} %collective-permute-done.1.refs_0_, f32[512,128]{1,0:T(8,128)S(1)} %collective-permute-done.2.refs_1_, ...), custom_call_target="tpu_custom_call" | custom-call | flops 4026531840 | bytes 1572864 | tf_op jit(solution)/shard_map/pallas_call | solution.py:133
  62.4 7.9 %collective-permute-done.15.got = f32[512,128]{1,0:T(8,128)S(1)} collective-permute-done((f32[512,128]{1,0:T(8,128)S(1)}, f32[512,128]{1,0:T(8,128)S(1)}, u32[]{:S(2)}, u32[]{:S(2)}) %collective-permute-start.15) | collective-permute-done | bytes 262176 | tf_op jit(solution)/shard_map/ppermute | solution.py:280
  70.4 1.7 %shard_map.125 = (f32[512,256]{1,0:T(8,128)}, f32[136,256]{1,0:T(8,128)S(1)}, f32[136,256]{1,0:T(8,128)S(1)}) custom-call(s32[1]{0:T(128)} %bitcast.core, f32[512,128]{1,0:T(8,128)S(1)} %dynamic-slice_bitcast_fusion.own, f32[512,128]{1,0:T(8,128)S(1)} %get-tuple-element.9.kept, f32[512,128]{1,0:T(8,128)S(1)} %collective-permute-done.15.got, ...), custom_call_target="tpu_custom_call" | custom-call | flops 402653184 | bytes 1572864 | tf_op jit(solution)/shard_map/pallas_call | solution.py:189
  72.0 1.4 %collective-permute-done.16 = f32[136,256]{1,0:T(8,128)S(1)} collective-permute-done((f32[136,256]{1,0:T(8,128)S(1)}, f32[136,256]{1,0:T(8,128)S(1)}, u32[]{:S(2)}, u32[]{:S(2)}) %collective-permute-start.16) | collective-permute-done | bytes 139296 | tf_op jit(solution)/shard_map/ppermute | solution.py:280
  73.8 5.4 %collective-permute-done.17 = f32[136,256]{1,0:T(8,128)S(1)} collective-permute-done((f32[136,256]{1,0:T(8,128)S(1)}, f32[136,256]{1,0:T(8,128)S(1)}, u32[]{:S(2)}, u32[]{:S(2)}) %collective-permute-start.17) | collective-permute-done | bytes 139296 | tf_op jit(solution)/shard_map/ppermute | solution.py:280
  79.2 1.7 %collective-permute-start.18 = (f32[136,256]{1,0:T(8,128)S(1)}, f32[136,256]{1,0:T(8,128)S(1)}, u32[]{:S(2)}, u32[]{:S(2)}) collective-permute-start(f32[136,256]{1,0:T(8,128)S(1)} %add.126), channel_id=1, source_target_pairs={{0,2},{1,3},{2,0},{3,1},{4,6},{5,7},{6,4},{7,5},{8,10},{9,11},{10,... | collective-permute-start | bytes 417800 | tf_op jit(solution)/shard_map/ppermute | solution.py:280
  81.0 3.4 %collective-permute-done.18 = f32[136,256]{1,0:T(8,128)S(1)} collective-permute-done((f32[136,256]{1,0:T(8,128)S(1)}, f32[136,256]{1,0:T(8,128)S(1)}, u32[]{:S(2)}, u32[]{:S(2)}) %collective-permute-start.18) | collective-permute-done | bytes 139296 | tf_op jit(solution)/shard_map/ppermute | solution.py:280
  84.4 1.4 %collective-permute-start.19 = (f32[136,256]{1,0:T(8,128)S(1)}, f32[136,256]{1,0:T(8,128)S(1)}, u32[]{:S(2)}, u32[]{:S(2)}) collective-permute-start(f32[136,256]{1,0:T(8,128)S(1)} %add.127), channel_id=1, source_target_pairs={{0,4},{1,5},{2,6},{3,7},{4,0},{5,1},{6,2},{7,3},{8,12},{9,13},{10,... | collective-permute-start | bytes 417800 | tf_op jit(solution)/shard_map/ppermute | solution.py:280
  85.8 3.7 %collective-permute-done.19 = f32[136,256]{1,0:T(8,128)S(1)} collective-permute-done((f32[136,256]{1,0:T(8,128)S(1)}, f32[136,256]{1,0:T(8,128)S(1)}, u32[]{:S(2)}, u32[]{:S(2)}) %collective-permute-start.19) | collective-permute-done | bytes 139296 | tf_op jit(solution)/shard_map/ppermute | solution.py:280
  89.5 3.0 %collective-permute-start.20 = (f32[136,256]{1,0:T(8,128)S(1)}, f32[136,256]{1,0:T(8,128)S(1)}, u32[]{:S(2)}, u32[]{:S(2)}) collective-permute-start(f32[136,256]{1,0:T(8,128)S(1)} %add.128), channel_id=1, source_target_pairs={{0,8},{1,9},{2,10},{3,11},{4,12},{5,13},{6,14},{7,15},{8,0},{9,1},... | collective-permute-start | bytes 417800 | tf_op jit(solution)/shard_map/ppermute | solution.py:280
  92.5 4.8 %collective-permute-done.20 = f32[136,256]{1,0:T(8,128)S(1)} collective-permute-done((f32[136,256]{1,0:T(8,128)S(1)}, f32[136,256]{1,0:T(8,128)S(1)}, u32[]{:S(2)}, u32[]{:S(2)}) %collective-permute-start.20) | collective-permute-done | bytes 139296 | tf_op jit(solution)/shard_map/ppermute | solution.py:280
  (62 shorter events, 10.1 us)
Async XLA Ops:
  0.6 16.4 %collective-permute-start.13 = (f32[1024,128]{1,0:T(8,128)}, f32[1024,128]{1,0:T(8,128)S(1)}, u32[]{:S(2)}, u32[]{:S(2)}) collective-permute-start(f32[1024,128]{1,0:T(8,128)} %bitcast.26), channel_id=1, source_target_pairs={{0,2},{1,3},{4,6},{5,7},{8,10},{9,11},{12,14},{13,15},{18,16},{19,... | collective-permute-start | bytes 1572872 | tf_op jit(solution)/shard_map/ppermute | solution.py:280
  5.5 15.5 %collective-permute-start.9 = (f32[1024,128]{1,0:T(8,128)}, f32[1024,128]{1,0:T(8,128)S(1)}, u32[]{:S(2)}, u32[]{:S(2)}) collective-permute-start(f32[1024,128]{1,0:T(8,128)} %bitcast.27), channel_id=1, source_target_pairs={{0,4},{1,5},{2,6},{3,7},{4,8},{5,9},{6,10},{7,11},{8,12},{9,13},{1... | collective-permute-start | bytes 1572872 | tf_op jit(solution)/shard_map/ppermute | solution.py:280
  7.2 14.0 %collective-permute-start = (f32[1024,128]{1,0:T(8,128)}, f32[1024,128]{1,0:T(8,128)S(1)}, u32[]{:S(2)}, u32[]{:S(2)}) collective-permute-start(f32[1024,128]{1,0:T(8,128)} %bitcast.28), channel_id=1, source_target_pairs={{0,1},{1,0},{2,3},{3,2},{4,5},{5,4},{6,7},{7,6},{8,9},{9,8},{10,11... | collective-permute-start | bytes 1572872 | tf_op jit(solution)/shard_map/ppermute | solution.py:280
  17.0 25.3 %collective-permute-start.14 = (f32[1024,128]{1,0:T(8,128)S(1)}, f32[1024,128]{1,0:T(8,128)S(1)}, u32[]{:S(2)}, u32[]{:S(2)}) collective-permute-start(f32[1024,128]{1,0:T(8,128)S(1)} %collective-permute-done.13.refs_0_), channel_id=1, source_target_pairs={{0,1},{1,0},{2,3},{3,2},{4,5},{5,4},{6,7},{7,6},{8,9},{9,8},{10,11... | collective-permute-start | bytes 1572872 | tf_op jit(solution)/shard_map/ppermute | solution.py:280
  21.1 23.1 %collective-permute-start.10 = (f32[1024,128]{1,0:T(8,128)S(1)}, f32[1024,128]{1,0:T(8,128)S(1)}, u32[]{:S(2)}, u32[]{:S(2)}) collective-permute-start(f32[1024,128]{1,0:T(8,128)S(1)} %collective-permute-done.9.refs_0_), channel_id=1, source_target_pairs={{0,2},{1,3},{2,0},{3,1},{4,6},{5,7},{6,4},{7,5},{8,10},{9,11},{10,... | collective-permute-start | bytes 1572872 | tf_op jit(solution)/shard_map/ppermute | solution.py:280
  22.8 13.8 %collective-permute-start.1 = (f32[512,128]{1,0:T(8,128)}, f32[512,128]{1,0:T(8,128)}, u32[]{:S(2)}, u32[]{:S(2)}) collective-permute-start(f32[512,128]{1,0:T(8,128)} %dynamic-slice_select_fusion), channel_id=1, source_target_pairs={{0,8},{1,9},{2,10},{3,11},{4,12},{5,13},{6,14},{7,15},{8,0},{9,1},... | collective-permute-start | bytes 786440 | tf_op jit(solution)/shard_map/ppermute | solution.py:280
  23.8 28.6 %collective-permute-start.12 = (f32[1024,128]{1,0:T(8,128)S(1)}, f32[1024,128]{1,0:T(8,128)S(1)}, u32[]{:S(2)}, u32[]{:S(2)}) collective-permute-start(f32[1024,128]{1,0:T(8,128)S(1)} %collective-permute-done.9.refs_0_), channel_id=1, source_target_pairs={{0,1},{1,0},{2,3},{3,2},{4,5},{5,4},{6,7},{7,6},{8,9},{9,8},{10,11... | collective-permute-start | bytes 1572872 | tf_op jit(solution)/shard_map/ppermute | solution.py:280
  36.6 16.8 %collective-permute-start.3 = (f32[512,128]{1,0:T(8,128)}, f32[512,128]{1,0:T(8,128)S(1)}, u32[]{:S(2)}, u32[]{:S(2)}) collective-permute-start(f32[512,128]{1,0:T(8,128)} %collective-permute-done.1.refs_0_), channel_id=1, source_target_pairs={{2,0},{3,1},{6,4},{7,5},{10,8},{11,9},{14,12},{15,13},{16,18},{17,... | collective-permute-start | bytes 786440 | tf_op jit(solution)/shard_map/ppermute | solution.py:280
  37.9 15.6 %collective-permute-start.5 = (f32[512,128]{1,0:T(8,128)}, f32[512,128]{1,0:T(8,128)S(1)}, u32[]{:S(2)}, u32[]{:S(2)}) collective-permute-start(f32[512,128]{1,0:T(8,128)} %collective-permute-done.1.refs_0_), channel_id=1, source_target_pairs={{0,16},{1,17},{2,18},{3,19},{4,20},{5,21},{6,22},{7,23},{8,24},{9,... | collective-permute-start | bytes 786440 | tf_op jit(solution)/shard_map/ppermute | solution.py:280
  42.3 11.7 %collective-permute-start.7 = (f32[512,128]{1,0:T(8,128)}, f32[512,128]{1,0:T(8,128)S(1)}, u32[]{:S(2)}, u32[]{:S(2)}) collective-permute-start(f32[512,128]{1,0:T(8,128)} %collective-permute-done.1.refs_0_), channel_id=1, source_target_pairs={{0,18},{1,19},{4,22},{5,23},{8,26},{9,27},{12,30},{13,31},{18,0},{... | collective-permute-start | bytes 786440 | tf_op jit(solution)/shard_map/ppermute | solution.py:280
  44.2 12.0 %collective-permute-start.11 = (f32[1024,128]{1,0:T(8,128)S(1)}, f32[1024,128]{1,0:T(8,128)S(1)}, u32[]{:S(2)}, u32[]{:S(2)}) collective-permute-start(f32[1024,128]{1,0:T(8,128)S(1)} %collective-permute-done.10.refs_0_), channel_id=1, source_target_pairs={{0,1},{1,0},{2,3},{3,2},{4,5},{5,4},{6,7},{7,6},{8,9},{9,8},{10,11... | collective-permute-start | bytes 1572872 | tf_op jit(solution)/shard_map/ppermute | solution.py:280
  52.4 6.2 %collective-permute-start.2 = (f32[512,128]{1,0:T(8,128)}, f32[512,128]{1,0:T(8,128)S(1)}, u32[]{:S(2)}, u32[]{:S(2)}) collective-permute-start(f32[512,128]{1,0:T(8,128)} %collective-permute-done.1.refs_0_), channel_id=1, source_target_pairs={{0,1},{1,0},{2,3},{3,2},{4,5},{5,4},{6,7},{7,6},{8,9},{9,8},{10,11... | collective-permute-start | bytes 786440 | tf_op jit(solution)/shard_map/ppermute | solution.py:280
  53.4 5.2 %collective-permute-start.4 = (f32[512,128]{1,0:T(8,128)S(1)}, f32[512,128]{1,0:T(8,128)S(1)}, u32[]{:S(2)}, u32[]{:S(2)}) collective-permute-start(f32[512,128]{1,0:T(8,128)S(1)} %collective-permute-done.3.refs_2_), channel_id=1, source_target_pairs={{0,1},{1,0},{2,3},{3,2},{4,5},{5,4},{6,7},{7,6},{8,9},{9,8},{10,11... | collective-permute-start | bytes 786440 | tf_op jit(solution)/shard_map/ppermute | solution.py:280
  53.5 5.2 %collective-permute-start.6 = (f32[512,128]{1,0:T(8,128)S(1)}, f32[512,128]{1,0:T(8,128)S(1)}, u32[]{:S(2)}, u32[]{:S(2)}) collective-permute-start(f32[512,128]{1,0:T(8,128)S(1)} %collective-permute-done.5.refs_4_), channel_id=1, source_target_pairs={{0,1},{1,0},{2,3},{3,2},{4,5},{5,4},{6,7},{7,6},{8,9},{9,8},{10,11... | collective-permute-start | bytes 786440 | tf_op jit(solution)/shard_map/ppermute | solution.py:280
  53.9 4.7 %collective-permute-start.8 = (f32[512,128]{1,0:T(8,128)S(1)}, f32[512,128]{1,0:T(8,128)S(1)}, u32[]{:S(2)}, u32[]{:S(2)}) collective-permute-start(f32[512,128]{1,0:T(8,128)S(1)} %collective-permute-done.7.refs_6_), channel_id=1, source_target_pairs={{0,1},{1,0},{2,3},{3,2},{4,5},{5,4},{6,7},{7,6},{8,9},{9,8},{10,11... | collective-permute-start | bytes 786440 | tf_op jit(solution)/shard_map/ppermute | solution.py:280
  58.6 11.7 %copy-start = (f32[1,512,256]{2,1,0:T(8,128)S(1)}, f32[1,512,256]{2,1,0:T(8,128)}, u32[]{:S(2)}) copy-start(f32[1,512,256]{2,1,0:T(8,128)} %param.17) | copy-start | bytes 1572868
  58.6 11.7 %copy-start.3 = (f32[128,256]{1,0:T(8,128)S(1)}, f32[128,256]{1,0:T(8,128)}, u32[]{:S(2)}) copy-start(f32[128,256]{1,0:T(8,128)} %self_weight.1) | copy-start | bytes 393220
  62.3 8.0 %collective-permute-start.15 = (f32[512,128]{1,0:T(8,128)S(1)}, f32[512,128]{1,0:T(8,128)S(1)}, u32[]{:S(2)}, u32[]{:S(2)}) collective-permute-start(f32[512,128]{1,0:T(8,128)S(1)} %get-tuple-element.10), channel_id=1, source_target_pairs={{0,16},{1,17},{2,18},{3,19},{4,20},{5,21},{6,22},{7,23},{8,24},{9,... | collective-permute-start | bytes 786440 | tf_op jit(solution)/shard_map/ppermute | solution.py:280
  72.0 1.4 %collective-permute-start.16 = (f32[136,256]{1,0:T(8,128)S(1)}, f32[136,256]{1,0:T(8,128)S(1)}, u32[]{:S(2)}, u32[]{:S(2)}) collective-permute-start(f32[136,256]{1,0:T(8,128)S(1)} %get-tuple-element.13), channel_id=1, source_target_pairs={{0,1},{1,0},{2,3},{3,2},{4,5},{5,4},{6,7},{7,6},{8,9},{9,8},{10,11... | collective-permute-start | bytes 417800 | tf_op jit(solution)/shard_map/ppermute | solution.py:280
  73.4 5.8 %collective-permute-start.17 = (f32[136,256]{1,0:T(8,128)S(1)}, f32[136,256]{1,0:T(8,128)S(1)}, u32[]{:S(2)}, u32[]{:S(2)}) collective-permute-start(f32[136,256]{1,0:T(8,128)S(1)} %add.125), channel_id=1, source_target_pairs={{0,16},{1,17},{2,18},{3,19},{4,20},{5,21},{6,22},{7,23},{8,24},{9,... | collective-permute-start | bytes 417800 | tf_op jit(solution)/shard_map/ppermute | solution.py:280
  79.2 5.1 %collective-permute-start.18 = (f32[136,256]{1,0:T(8,128)S(1)}, f32[136,256]{1,0:T(8,128)S(1)}, u32[]{:S(2)}, u32[]{:S(2)}) collective-permute-start(f32[136,256]{1,0:T(8,128)S(1)} %add.126), channel_id=1, source_target_pairs={{0,2},{1,3},{2,0},{3,1},{4,6},{5,7},{6,4},{7,5},{8,10},{9,11},{10,... | collective-permute-start | bytes 417800 | tf_op jit(solution)/shard_map/ppermute | solution.py:280
  84.4 5.1 %collective-permute-start.19 = (f32[136,256]{1,0:T(8,128)S(1)}, f32[136,256]{1,0:T(8,128)S(1)}, u32[]{:S(2)}, u32[]{:S(2)}) collective-permute-start(f32[136,256]{1,0:T(8,128)S(1)} %add.127), channel_id=1, source_target_pairs={{0,4},{1,5},{2,6},{3,7},{4,0},{5,1},{6,2},{7,3},{8,12},{9,13},{10,... | collective-permute-start | bytes 417800 | tf_op jit(solution)/shard_map/ppermute | solution.py:280
  89.5 7.8 %collective-permute-start.20 = (f32[136,256]{1,0:T(8,128)S(1)}, f32[136,256]{1,0:T(8,128)S(1)}, u32[]{:S(2)}, u32[]{:S(2)}) collective-permute-start(f32[136,256]{1,0:T(8,128)S(1)} %add.128), channel_id=1, source_target_pairs={{0,8},{1,9},{2,10},{3,11},{4,12},{5,13},{6,14},{7,15},{8,0},{9,1},... | collective-permute-start | bytes 417800 | tf_op jit(solution)/shard_map/ppermute | solution.py:280
  97.3 1.4 %collective-permute-start.21 = (f32[136,256]{1,0:T(8,128)S(1)}, f32[136,256]{1,0:T(8,128)S(1)}, u32[]{:S(2)}, u32[]{:S(2)}) collective-permute-start(f32[136,256]{1,0:T(8,128)S(1)} %add.129), channel_id=1, source_target_pairs={{0,1},{1,0},{2,3},{3,2},{4,5},{5,4},{6,7},{7,6},{8,9},{9,8},{10,11... | collective-permute-start | bytes 417800 | tf_op jit(solution)/shard_map/ppermute | solution.py:280
  (9 other events, 34.1 us)

commit v2 on v1

v2 whole, which is shorter than its diff:
```python
import functools

import jax
import jax.numpy as jnp
from jax import lax
from jax.experimental import pallas as pl
from jax.experimental.pallas import tpu as pltpu
from jax.sharding import PartitionSpec as P

VMEM = pltpu.VMEM
SMEM = pltpu.SMEM
F32 = jnp.float32
BF16 = jnp.bfloat16
LIMIT = 24 * 1024 * 1024
GROUP = 4
COST = 10


def split(value):
    high = value.astype(BF16)
    low = (value - high.astype(F32)).astype(BF16)
    return high, low


def dot3(left, right, dims):
    lh, ll = left
    rh, rl = right
    mul = functools.partial(
        lax.dot_general, dimension_numbers=(dims, ((), ())), preferred_element_type=F32
    )
    return mul(lh, rh) + (mul(lh, rl) + mul(ll, rh))


def spec(space):
    return pl.BlockSpec(memory_space=space)


def tiles_kernel(goals, pieces, has_acc, finish, slots, stops, rows, cols, counts, *refs):
    blocks = []
    for count in pieces:
        blocks.append(refs[:count])
        refs = refs[count:]
    tiles, refs = refs[0], refs[1:]
    if has_acc:
        acc_in, refs = refs[0], refs[1:]
    if finish:
        keep, send, acc, pair = refs
    else:
        acc, pair = refs
    row = lax.axis_index("row")
    col = lax.axis_index("col")
    across = lax.axis_size("col")
    if has_acc:
        acc[...] = acc_in[...]
    else:
        acc[...] = jnp.zeros_like(acc)
    width = acc.shape[1]
    side = tiles.shape[1]
    for goal, block in zip(goals, blocks):
        stop = lax.rem(col - stops * row - goal(row, col) + 2 * across, across)

        @pl.when(stop < stops)
        def _(block=block, stop=stop):
            for place, piece in enumerate(block):
                high, low = split(piece[...].reshape(-1, width))
                size = high.shape[0]
                if len(block) == 1:
                    start = 0
                else:
                    start = pl.multiple_of((1 - row if place else row) * size, size)
                pair[pl.ds(start, size), :width] = high
                pair[pl.ds(start, size), width:] = low
            live = counts[0, 0, stop]
            base = stop * slots
            for first in range(0, slots, GROUP):
                here = range(first, min(first + GROUP, slots))

                @pl.when(first < live)
                def _(here=here):
                    prods = []
                    for t in here:
                        at = pl.multiple_of(cols[0, 0, base + t] * side, side)
                        both = jnp.dot(
                            tiles[base + t], pair[pl.ds(at, side), :],
                            preferred_element_type=F32,
                        )
                        prods.append(both[:, :width] + both[:, width:])
                    for t, prod in zip(here, prods):
                        at = pl.multiple_of(rows[0, 0, base + t] * side, side)
                        acc[pl.ds(at, side), :] += jnp.where(t < live, prod, 0.0)

    if finish:
        half = keep.shape[0]
        for out, place in ((keep, row), (send, 1 - row)):
            out[...] = acc[pl.ds(pl.multiple_of(place * half, half), half), :]


def add_products(blocks, goals, index, stops, tiles, acc, finish):
    blocks = [b if isinstance(b, tuple) else (b,) for b in blocks]
    pieces = tuple(len(b) for b in blocks)
    flat = [piece for b in blocks for piece in b]
    n = len(blocks)
    width = flat[0].shape[-1]
    nodes = sum(piece.size for piece in blocks[0]) // width
    slots = tiles.shape[0] // stops
    side = tiles.shape[1]
    whole = jax.ShapeDtypeStruct((nodes, width), F32)
    part = jax.ShapeDtypeStruct((nodes // 2, width), F32)
    body = functools.partial(
        tiles_kernel, tuple(goals), pieces, acc is not None, finish, slots, stops
    )
    scratch = [VMEM((nodes, 2 * width), BF16)]
    if finish:
        scratch = [VMEM((nodes, width), F32)] + scratch
    return pl.pallas_call(
        body,
        out_shape=(part, part) if finish else whole,
        in_specs=[spec(SMEM)] * 3
        + [spec(VMEM)] * (len(flat) + 1)
        + ([spec(VMEM)] if acc is not None else []),
        out_specs=(spec(VMEM),) * 2 if finish else spec(VMEM),
        scratch_shapes=scratch,
        compiler_params=pltpu.CompilerParams(vmem_limit_bytes=LIMIT),
        cost_estimate=pl.CostEstimate(
            flops=n * slots * side * side * width * COST,
            bytes_accessed=n * slots * side * side * 2,
            transcendentals=0,
        ),
    )(*index, *flat, tiles, *(() if acc is None else (acc,)))


def half_kernel(block, out):
    half = out.shape[0]
    at = pl.multiple_of(lax.axis_index("row") * half, half)
    out[...] = block[0, pl.ds(at, half), :]


def row_half(block):
    _, nodes, width = block.shape
    return pl.pallas_call(
        half_kernel,
        out_shape=jax.ShapeDtypeStruct((nodes // 2, width), F32),
        in_specs=[spec(VMEM)],
        out_specs=spec(VMEM),
        compiler_params=pltpu.CompilerParams(vmem_limit_bytes=LIMIT),
    )(block)


def gate_kernel(value, _, out):
    out[...] = value[...]


def gate(value, after):
    return pl.pallas_call(
        gate_kernel,
        out_shape=jax.ShapeDtypeStruct(value.shape, F32),
        in_specs=[spec(VMEM), spec(pl.ANY)],
        out_specs=spec(VMEM),
        compiler_params=pltpu.CompilerParams(vmem_limit_bytes=LIMIT),
        cost_estimate=pl.CostEstimate(
            flops=1024, bytes_accessed=8 * value.size, transcendentals=0
        ),
    )(value, after)


def layer_kernel(
    block, kept, got, self_weight, neigh_weight, bias, cotangent, output, keep, send
):
    depth = self_weight.shape[0]
    units = self_weight.shape[1]
    nodes = kept.shape[0]
    own = block[0, pl.ds(pl.multiple_of(lax.axis_index("row") * nodes, nodes), nodes), :]
    both = jnp.concatenate([own, kept[...] + got[...]], axis=1)
    inputs = split(both)
    weights = split(jnp.concatenate([self_weight[...], neigh_weight[...]], axis=0))
    pre = dot3(inputs, weights, ((1,), (0,))) + bias[...].reshape(1, units)
    root = 0.7978845608028654
    square = pre * pre
    bend = jnp.tanh(root * (pre + 0.044715 * (square * pre)))
    rise = 0.5 * (1.0 + bend)
    hidden = pre * rise
    scale = lax.rsqrt(jnp.mean(hidden * hidden, axis=-1, keepdims=True) + 1e-06)
    out = hidden * scale
    output[0] = out
    weight = cotangent[0]
    along = jnp.mean(weight * out, axis=-1, keepdims=True)
    slope = rise + (0.5 * root) * pre * (1.0 - bend * bend) * (
        1.0 + (3 * 0.044715) * square
    )
    back = scale * (weight - out * along) * slope
    grads = dot3(inputs, split(back), ((0,), (0,)))
    grad_bias = jnp.sum(back, axis=0, keepdims=True)
    first = lax.rem(lax.axis_index("col"), 2) == 0
    tail = jnp.broadcast_to(grad_bias, (8, units))
    keep[:depth, :] = jnp.where(first, grads[:depth], grads[depth:])
    send[:depth, :] = jnp.where(first, grads[depth:], grads[:depth])
    keep[depth:, :] = tail
    send[depth:, :] = tail


def run_layer(block, kept, got, self_weight, neigh_weight, bias, cotangent):
    nodes, depth = kept.shape
    units = self_weight.shape[1]
    part = jax.ShapeDtypeStruct((depth + 8, units), F32)
    return pl.pallas_call(
        layer_kernel,
        out_shape=(jax.ShapeDtypeStruct((1, nodes, units), F32), part, part),
        in_specs=[spec(VMEM)] * 7,
        out_specs=(spec(VMEM),) * 3,
        compiler_params=pltpu.CompilerParams(vmem_limit_bytes=LIMIT),
        cost_estimate=pl.CostEstimate(
            flops=12 * nodes * 2 * depth * units,
            bytes_accessed=nodes * units * 12,
            transcendentals=nodes * units,
        ),
    )(block, kept, got, self_weight, neigh_weight, bias, cotangent)


def grads_kernel(total, other, grad_self, grad_neigh, grad_bias):
    depth = grad_self.shape[0]
    first = lax.rem(lax.axis_index("col"), 2) == 0
    mine, theirs = total[:depth, :], other[:depth, :]
    grad_self[...] = jnp.where(first, mine, theirs)
    grad_neigh[...] = jnp.where(first, theirs, mine)
    grad_bias[...] = total[depth, :]


def place_grads(total, other):
    depth, units = total.shape[0] - 8, total.shape[1]
    part = jax.ShapeDtypeStruct((depth, units), F32)
    return pl.pallas_call(
        grads_kernel,
        out_shape=(part, part, jax.ShapeDtypeStruct((units,), F32)),
        in_specs=[spec(VMEM)] * 2,
        out_specs=(spec(VMEM),) * 3,
        compiler_params=pltpu.CompilerParams(vmem_limit_bytes=LIMIT),
    )(total, other)


def gather_small(block, send, add):
    swap = lambda value: send(value, lambda r, c: (r, c ^ 1))
    near_of = lambda r, c: lax.rem(c + 12 - 8 * r, 16)
    near = send(block, lambda r, c: (r, (c + (4 if r == 0 else 12)) % 16))
    far = send(row_half(block), lambda r, c: (r, c ^ 8))
    level = send(block, lambda r, c: (r, c ^ 2) if (c // 2) % 2 == r else None)
    beside = swap(block)
    cross = send(near, lambda r, c: (r, c ^ 2))
    level_beside = swap(level)
    near_beside = swap(near)
    over_x = send(far, lambda r, c: (1 - r, c))
    over_y = send(far, lambda r, c: (r, c ^ 2))
    over_d = send(far, lambda r, c: (1 - r, c ^ 2))
    acc = add(
        [block, beside, near, near_beside, level, level_beside],
        [
            lambda r, c: c, lambda r, c: c ^ 1, near_of,
            lambda r, c: near_of(r, c) ^ 1, lambda r, c: c ^ 2, lambda r, c: c ^ 3,
        ],
    )
    over_d = gate(over_d, acc)
    acc = add(
        [(far, over_x), (swap(far), swap(over_x)),
         (over_y, over_d), (swap(over_y), swap(over_d))],
        [lambda r, c, bits=bits: c ^ bits for bits in (8, 9, 10, 11)], acc,
    )
    return add(
        [cross, swap(cross)],
        [lambda r, c: near_of(r, c) ^ 2, lambda r, c: near_of(r, c) ^ 3], acc, True,
    )


def gather_ring(block, send, add, rows, cols, stops):
    held = send(block, lambda r, c: (r, (c + stops * r) % cols))
    held = jnp.where(lax.axis_index("row") == 0, block, held)
    acc = None
    for stop in range(stops):
        if stop:
            held = send(held, lambda r, c: (r, (c + 1) % cols))
        at = lambda r, c, stop=stop: lax.rem(c - stops * r - stop + 2 * cols, cols)
        acc = add([held], [at], acc)
    return acc


def on_device(
    features, self_weight, neigh_weight, bias, edge_tiles, tile_rows, tile_cols,
    tile_count, cotangent,
):
    rows = lax.axis_size("row")
    cols = lax.axis_size("col")
    stops = tile_count.shape[2]
    tiles = edge_tiles[0, 0]
    index = (tile_rows, tile_cols, tile_count)
    small = rows == 2 and cols == 16 and stops == 8

    def send(value, to):
        pairs = []
        for r in range(rows):
            for c in range(cols):
                goal = to(r, c)
                if goal is not None and goal != (r, c):
                    pairs.append((r * cols + c, goal[0] * cols + goal[1]))
        return lax.ppermute(value, ("row", "col"), pairs)

    def add(blocks, goals, acc=None, finish=False):
        return add_products(blocks, goals, index, stops, tiles, acc, finish)

    if small:
        kept, away = gather_small(features, send, add)
        got = send(away, lambda r, c: (1 - r, c))
    else:
        acc = gather_ring(features, send, add, rows, cols, stops)
        kept = lax.psum_scatter(acc, "row", scatter_dimension=0, tiled=True)
        got = jnp.zeros_like(kept)
    output, keep, away = run_layer(
        features, kept, got, self_weight, neigh_weight, bias, cotangent
    )
    swap = lambda value: send(value, lambda r, c: (r, c ^ 1))
    total = keep + swap(away)
    if small:
        total = total + send(total, lambda r, c: (1 - r, c))
    else:
        total = lax.psum(total, "row")
    bit = 2
    while bit < cols:
        total = total + send(total, lambda r, c: (r, c ^ bit))
        bit *= 2
    return (output, *place_grads(total, swap(total)))


def solution(mesh):
    in_specs = (
        P("col", None, None),
        P(),
        P(),
        P(),
        P("row", "col", None, None, None),
        P("row", "col", None),
        P("row", "col", None),
        P("row", "col", None),
        P("col", "row", None),
    )
    out_specs = (P("col", "row", None), P(), P(), P())
    return jax.shard_map(
        on_device, mesh=mesh, in_specs=in_specs, out_specs=out_specs, check_vma=False
    )
```

time: 100 us -> 89.8 us (0.90)
  waiting for transfers between devices: 53.5 us -> 46.4 us
  Pallas kernels: 13 us -> 9.53 us
  starting transfers between devices: 23.4 us -> 26.7 us
  other arithmetic: 2.82 us -> 0.1 us
    ppermute x22, waiting for transfers between devices: 53.5 us -> 46.4 us  [send(): return lax.ppermute(value, ('row', 'col'), pairs)]
    pallas_call x5 -> x3, Pallas kernels: 11.3 us -> 7.07 us  [add_products(): pl.pallas_call(body, out_shape=(part, part) if finish else whole, in_spec...]
    ppermute x22, starting transfers between devices: 23.4 us -> 26.7 us  [send(): return lax.ppermute(value, ('row', 'col'), pairs)]
    select_n x2 -> x0, other arithmetic: 2.41 us -> none  [the longest x1 1.68 us: gather_small(): mine = jnp.where(core == 1 - row, block, beside)]
    pallas_call x1 -> x4, Pallas kernels: 1.68 us -> 2.47 us  [the longest x1 1.71 us: run_layer(): pl.pallas_call(layer_kernel, out_shape=(jax.ShapeDtypeStruct((1, nodes, u...]
  transfers between devices with their start and end apart: 22 -> 22, of which waited for: 10 -> 12; matrix products, arithmetic and copies ran while one was open for 3% -> 0% of each run, Pallas kernels for 8% -> 6%
where the time goes in v2:
time: 89.8 us; the launch traced here: 88.4 us
  waiting for transfers between devices  46.4 us (52%)
  starting transfers between devices  26.7 us (30%)
  Pallas kernels  9.53 us (11%)
  local copies, waits for them, and re-layouts  4.92 us (5%)
    ppermute x22, waiting for transfers between devices, send(): return lax.ppermute(value, ('row', 'col'), pairs)  46.4 us
    ppermute x22, starting transfers between devices, send(): return lax.ppermute(value, ('row', 'col'), pairs)  26.7 us
    pallas_call x3, Pallas kernels, add_products(): pl.pallas_call(body, out_shape=(part, part) if finish else whole, in_spec...  7.07 us
    unnamed x22, local copies, waits for them, and re-layouts  4.92 us
  transfers between devices with their start and end apart: 22, of which 12 were waited for; matrix products, arithmetic and copies ran while one was open for 0% of the time, Pallas kernels for 6%

profile of v2, /device:TPU:0, one launch (start us, length us, event | category | flops | bytes accessed | tf_op | source)
XLA Modules:
  0.0 88.4 jit_solution(3190596595578512216)
XLA Ops:
  0.6 3.1 %collective-permute-start = (f32[1,1024,128]{2,1,0:T(8,128)}, f32[1,1024,128]{2,1,0:T(8,128)S(1)}, u32[]{:S(2)}, u32[]{:S(2)}) collective-permute-start(f32[1,1024,128]{2,1,0:T(8,128)} %block.3), channel_id=1, source_target_pairs={{0,4},{1,5},{2,6},{3,7},{4,8},{5,9},{6,10},{7,11},{8,12},{9,13},{1... | collective-permute-start | bytes 1572872 | tf_op jit(solution)/shard_map/ppermute | solution.py:302
  3.7 3.4 %collective-permute-start.11 = (f32[1,1024,128]{2,1,0:T(8,128)}, f32[1,1024,128]{2,1,0:T(8,128)S(1)}, u32[]{:S(2)}, u32[]{:S(2)}) collective-permute-start(f32[1,1024,128]{2,1,0:T(8,128)} %block.3), channel_id=1, source_target_pairs={{0,2},{1,3},{4,6},{5,7},{8,10},{9,11},{12,14},{13,15},{18,16},{19,... | collective-permute-start | bytes 1572872 | tf_op jit(solution)/shard_map/ppermute | solution.py:302
  8.3 2.7 %collective-permute-start.3 = (f32[512,128]{1,0:T(8,128)S(1)}, f32[512,128]{1,0:T(8,128)S(1)}, u32[]{:S(2)}, u32[]{:S(2)}) collective-permute-start(f32[512,128]{1,0:T(8,128)S(1)} %shard_map.120), channel_id=1, source_target_pairs={{0,8},{1,9},{2,10},{3,11},{4,12},{5,13},{6,14},{7,15},{8,0},{9,1},... | collective-permute-start | bytes 786440 | tf_op jit(solution)/shard_map/ppermute | solution.py:302
  11.0 7.8 %collective-permute-done.refs_2_ = f32[1,1024,128]{2,1,0:T(8,128)S(1)} collective-permute-done((f32[1,1024,128]{2,1,0:T(8,128)}, f32[1,1024,128]{2,1,0:T(8,128)S(1)}, u32[]{:S(2)}, u32[]{:S(2)}) %collective-permute-start) | collective-permute-done | bytes 524320 | tf_op jit(solution)/shard_map/ppermute | solution.py:302
  18.8 1.8 %collective-permute-start.1 = (f32[1,1024,128]{2,1,0:T(8,128)S(1)}, f32[1,1024,128]{2,1,0:T(8,128)S(1)}, u32[]{:S(2)}, u32[]{:S(2)}) collective-permute-start(f32[1,1024,128]{2,1,0:T(8,128)S(1)} %collective-permute-done.refs_2_), channel_id=1, source_target_pairs={{0,2},{1,3},{2,0},{3,1},{4,6},{5,7},{6,4},{7,5},{8,10},{9,11},{10,... | collective-permute-start | bytes 1572872 | tf_op jit(solution)/shard_map/ppermute | solution.py:302
  21.1 8.0 %collective-permute-done.3.refs_0_ = f32[512,128]{1,0:T(8,128)S(1)} collective-permute-done((f32[512,128]{1,0:T(8,128)S(1)}, f32[512,128]{1,0:T(8,128)S(1)}, u32[]{:S(2)}, u32[]{:S(2)}) %collective-permute-start.3) | collective-permute-done | bytes 262176 | tf_op jit(solution)/shard_map/ppermute | solution.py:302
  29.1 1.5 %collective-permute-start.7 = (f32[512,128]{1,0:T(8,128)S(1)}, f32[512,128]{1,0:T(8,128)S(1)}, u32[]{:S(2)}, u32[]{:S(2)}) collective-permute-start(f32[512,128]{1,0:T(8,128)S(1)} %collective-permute-done.3.refs_0_), channel_id=1, source_target_pairs={{0,2},{1,3},{2,0},{3,1},{4,6},{5,7},{6,4},{7,5},{8,10},{9,11},{10,... | collective-permute-start | bytes 786440 | tf_op jit(solution)/shard_map/ppermute | solution.py:302
  31.3 6.1 %collective-permute-done.7.refs_4_ = f32[512,128]{1,0:T(8,128)S(1)} collective-permute-done((f32[512,128]{1,0:T(8,128)S(1)}, f32[512,128]{1,0:T(8,128)S(1)}, u32[]{:S(2)}, u32[]{:S(2)}) %collective-permute-start.7) | collective-permute-done | bytes 262176 | tf_op jit(solution)/shard_map/ppermute | solution.py:302
  39.6 1.9 %copy-done = bf16[1,1,96,128,128]{4,3,2,1,0:T(8,128)(2,1)S(1)} copy-done((bf16[1,1,96,128,128]{4,3,2,1,0:T(8,128)(2,1)S(1)}, bf16[1,1,96,128,128]{4,3,2,1,0:T(8,128)(2,1)}, u32[]{:S(2)}) %copy-start) | copy-done | bytes 3145752
  43.4 2.6 %shard_map.121._.refs_9_ = f32[1024,128]{1,0:T(8,128)S(1)} custom-call(s32[1,1,96]{2,1,0:T(1,128)S(1)} %copy-done.7, s32[1,1,96]{2,1,0:T(1,128)S(1)} %copy-done.8, s32[1,1,8]{2,1,0:T(1,128)S(1)} %copy-done.9, f32[1,1024,128]{2,1,0:T(8,128)S(1)} %copy-done.2, f32[1,1024,128]{2,1,0:T(8,128)S(1)} %collective-permute-done.9.refs_1_, ...), custom_call_target="tpu_custom_call" | custom-call | flops 1509949440 | bytes 2359296 | tf_op jit(solution)/shard_map/pallas_call | solution.py:115
  48.2 2.5 %shard_map.123.refs_3_ = f32[1024,128]{1,0:T(8,128)S(1)} custom-call(s32[1,1,96]{2,1,0:T(1,128)S(1)} %copy-done.7, s32[1,1,96]{2,1,0:T(1,128)S(1)} %copy-done.8, s32[1,1,8]{2,1,0:T(1,128)S(1)} %copy-done.9, f32[512,128]{1,0:T(8,128)S(1)} %collective-permute-done.3.refs_0_, f32[512,128]{1,0:T(8,128)S(1)} %collective-permute-done.4.refs_1_, ...), custom_call_target="tpu_custom_call" | custom-call | flops 1006632960 | bytes 1572864 | tf_op jit(solution)/shard_map/pallas_call | solution.py:115
  50.7 2.0 %shard_map.124 = (f32[512,128]{1,0:T(8,128)S(1)}, f32[512,128]{1,0:T(8,128)S(1)}) custom-call(s32[1,1,96]{2,1,0:T(1,128)S(1)} %copy-done.7, s32[1,1,96]{2,1,0:T(1,128)S(1)} %copy-done.8, s32[1,1,8]{2,1,0:T(1,128)S(1)} %copy-done.9, f32[1,1024,128]{2,1,0:T(8,128)S(1)} %collective-permute-done.1.refs_0_, f32[1,1024,128]{2,1,0:T(8,128)S(1)} %collective-permute-done.2.refs_1_, ...), custom_call_target="tpu_custom_call" | custom-call | flops 503316480 | bytes 786432 | tf_op jit(solution)/shard_map/pallas_call | solution.py:115
  53.7 7.2 %collective-permute-done.15.got = f32[512,128]{1,0:T(8,128)S(1)} collective-permute-done((f32[512,128]{1,0:T(8,128)S(1)}, f32[512,128]{1,0:T(8,128)S(1)}, u32[]{:S(2)}, u32[]{:S(2)}) %collective-permute-start.15) | collective-permute-done | bytes 262176 | tf_op jit(solution)/shard_map/ppermute | solution.py:302
  60.9 1.7 %shard_map.125 = (f32[1,512,256]{2,1,0:T(8,128)}, f32[136,256]{1,0:T(8,128)S(1)}, f32[136,256]{1,0:T(8,128)S(1)}) custom-call(f32[1,1024,128]{2,1,0:T(8,128)S(1)} %copy-done.3, f32[512,128]{1,0:T(8,128)S(1)} %get-tuple-element.12.kept, f32[512,128]{1,0:T(8,128)S(1)} %collective-permute-done.15.got, f32[128,256]{1,0:T(8,128)S(1)} %copy-done.5, ...), custom_call_target="tpu_custom_call" | custom-call | flops 402653184 | bytes 1572864 | tf_op jit(solution)/shard_map/pallas_call | solution.py:205
  62.6 1.4 %collective-permute-done.16 = f32[136,256]{1,0:T(8,128)S(1)} collective-permute-done((f32[136,256]{1,0:T(8,128)S(1)}, f32[136,256]{1,0:T(8,128)S(1)}, u32[]{:S(2)}, u32[]{:S(2)}) %collective-permute-start.16) | collective-permute-done | bytes 139296 | tf_op jit(solution)/shard_map/ppermute | solution.py:302
  64.0 1.8 %collective-permute-start.17 = (f32[136,256]{1,0:T(8,128)S(1)}, f32[136,256]{1,0:T(8,128)S(1)}, u32[]{:S(2)}, u32[]{:S(2)}) collective-permute-start(f32[136,256]{1,0:T(8,128)S(1)} %add.15), channel_id=1, source_target_pairs={{0,16},{1,17},{2,18},{3,19},{4,20},{5,21},{6,22},{7,23},{8,24},{9,... | collective-permute-start | bytes 417800 | tf_op jit(solution)/shard_map/ppermute | solution.py:302
  65.8 4.0 %collective-permute-done.17 = f32[136,256]{1,0:T(8,128)S(1)} collective-permute-done((f32[136,256]{1,0:T(8,128)S(1)}, f32[136,256]{1,0:T(8,128)S(1)}, u32[]{:S(2)}, u32[]{:S(2)}) %collective-permute-start.17) | collective-permute-done | bytes 139296 | tf_op jit(solution)/shard_map/ppermute | solution.py:302
  69.8 2.1 %collective-permute-start.18 = (f32[136,256]{1,0:T(8,128)S(1)}, f32[136,256]{1,0:T(8,128)S(1)}, u32[]{:S(2)}, u32[]{:S(2)}) collective-permute-start(f32[136,256]{1,0:T(8,128)S(1)} %add.16), channel_id=1, source_target_pairs={{0,2},{1,3},{2,0},{3,1},{4,6},{5,7},{6,4},{7,5},{8,10},{9,11},{10,... | collective-permute-start | bytes 417800 | tf_op jit(solution)/shard_map/ppermute | solution.py:302
  71.9 3.2 %collective-permute-done.18 = f32[136,256]{1,0:T(8,128)S(1)} collective-permute-done((f32[136,256]{1,0:T(8,128)S(1)}, f32[136,256]{1,0:T(8,128)S(1)}, u32[]{:S(2)}, u32[]{:S(2)}) %collective-permute-start.18) | collective-permute-done | bytes 139296 | tf_op jit(solution)/shard_map/ppermute | solution.py:302
  75.0 2.1 %collective-permute-start.19 = (f32[136,256]{1,0:T(8,128)S(1)}, f32[136,256]{1,0:T(8,128)S(1)}, u32[]{:S(2)}, u32[]{:S(2)}) collective-permute-start(f32[136,256]{1,0:T(8,128)S(1)} %add.17), channel_id=1, source_target_pairs={{0,4},{1,5},{2,6},{3,7},{4,0},{5,1},{6,2},{7,3},{8,12},{9,13},{10,... | collective-permute-start | bytes 417800 | tf_op jit(solution)/shard_map/ppermute | solution.py:302
  77.1 3.0 %collective-permute-done.19 = f32[136,256]{1,0:T(8,128)S(1)} collective-permute-done((f32[136,256]{1,0:T(8,128)S(1)}, f32[136,256]{1,0:T(8,128)S(1)}, u32[]{:S(2)}, u32[]{:S(2)}) %collective-permute-start.19) | collective-permute-done | bytes 139296 | tf_op jit(solution)/shard_map/ppermute | solution.py:302
  80.2 3.0 %collective-permute-start.20 = (f32[136,256]{1,0:T(8,128)S(1)}, f32[136,256]{1,0:T(8,128)S(1)}, u32[]{:S(2)}, u32[]{:S(2)}) collective-permute-start(f32[136,256]{1,0:T(8,128)S(1)} %add.18), channel_id=1, source_target_pairs={{0,8},{1,9},{2,10},{3,11},{4,12},{5,13},{6,14},{7,15},{8,0},{9,1},... | collective-permute-start | bytes 417800 | tf_op jit(solution)/shard_map/ppermute | solution.py:302
  83.2 3.0 %collective-permute-done.20 = f32[136,256]{1,0:T(8,128)S(1)} collective-permute-done((f32[136,256]{1,0:T(8,128)S(1)}, f32[136,256]{1,0:T(8,128)S(1)}, u32[]{:S(2)}, u32[]{:S(2)}) %collective-permute-start.20) | collective-permute-done | bytes 139296 | tf_op jit(solution)/shard_map/ppermute | solution.py:302
  86.3 1.3 %collective-permute-done.21.other = f32[136,256]{1,0:T(8,128)S(1)} collective-permute-done((f32[136,256]{1,0:T(8,128)S(1)}, f32[136,256]{1,0:T(8,128)S(1)}, u32[]{:S(2)}, u32[]{:S(2)}) %collective-permute-start.21) | collective-permute-done | bytes 139296 | tf_op jit(solution)/shard_map/ppermute | solution.py:302
  (54 shorter events, 10.4 us)
Async XLA Ops:
  0.6 18.2 %collective-permute-start = (f32[1,1024,128]{2,1,0:T(8,128)}, f32[1,1024,128]{2,1,0:T(8,128)S(1)}, u32[]{:S(2)}, u32[]{:S(2)}) collective-permute-start(f32[1,1024,128]{2,1,0:T(8,128)} %block.3), channel_id=1, source_target_pairs={{0,4},{1,5},{2,6},{3,7},{4,8},{5,9},{6,10},{7,11},{8,12},{9,13},{1... | collective-permute-start | bytes 1572872 | tf_op jit(solution)/shard_map/ppermute | solution.py:302
  3.7 16.9 %collective-permute-start.11 = (f32[1,1024,128]{2,1,0:T(8,128)}, f32[1,1024,128]{2,1,0:T(8,128)S(1)}, u32[]{:S(2)}, u32[]{:S(2)}) collective-permute-start(f32[1,1024,128]{2,1,0:T(8,128)} %block.3), channel_id=1, source_target_pairs={{0,2},{1,3},{4,6},{5,7},{8,10},{9,11},{12,14},{13,15},{18,16},{19,... | collective-permute-start | bytes 1572872 | tf_op jit(solution)/shard_map/ppermute | solution.py:302
  7.2 23.5 %collective-permute-start.9 = (f32[1,1024,128]{2,1,0:T(8,128)}, f32[1,1024,128]{2,1,0:T(8,128)S(1)}, u32[]{:S(2)}, u32[]{:S(2)}) collective-permute-start(f32[1,1024,128]{2,1,0:T(8,128)} %block.3), channel_id=1, source_target_pairs={{0,1},{1,0},{2,3},{3,2},{4,5},{5,4},{6,7},{7,6},{8,9},{9,8},{10,11... | collective-permute-start | bytes 1572872 | tf_op jit(solution)/shard_map/ppermute | solution.py:302
  8.3 20.8 %collective-permute-start.3 = (f32[512,128]{1,0:T(8,128)S(1)}, f32[512,128]{1,0:T(8,128)S(1)}, u32[]{:S(2)}, u32[]{:S(2)}) collective-permute-start(f32[512,128]{1,0:T(8,128)S(1)} %shard_map.120), channel_id=1, source_target_pairs={{0,8},{1,9},{2,10},{3,11},{4,12},{5,13},{6,14},{7,15},{8,0},{9,1},... | collective-permute-start | bytes 786440 | tf_op jit(solution)/shard_map/ppermute | solution.py:302
  18.8 19.7 %collective-permute-start.1 = (f32[1,1024,128]{2,1,0:T(8,128)S(1)}, f32[1,1024,128]{2,1,0:T(8,128)S(1)}, u32[]{:S(2)}, u32[]{:S(2)}) collective-permute-start(f32[1,1024,128]{2,1,0:T(8,128)S(1)} %collective-permute-done.refs_2_), channel_id=1, source_target_pairs={{0,2},{1,3},{2,0},{3,1},{4,6},{5,7},{6,4},{7,5},{8,10},{9,11},{10,... | collective-permute-start | bytes 1572872 | tf_op jit(solution)/shard_map/ppermute | solution.py:302
  20.6 18.5 %collective-permute-start.10 = (f32[1,1024,128]{2,1,0:T(8,128)S(1)}, f32[1,1024,128]{2,1,0:T(8,128)S(1)}, u32[]{:S(2)}, u32[]{:S(2)}) collective-permute-start(f32[1,1024,128]{2,1,0:T(8,128)S(1)} %collective-permute-done.refs_2_), channel_id=1, source_target_pairs={{0,1},{1,0},{2,3},{3,2},{4,5},{5,4},{6,7},{7,6},{8,9},{9,8},{10,11... | collective-permute-start | bytes 1572872 | tf_op jit(solution)/shard_map/ppermute | solution.py:302
  20.6 18.6 %collective-permute-start.12 = (f32[1,1024,128]{2,1,0:T(8,128)S(1)}, f32[1,1024,128]{2,1,0:T(8,128)S(1)}, u32[]{:S(2)}, u32[]{:S(2)}) collective-permute-start(f32[1,1024,128]{2,1,0:T(8,128)S(1)} %collective-permute-done.11.refs_4_), channel_id=1, source_target_pairs={{0,1},{1,0},{2,3},{3,2},{4,5},{5,4},{6,7},{7,6},{8,9},{9,8},{10,11... | collective-permute-start | bytes 1572872 | tf_op jit(solution)/shard_map/ppermute | solution.py:302
  29.1 8.3 %collective-permute-start.7 = (f32[512,128]{1,0:T(8,128)S(1)}, f32[512,128]{1,0:T(8,128)S(1)}, u32[]{:S(2)}, u32[]{:S(2)}) collective-permute-start(f32[512,128]{1,0:T(8,128)S(1)} %collective-permute-done.3.refs_0_), channel_id=1, source_target_pairs={{0,2},{1,3},{2,0},{3,1},{4,6},{5,7},{6,4},{7,5},{8,10},{9,11},{10,... | collective-permute-start | bytes 786440 | tf_op jit(solution)/shard_map/ppermute | solution.py:302
  30.6 8.0 %collective-permute-start.4 = (f32[512,128]{1,0:T(8,128)S(1)}, f32[512,128]{1,0:T(8,128)S(1)}, u32[]{:S(2)}, u32[]{:S(2)}) collective-permute-start(f32[512,128]{1,0:T(8,128)S(1)} %collective-permute-done.3.refs_0_), channel_id=1, source_target_pairs={{0,16},{1,17},{2,18},{3,19},{4,20},{5,21},{6,22},{7,23},{8,24},{9,... | collective-permute-start | bytes 786440 | tf_op jit(solution)/shard_map/ppermute | solution.py:302
  37.4 8.6 %collective-permute-start.8 = (f32[512,128]{1,0:T(8,128)S(1)}, f32[512,128]{1,0:T(8,128)S(1)}, u32[]{:S(2)}, u32[]{:S(2)}) collective-permute-start(f32[512,128]{1,0:T(8,128)S(1)} %collective-permute-done.3.refs_0_), channel_id=1, source_target_pairs={{0,18},{1,19},{2,16},{3,17},{4,22},{5,23},{6,20},{7,21},{8,26},{9,... | collective-permute-start | bytes 786440 | tf_op jit(solution)/shard_map/ppermute | solution.py:302
  38.5 12.2 %collective-permute-start.2 = (f32[1,1024,128]{2,1,0:T(8,128)S(1)}, f32[1,1024,128]{2,1,0:T(8,128)S(1)}, u32[]{:S(2)}, u32[]{:S(2)}) collective-permute-start(f32[1,1024,128]{2,1,0:T(8,128)S(1)} %collective-permute-done.1.refs_0_), channel_id=1, source_target_pairs={{0,1},{1,0},{2,3},{3,2},{4,5},{5,4},{6,7},{7,6},{8,9},{9,8},{10,11... | collective-permute-start | bytes 1572872 | tf_op jit(solution)/shard_map/ppermute | solution.py:302
  38.6 8.4 %collective-permute-start.5 = (f32[512,128]{1,0:T(8,128)S(1)}, f32[512,128]{1,0:T(8,128)S(1)}, u32[]{:S(2)}, u32[]{:S(2)}) collective-permute-start(f32[512,128]{1,0:T(8,128)S(1)} %collective-permute-done.3.refs_0_), channel_id=1, source_target_pairs={{0,1},{1,0},{2,3},{3,2},{4,5},{5,4},{6,7},{7,6},{8,9},{9,8},{10,11... | collective-permute-start | bytes 786440 | tf_op jit(solution)/shard_map/ppermute | solution.py:302
  39.1 7.9 %collective-permute-start.13 = (f32[512,128]{1,0:T(8,128)S(1)}, f32[512,128]{1,0:T(8,128)S(1)}, u32[]{:S(2)}, u32[]{:S(2)}) collective-permute-start(f32[512,128]{1,0:T(8,128)S(1)} %collective-permute-done.7.refs_4_), channel_id=1, source_target_pairs={{0,1},{1,0},{2,3},{3,2},{4,5},{5,4},{6,7},{7,6},{8,9},{9,8},{10,11... | collective-permute-start | bytes 786440 | tf_op jit(solution)/shard_map/ppermute | solution.py:302
  39.1 7.8 %collective-permute-start.6 = (f32[512,128]{1,0:T(8,128)S(1)}, f32[512,128]{1,0:T(8,128)S(1)}, u32[]{:S(2)}, u32[]{:S(2)}) collective-permute-start(f32[512,128]{1,0:T(8,128)S(1)} %collective-permute-done.4.refs_1_), channel_id=1, source_target_pairs={{0,1},{1,0},{2,3},{3,2},{4,5},{5,4},{6,7},{7,6},{8,9},{9,8},{10,11... | collective-permute-start | bytes 786440 | tf_op jit(solution)/shard_map/ppermute | solution.py:302
  46.0 2.1 %collective-permute-start.14 = (f32[512,128]{1,0:T(8,128)S(1)}, f32[512,128]{1,0:T(8,128)S(1)}, u32[]{:S(2)}, u32[]{:S(2)}) collective-permute-start(f32[512,128]{1,0:T(8,128)S(1)} %shard_map.122.refs_5_), channel_id=1, source_target_pairs={{0,1},{1,0},{2,3},{3,2},{4,5},{5,4},{6,7},{7,6},{8,9},{9,8},{10,11... | collective-permute-start | bytes 786440 | tf_op jit(solution)/shard_map/ppermute | solution.py:302
  50.7 10.2 %copy-start.3 = (f32[1,1024,128]{2,1,0:T(8,128)S(1)}, f32[1,1024,128]{2,1,0:T(8,128)}, u32[]{:S(2)}) copy-start(f32[1,1024,128]{2,1,0:T(8,128)} %block.3) | copy-start | bytes 1572868
  50.7 10.2 %copy-start.4 = (f32[1,512,256]{2,1,0:T(8,128)S(1)}, f32[1,512,256]{2,1,0:T(8,128)}, u32[]{:S(2)}) copy-start(f32[1,512,256]{2,1,0:T(8,128)} %cotangent.1) | copy-start | bytes 1572868
  52.7 8.1 %collective-permute-start.15 = (f32[512,128]{1,0:T(8,128)S(1)}, f32[512,128]{1,0:T(8,128)S(1)}, u32[]{:S(2)}, u32[]{:S(2)}) collective-permute-start(f32[512,128]{1,0:T(8,128)S(1)} %get-tuple-element.13), channel_id=1, source_target_pairs={{0,16},{1,17},{2,18},{3,19},{4,20},{5,21},{6,22},{7,23},{8,24},{9,... | collective-permute-start | bytes 786440 | tf_op jit(solution)/shard_map/ppermute | solution.py:302
  62.6 1.4 %collective-permute-start.16 = (f32[136,256]{1,0:T(8,128)S(1)}, f32[136,256]{1,0:T(8,128)S(1)}, u32[]{:S(2)}, u32[]{:S(2)}) collective-permute-start(f32[136,256]{1,0:T(8,128)S(1)} %get-tuple-element.16), channel_id=1, source_target_pairs={{0,1},{1,0},{2,3},{3,2},{4,5},{5,4},{6,7},{7,6},{8,9},{9,8},{10,11... | collective-permute-start | bytes 417800 | tf_op jit(solution)/shard_map/ppermute | solution.py:302
  64.0 5.8 %collective-permute-start.17 = (f32[136,256]{1,0:T(8,128)S(1)}, f32[136,256]{1,0:T(8,128)S(1)}, u32[]{:S(2)}, u32[]{:S(2)}) collective-permute-start(f32[136,256]{1,0:T(8,128)S(1)} %add.15), channel_id=1, source_target_pairs={{0,16},{1,17},{2,18},{3,19},{4,20},{5,21},{6,22},{7,23},{8,24},{9,... | collective-permute-start | bytes 417800 | tf_op jit(solution)/shard_map/ppermute | solution.py:302
  69.8 5.2 %collective-permute-start.18 = (f32[136,256]{1,0:T(8,128)S(1)}, f32[136,256]{1,0:T(8,128)S(1)}, u32[]{:S(2)}, u32[]{:S(2)}) collective-permute-start(f32[136,256]{1,0:T(8,128)S(1)} %add.16), channel_id=1, source_target_pairs={{0,2},{1,3},{2,0},{3,1},{4,6},{5,7},{6,4},{7,5},{8,10},{9,11},{10,... | collective-permute-start | bytes 417800 | tf_op jit(solution)/shard_map/ppermute | solution.py:302
  75.0 5.1 %collective-permute-start.19 = (f32[136,256]{1,0:T(8,128)S(1)}, f32[136,256]{1,0:T(8,128)S(1)}, u32[]{:S(2)}, u32[]{:S(2)}) collective-permute-start(f32[136,256]{1,0:T(8,128)S(1)} %add.17), channel_id=1, source_target_pairs={{0,4},{1,5},{2,6},{3,7},{4,0},{5,1},{6,2},{7,3},{8,12},{9,13},{10,... | collective-permute-start | bytes 417800 | tf_op jit(solution)/shard_map/ppermute | solution.py:302
  80.2 6.1 %collective-permute-start.20 = (f32[136,256]{1,0:T(8,128)S(1)}, f32[136,256]{1,0:T(8,128)S(1)}, u32[]{:S(2)}, u32[]{:S(2)}) collective-permute-start(f32[136,256]{1,0:T(8,128)S(1)} %add.18), channel_id=1, source_target_pairs={{0,8},{1,9},{2,10},{3,11},{4,12},{5,13},{6,14},{7,15},{8,0},{9,1},... | collective-permute-start | bytes 417800 | tf_op jit(solution)/shard_map/ppermute | solution.py:302
  86.3 1.4 %collective-permute-start.21 = (f32[136,256]{1,0:T(8,128)S(1)}, f32[136,256]{1,0:T(8,128)S(1)}, u32[]{:S(2)}, u32[]{:S(2)}) collective-permute-start(f32[136,256]{1,0:T(8,128)S(1)} %add.19.total), channel_id=1, source_target_pairs={{0,1},{1,0},{2,3},{3,2},{4,5},{5,4},{6,7},{7,6},{8,9},{9,8},{10,11... | collective-permute-start | bytes 417800 | tf_op jit(solution)/shard_map/ppermute | solution.py:302
  (9 other events, 40.1 us)

commit v3 on v2

--- a/solution.py
+++ b/solution.py
@@ -38,8 +38,12 @@
 def tiles_kernel(goals, pieces, has_acc, finish, slots, stops, rows, cols, counts, *refs):
     blocks = []
     for count in pieces:
-        blocks.append(refs[:count])
-        refs = refs[count:]
+        if count < 0:
+            blocks += [(refs[0].at[at],) for at in range(-count)]
+            refs = refs[1:]
+        else:
+            blocks.append(refs[:count])
+            refs = refs[count:]
     tiles, refs = refs[0], refs[1:]
     if has_acc:
         acc_in, refs = refs[0], refs[1:]
@@ -50,10 +54,10 @@
     row = lax.axis_index("row")
     col = lax.axis_index("col")
     across = lax.axis_size("col")
-    if has_acc:
+    if not has_acc:
+        acc[...] = jnp.zeros_like(acc)
+    elif finish:
         acc[...] = acc_in[...]
-    else:
-        acc[...] = jnp.zeros_like(acc)
     width = acc.shape[1]
     side = tiles.shape[1]
     for goal, block in zip(goals, blocks):
@@ -62,7 +66,7 @@
         @pl.when(stop < stops)
         def _(block=block, stop=stop):
             for place, piece in enumerate(block):
-                high, low = split(piece[...].reshape(-1, width))
+                high, low = split(piece[...])
                 size = high.shape[0]
                 if len(block) == 1:
                     start = 0
@@ -95,13 +99,13 @@
             out[...] = acc[pl.ds(pl.multiple_of(place * half, half), half), :]
 
 
-def add_products(blocks, goals, index, stops, tiles, acc, finish):
+def add_products(blocks, goals, index, stops, tiles, acc, finish, cost):
     blocks = [b if isinstance(b, tuple) else (b,) for b in blocks]
-    pieces = tuple(len(b) for b in blocks)
+    pieces = tuple(len(b) if len(b) > 1 else -b[0].shape[0] for b in blocks)
     flat = [piece for b in blocks for piece in b]
-    n = len(blocks)
+    n = len(goals)
     width = flat[0].shape[-1]
-    nodes = sum(piece.size for piece in blocks[0]) // width
+    nodes = max(len(b) * b[0].shape[-2] for b in blocks)
     slots = tiles.shape[0] // stops
     side = tiles.shape[1]
     whole = jax.ShapeDtypeStruct((nodes, width), F32)
@@ -120,9 +124,10 @@
         + ([spec(VMEM)] if acc is not None else []),
         out_specs=(spec(VMEM),) * 2 if finish else spec(VMEM),
         scratch_shapes=scratch,
+        input_output_aliases={} if finish or acc is None else {len(flat) + 4: 0},
         compiler_params=pltpu.CompilerParams(vmem_limit_bytes=LIMIT),
         cost_estimate=pl.CostEstimate(
-            flops=n * slots * side * side * width * COST,
+            flops=n * slots * side * side * width * cost,
             bytes_accessed=n * slots * side * side * 2,
             transcendentals=0,
         ),
@@ -131,7 +136,8 @@
 
 def half_kernel(block, out):
     half = out.shape[0]
-    at = pl.multiple_of(lax.axis_index("row") * half, half)
+    row = lax.axis_index("row")
+    at = pl.multiple_of(row * half, half)
     out[...] = block[0, pl.ds(at, half), :]
 
 
@@ -146,21 +152,34 @@
     )(block)
 
 
-def gate_kernel(value, _, out):
-    out[...] = value[...]
-
-
-def gate(value, after):
-    return pl.pallas_call(
-        gate_kernel,
-        out_shape=jax.ShapeDtypeStruct(value.shape, F32),
-        in_specs=[spec(VMEM), spec(pl.ANY)],
+ROW, OTHER = "row", "other"
+
+
+def bundle_kernel(places, *refs):
+    out = refs[-1]
+    row = lax.axis_index("row")
+    for ref, (block, half) in zip(refs, places):
+        if half is None:
+            out[block] = ref[0]
+            continue
+        size = ref.shape[0]
+        half = {ROW: row, OTHER: 1 - row}.get(half, half)
+        out[block, pl.ds(pl.multiple_of(half * size, size), size), :] = ref[...]
+
+
+def bundle(pieces, blocks, after=()):
+    piece, (_, half) = pieces[0]
+    nodes, width = piece.shape[-2] * (1 if half is None else 2), piece.shape[-1]
+    return pl.pallas_call(
+        functools.partial(bundle_kernel, tuple(place for _, place in pieces)),
+        out_shape=jax.ShapeDtypeStruct((blocks, nodes, width), F32),
+        in_specs=[spec(VMEM)] * len(pieces) + [spec(pl.ANY)] * len(after),
         out_specs=spec(VMEM),
         compiler_params=pltpu.CompilerParams(vmem_limit_bytes=LIMIT),
         cost_estimate=pl.CostEstimate(
-            flops=1024, bytes_accessed=8 * value.size, transcendentals=0
+            flops=1024, bytes_accessed=8 * nodes * width * blocks, transcendentals=0
         ),
-    )(value, after)
+    )(*[piece for piece, _ in pieces], *after)
 
 
 def layer_kernel(
@@ -238,35 +257,31 @@
 
 
 def gather_small(block, send, add):
+    after = lax.optimization_barrier
     swap = lambda value: send(value, lambda r, c: (r, c ^ 1))
     near_of = lambda r, c: lax.rem(c + 12 - 8 * r, 16)
     near = send(block, lambda r, c: (r, (c + (4 if r == 0 else 12)) % 16))
     far = send(row_half(block), lambda r, c: (r, c ^ 8))
     level = send(block, lambda r, c: (r, c ^ 2) if (c // 2) % 2 == r else None)
     beside = swap(block)
+    acc = add([block, beside], [lambda r, c: c, lambda r, c: c ^ 1])
+    near, acc = after((near, acc))
     cross = send(near, lambda r, c: (r, c ^ 2))
     level_beside = swap(level)
     near_beside = swap(near)
     over_x = send(far, lambda r, c: (1 - r, c))
     over_y = send(far, lambda r, c: (r, c ^ 2))
     over_d = send(far, lambda r, c: (1 - r, c ^ 2))
-    acc = add(
-        [block, beside, near, near_beside, level, level_beside],
-        [
-            lambda r, c: c, lambda r, c: c ^ 1, near_of,
-            lambda r, c: near_of(r, c) ^ 1, lambda r, c: c ^ 2, lambda r, c: c ^ 3,
-        ],
-    )
-    over_d = gate(over_d, acc)
-    acc = add(
-        [(far, over_x), (swap(far), swap(over_x)),
-         (over_y, over_d), (swap(over_y), swap(over_d))],
-        [lambda r, c, bits=bits: c ^ bits for bits in (8, 9, 10, 11)], acc,
-    )
-    return add(
-        [cross, swap(cross)],
-        [lambda r, c: near_of(r, c) ^ 2, lambda r, c: near_of(r, c) ^ 3], acc, True,
-    )
+    cross_beside = swap(cross)
+    acc = add([near, level], [near_of, lambda r, c: c ^ 2], acc)
+    far_pair = bundle([(far, (0, ROW)), (over_x, (0, OTHER))], 1, (acc,))
+    far_beside = swap(far_pair)
+    acc = add([near_beside, level_beside, cross, far_pair], [lambda r, c: near_of(r, c) ^ 1, lambda r, c: c ^ 3, lambda r, c: near_of(r, c) ^ 2, lambda r, c: c ^ 8], acc)
+    over_pair = bundle([(over_y, (0, ROW)), (over_d, (0, OTHER))], 1, (acc,))
+    over_beside = swap(over_pair)
+    acc = add([far_beside, cross_beside, over_pair], [lambda r, c: c ^ 9, lambda r, c: near_of(r, c) ^ 3, lambda r, c: c ^ 10], acc)
+    acc = add([over_beside], [lambda r, c: c ^ 11], acc, True)
+    return acc
 
 
 def gather_ring(block, send, add, rows, cols, stops):
@@ -301,8 +316,8 @@
                     pairs.append((r * cols + c, goal[0] * cols + goal[1]))
         return lax.ppermute(value, ("row", "col"), pairs)
 
-    def add(blocks, goals, acc=None, finish=False):
-        return add_products(blocks, goals, index, stops, tiles, acc, finish)
+    def add(blocks, goals, acc=None, finish=False, cost=COST):
+        return add_products(blocks, goals, index, stops, tiles, acc, finish, cost)
 
     if small:
         kept, away = gather_small(features, send, add)

time: 89.8 us -> 87.3 us (0.972); the launches traced: 88.4 us -> 86.9 us
  starting transfers between devices: 26.7 us -> 20.8 us
  waiting for transfers between devices: 46.4 us -> 49.9 us
    ppermute x22 -> x20, starting transfers between devices: 26.7 us -> 20.8 us  [send(): return lax.ppermute(value, ('row', 'col'), pairs)]
    ppermute x22 -> x20, waiting for transfers between devices: 46.4 us -> 49.9 us  [send(): return lax.ppermute(value, ('row', 'col'), pairs)]
    pallas_call x3 -> x5, Pallas kernels: 7.07 us -> 7.76 us  [add_products(): pl.pallas_call(body, out_shape=(part, part) if finish else whole, in_spec...]
    unnamed x22 -> x28, local copies, waits for them, and re-layouts: 4.92 us -> 4.96 us
  transfers between devices with their start and end apart: 22 -> 20, of which waited for: 12 -> 11; matrix products, arithmetic and copies ran while one was open for 0% -> 0% of each run, Pallas kernels for 6% -> 8%
where the time goes in v3:
time: 87.3 us; the launch traced here: 86.9 us
  waiting for transfers between devices  49.9 us (57%)
  starting transfers between devices  20.8 us (24%)
  Pallas kernels  10.3 us (12%)
  local copies, waits for them, and re-layouts  4.96 us (6%)
  between operations  0.88 us (1%)
    ppermute x20, waiting for transfers between devices, send(): return lax.ppermute(value, ('row', 'col'), pairs)  49.9 us
    ppermute x20, starting transfers between devices, send(): return lax.ppermute(value, ('row', 'col'), pairs)  20.8 us
    pallas_call x5, Pallas kernels, add_products(): pl.pallas_call(body, out_shape=(part, part) if finish else whole, in_spec...  7.76 us
    unnamed x28, local copies, waits for them, and re-layouts  4.96 us
  transfers between devices with their start and end apart: 20, of which 11 were waited for; matrix products, arithmetic and copies ran while one was open for 0% of the time, Pallas kernels for 8%

profile of v3, /device:TPU:0, one launch (start us, length us, event | category | flops | bytes accessed | tf_op | source)
XLA Modules:
  0.0 86.9 jit_solution(10317691758971895063)
XLA Ops:
  1.1 2.6 %collective-permute-start.3 = (f32[1,1024,128]{2,1,0:T(8,128)}, f32[1,1024,128]{2,1,0:T(8,128)S(1)}, u32[]{:S(2)}, u32[]{:S(2)}) collective-permute-start(f32[1,1024,128]{2,1,0:T(8,128)} %block.3), channel_id=1, source_target_pairs={{0,4},{1,5},{2,6},{3,7},{4,8},{5,9},{6,10},{7,11},{8,12},{9,13},{1... | collective-permute-start | bytes 1572872 | tf_op jit(solution)/shard_map/ppermute | solution.py:317
  3.8 3.4 %collective-permute-start.6 = (f32[1,1024,128]{2,1,0:T(8,128)}, f32[1,1024,128]{2,1,0:T(8,128)S(1)}, u32[]{:S(2)}, u32[]{:S(2)}) collective-permute-start(f32[1,1024,128]{2,1,0:T(8,128)} %block.3), channel_id=1, source_target_pairs={{0,2},{1,3},{4,6},{5,7},{8,10},{9,11},{12,14},{13,15},{18,16},{19,... | collective-permute-start | bytes 1572872 | tf_op jit(solution)/shard_map/ppermute | solution.py:317
  8.3 2.7 %collective-permute-start = (f32[512,128]{1,0:T(8,128)S(1)}, f32[512,128]{1,0:T(8,128)S(1)}, u32[]{:S(2)}, u32[]{:S(2)}) collective-permute-start(f32[512,128]{1,0:T(8,128)S(1)} %shard_map.120), channel_id=1, source_target_pairs={{0,8},{1,9},{2,10},{3,11},{4,12},{5,13},{6,14},{7,15},{8,0},{9,1},... | collective-permute-start | bytes 786440 | tf_op jit(solution)/shard_map/ppermute | solution.py:317
  11.0 1.9 %copy-done = bf16[1,1,96,128,128]{4,3,2,1,0:T(8,128)(2,1)S(1)} copy-done((bf16[1,1,96,128,128]{4,3,2,1,0:T(8,128)(2,1)S(1)}, bf16[1,1,96,128,128]{4,3,2,1,0:T(8,128)(2,1)}, u32[]{:S(2)}) %copy-start) | copy-done | bytes 3145752
  14.9 1.4 %shard_map.121.refs_3_ = f32[1024,128]{1,0:T(8,128)S(1)} custom-call(s32[1,1,96]{2,1,0:T(1,128)S(1)} %copy-done.7, s32[1,1,96]{2,1,0:T(1,128)S(1)} %copy-done.9, s32[1,1,8]{2,1,0:T(1,128)S(1)} %copy-done.11, f32[1,1024,128]{2,1,0:T(8,128)S(1)} %copy-done.2, f32[1,1024,128]{2,1,0:T(8,128)S(1)} %collective-permute-done.4.refs_1_, bf16[96,128,128]{2,1,0:T(8,128)(2,1)S(1)} %bitcast.1), custom_call_target="tpu_custom_call" | custom-call | flops 503316480 | bytes 786432 | tf_op jit(solution)/shard_map/pallas_call | solution.py:119
  16.2 2.7 %collective-permute-done.3.refs_0_ = f32[1,1024,128]{2,1,0:T(8,128)S(1)} collective-permute-done((f32[1,1024,128]{2,1,0:T(8,128)}, f32[1,1024,128]{2,1,0:T(8,128)S(1)}, u32[]{:S(2)}, u32[]{:S(2)}) %collective-permute-start.3) | collective-permute-done | bytes 524320 | tf_op jit(solution)/shard_map/ppermute | solution.py:317
  18.9 1.7 %collective-permute-start.8 = (f32[1,1024,128]{2,1,0:T(8,128)S(1)}, f32[1,1024,128]{2,1,0:T(8,128)S(1)}, u32[]{:S(2)}, u32[]{:S(2)}) collective-permute-start(f32[1,1024,128]{2,1,0:T(8,128)S(1)} %collective-permute-done.3.refs_0_), channel_id=1, source_target_pairs={{0,2},{1,3},{2,0},{3,1},{4,6},{5,7},{6,4},{7,5},{8,10},{9,11},{10,... | collective-permute-start | bytes 1572872 | tf_op jit(solution)/shard_map/ppermute | solution.py:317
  21.1 8.7 %collective-permute-done.refs_0_ = f32[512,128]{1,0:T(8,128)S(1)} collective-permute-done((f32[512,128]{1,0:T(8,128)S(1)}, f32[512,128]{1,0:T(8,128)S(1)}, u32[]{:S(2)}, u32[]{:S(2)}) %collective-permute-start) | collective-permute-done | bytes 262176 | tf_op jit(solution)/shard_map/ppermute | solution.py:317
  30.4 1.5 %collective-permute-start.1 = (f32[512,128]{1,0:T(8,128)S(1)}, f32[512,128]{1,0:T(8,128)S(1)}, u32[]{:S(2)}, u32[]{:S(2)}) collective-permute-start(f32[512,128]{1,0:T(8,128)S(1)} %collective-permute-done.refs_0_), channel_id=1, source_target_pairs={{0,2},{1,3},{2,0},{3,1},{4,6},{5,7},{6,4},{7,5},{8,10},{9,11},{10,... | collective-permute-start | bytes 786440 | tf_op jit(solution)/shard_map/ppermute | solution.py:317
  32.0 6.1 %collective-permute-done.9.refs_1_ = f32[512,128]{1,0:T(8,128)S(1)} collective-permute-done((f32[512,128]{1,0:T(8,128)S(1)}, f32[512,128]{1,0:T(8,128)S(1)}, u32[]{:S(2)}, u32[]{:S(2)}) %collective-permute-start.9) | collective-permute-done | bytes 262176 | tf_op jit(solution)/shard_map/ppermute | solution.py:317
  38.0 1.3 %collective-permute-start.2 = (f32[512,128]{1,0:T(8,128)S(1)}, f32[512,128]{1,0:T(8,128)S(1)}, u32[]{:S(2)}, u32[]{:S(2)}) collective-permute-start(f32[512,128]{1,0:T(8,128)S(1)} %collective-permute-done.refs_0_), channel_id=1, source_target_pairs={{0,18},{1,19},{2,16},{3,17},{4,22},{5,23},{6,20},{7,21},{8,26},{9,... | collective-permute-start | bytes 786440 | tf_op jit(solution)/shard_map/ppermute | solution.py:317
  41.1 2.0 %shard_map.124.refs_2_.refs_4_ = f32[1024,128]{1,0:T(8,128)S(1)} custom-call(s32[1,1,96]{2,1,0:T(1,128)S(1)} %copy-done.8, s32[1,1,96]{2,1,0:T(1,128)S(1)} %copy-done.10, s32[1,1,8]{2,1,0:T(1,128)S(1)} %copy-done.12, f32[1,1024,128]{2,1,0:T(8,128)S(1)} %collective-permute-done.5.refs_0_, ...), custom_call_target="tpu_custom_call", output_to_operand_aliasing={{}: (8, {})} | custom-call | flops 1006632960 | bytes 1572864 | tf_op jit(solution)/shard_map/pallas_call | solution.py:119
  43.1 3.2 %collective-permute-done.2.refs_1_ = f32[512,128]{1,0:T(8,128)S(1)} collective-permute-done((f32[512,128]{1,0:T(8,128)S(1)}, f32[512,128]{1,0:T(8,128)S(1)}, u32[]{:S(2)}, u32[]{:S(2)}) %collective-permute-start.2) | collective-permute-done | bytes 262176 | tf_op jit(solution)/shard_map/ppermute | solution.py:317
  46.4 2.1 %shard_map.126.refs_2_ = f32[1024,128]{1,0:T(8,128)S(1)} custom-call(s32[1,1,96]{2,1,0:T(1,128)S(1)} %copy-done.8, s32[1,1,96]{2,1,0:T(1,128)S(1)} %copy-done.10, s32[1,1,8]{2,1,0:T(1,128)S(1)} %copy-done.12, f32[1,1024,128]{2,1,0:T(8,128)S(1)} %collective-permute-done.11.refs_0_, ...), custom_call_target="tpu_custom_call", output_to_operand_aliasing={{}: (7, {})} | custom-call | flops 754974720 | bytes 1179648 | tf_op jit(solution)/shard_map/pallas_call | solution.py:119
  49.9 8.1 %collective-permute-done.13.got = f32[512,128]{1,0:T(8,128)S(1)} collective-permute-done((f32[512,128]{1,0:T(8,128)S(1)}, f32[512,128]{1,0:T(8,128)S(1)}, u32[]{:S(2)}, u32[]{:S(2)}) %collective-permute-start.13) | collective-permute-done | bytes 262176 | tf_op jit(solution)/shard_map/ppermute | solution.py:317
  58.0 1.7 %shard_map.128 = (f32[1,512,256]{2,1,0:T(8,128)}, f32[136,256]{1,0:T(8,128)S(1)}, f32[136,256]{1,0:T(8,128)S(1)}) custom-call(f32[1,1024,128]{2,1,0:T(8,128)S(1)} %copy-done.3, f32[512,128]{1,0:T(8,128)S(1)} %get-tuple-element.16.kept, f32[512,128]{1,0:T(8,128)S(1)} %collective-permute-done.13.got, f32[128,256]{1,0:T(8,128)S(1)} %copy-done.5, ...), custom_call_target="tpu_custom_call" | custom-call | flops 402653184 | bytes 1572864 | tf_op jit(solution)/shard_map/pallas_call | solution.py:224
  59.7 1.4 %collective-permute-done.14 = f32[136,256]{1,0:T(8,128)S(1)} collective-permute-done((f32[136,256]{1,0:T(8,128)S(1)}, f32[136,256]{1,0:T(8,128)S(1)}, u32[]{:S(2)}, u32[]{:S(2)}) %collective-permute-start.14) | collective-permute-done | bytes 139296 | tf_op jit(solution)/shard_map/ppermute | solution.py:317
  61.5 5.4 %collective-permute-done.15 = f32[136,256]{1,0:T(8,128)S(1)} collective-permute-done((f32[136,256]{1,0:T(8,128)S(1)}, f32[136,256]{1,0:T(8,128)S(1)}, u32[]{:S(2)}, u32[]{:S(2)}) %collective-permute-start.15) | collective-permute-done | bytes 139296 | tf_op jit(solution)/shard_map/ppermute | solution.py:317
  67.9 4.1 %collective-permute-done.16 = f32[136,256]{1,0:T(8,128)S(1)} collective-permute-done((f32[136,256]{1,0:T(8,128)S(1)}, f32[136,256]{1,0:T(8,128)S(1)}, u32[]{:S(2)}, u32[]{:S(2)}) %collective-permute-start.16) | collective-permute-done | bytes 139296 | tf_op jit(solution)/shard_map/ppermute | solution.py:317
  72.1 1.5 %collective-permute-start.17 = (f32[136,256]{1,0:T(8,128)S(1)}, f32[136,256]{1,0:T(8,128)S(1)}, u32[]{:S(2)}, u32[]{:S(2)}) collective-permute-start(f32[136,256]{1,0:T(8,128)S(1)} %add.17), channel_id=1, source_target_pairs={{0,4},{1,5},{2,6},{3,7},{4,0},{5,1},{6,2},{7,3},{8,12},{9,13},{10,... | collective-permute-start | bytes 417800 | tf_op jit(solution)/shard_map/ppermute | solution.py:317
  73.5 3.7 %collective-permute-done.17 = f32[136,256]{1,0:T(8,128)S(1)} collective-permute-done((f32[136,256]{1,0:T(8,128)S(1)}, f32[136,256]{1,0:T(8,128)S(1)}, u32[]{:S(2)}, u32[]{:S(2)}) %collective-permute-start.17) | collective-permute-done | bytes 139296 | tf_op jit(solution)/shard_map/ppermute | solution.py:317
  77.2 2.3 %collective-permute-start.18 = (f32[136,256]{1,0:T(8,128)S(1)}, f32[136,256]{1,0:T(8,128)S(1)}, u32[]{:S(2)}, u32[]{:S(2)}) collective-permute-start(f32[136,256]{1,0:T(8,128)S(1)} %add.18), channel_id=1, source_target_pairs={{0,8},{1,9},{2,10},{3,11},{4,12},{5,13},{6,14},{7,15},{8,0},{9,1},... | collective-permute-start | bytes 417800 | tf_op jit(solution)/shard_map/ppermute | solution.py:317
  79.5 5.2 %collective-permute-done.18 = f32[136,256]{1,0:T(8,128)S(1)} collective-permute-done((f32[136,256]{1,0:T(8,128)S(1)}, f32[136,256]{1,0:T(8,128)S(1)}, u32[]{:S(2)}, u32[]{:S(2)}) %collective-permute-start.18) | collective-permute-done | bytes 139296 | tf_op jit(solution)/shard_map/ppermute | solution.py:317
  84.8 1.3 %collective-permute-done.19.other = f32[136,256]{1,0:T(8,128)S(1)} collective-permute-done((f32[136,256]{1,0:T(8,128)S(1)}, f32[136,256]{1,0:T(8,128)S(1)}, u32[]{:S(2)}, u32[]{:S(2)}) %collective-permute-start.19) | collective-permute-done | bytes 139296 | tf_op jit(solution)/shard_map/ppermute | solution.py:317
  (59 shorter events, 10.2 us)
Async XLA Ops:
  0.6 10.4 %collective-permute-start.4 = (f32[1,1024,128]{2,1,0:T(8,128)}, f32[1,1024,128]{2,1,0:T(8,128)S(1)}, u32[]{:S(2)}, u32[]{:S(2)}) collective-permute-start(f32[1,1024,128]{2,1,0:T(8,128)} %block.3), channel_id=1, source_target_pairs={{0,1},{1,0},{2,3},{3,2},{4,5},{5,4},{6,7},{7,6},{8,9},{9,8},{10,11... | collective-permute-start | bytes 1572872 | tf_op jit(solution)/shard_map/ppermute | solution.py:317
  1.1 17.8 %collective-permute-start.3 = (f32[1,1024,128]{2,1,0:T(8,128)}, f32[1,1024,128]{2,1,0:T(8,128)S(1)}, u32[]{:S(2)}, u32[]{:S(2)}) collective-permute-start(f32[1,1024,128]{2,1,0:T(8,128)} %block.3), channel_id=1, source_target_pairs={{0,4},{1,5},{2,6},{3,7},{4,8},{5,9},{6,10},{7,11},{8,12},{9,13},{1... | collective-permute-start | bytes 1572872 | tf_op jit(solution)/shard_map/ppermute | solution.py:317
  3.8 16.8 %collective-permute-start.6 = (f32[1,1024,128]{2,1,0:T(8,128)}, f32[1,1024,128]{2,1,0:T(8,128)S(1)}, u32[]{:S(2)}, u32[]{:S(2)}) collective-permute-start(f32[1,1024,128]{2,1,0:T(8,128)} %block.3), channel_id=1, source_target_pairs={{0,2},{1,3},{4,6},{5,7},{8,10},{9,11},{12,14},{13,15},{18,16},{19,... | collective-permute-start | bytes 1572872 | tf_op jit(solution)/shard_map/ppermute | solution.py:317
  8.3 31.0 %copy-start.8 = (s32[1,1,96]{2,1,0:T(1,128)S(1)}, s32[1,1,96]{2,1,0:T(1,128)}, u32[]{:S(2)}) copy-start(s32[1,1,96]{2,1,0:T(1,128)} %rows.9) | copy-start | bytes 1156
  8.3 31.0 %copy-start.10 = (s32[1,1,96]{2,1,0:T(1,128)S(1)}, s32[1,1,96]{2,1,0:T(1,128)}, u32[]{:S(2)}) copy-start(s32[1,1,96]{2,1,0:T(1,128)} %cols.9) | copy-start | bytes 1156
  8.3 31.0 %copy-start.12 = (s32[1,1,8]{2,1,0:T(1,128)S(1)}, s32[1,1,8]{2,1,0:T(1,128)}, u32[]{:S(2)}) copy-start(s32[1,1,8]{2,1,0:T(1,128)} %counts.9) | copy-start | bytes 100
  8.3 21.5 %collective-permute-start = (f32[512,128]{1,0:T(8,128)S(1)}, f32[512,128]{1,0:T(8,128)S(1)}, u32[]{:S(2)}, u32[]{:S(2)}) collective-permute-start(f32[512,128]{1,0:T(8,128)S(1)} %shard_map.120), channel_id=1, source_target_pairs={{0,8},{1,9},{2,10},{3,11},{4,12},{5,13},{6,14},{7,15},{8,0},{9,1},... | collective-permute-start | bytes 786440 | tf_op jit(solution)/shard_map/ppermute | solution.py:317
  14.8 24.4 %copy-start.1 = (bf16[1,1,96,128,128]{4,3,2,1,0:T(8,128)(2,1)S(1)}, bf16[1,1,96,128,128]{4,3,2,1,0:T(8,128)(2,1)}, u32[]{:S(2)}) copy-start(bf16[1,1,96,128,128]{4,3,2,1,0:T(8,128)(2,1)} %param.13) | copy-start | bytes 9437188
  18.9 21.6 %collective-permute-start.8 = (f32[1,1024,128]{2,1,0:T(8,128)S(1)}, f32[1,1024,128]{2,1,0:T(8,128)S(1)}, u32[]{:S(2)}, u32[]{:S(2)}) collective-permute-start(f32[1,1024,128]{2,1,0:T(8,128)S(1)} %collective-permute-done.3.refs_0_), channel_id=1, source_target_pairs={{0,2},{1,3},{2,0},{3,1},{4,6},{5,7},{6,4},{7,5},{8,10},{9,11},{10,... | collective-permute-start | bytes 1572872 | tf_op jit(solution)/shard_map/ppermute | solution.py:317
  20.6 20.0 %collective-permute-start.5 = (f32[1,1024,128]{2,1,0:T(8,128)S(1)}, f32[1,1024,128]{2,1,0:T(8,128)S(1)}, u32[]{:S(2)}, u32[]{:S(2)}) collective-permute-start(f32[1,1024,128]{2,1,0:T(8,128)S(1)} %collective-permute-done.3.refs_0_), channel_id=1, source_target_pairs={{0,1},{1,0},{2,3},{3,2},{4,5},{5,4},{6,7},{7,6},{8,9},{9,8},{10,11... | collective-permute-start | bytes 1572872 | tf_op jit(solution)/shard_map/ppermute | solution.py:317
  20.6 20.5 %collective-permute-start.7 = (f32[1,1024,128]{2,1,0:T(8,128)S(1)}, f32[1,1024,128]{2,1,0:T(8,128)S(1)}, u32[]{:S(2)}, u32[]{:S(2)}) collective-permute-start(f32[1,1024,128]{2,1,0:T(8,128)S(1)} %collective-permute-done.6.refs_1_), channel_id=1, source_target_pairs={{0,1},{1,0},{2,3},{3,2},{4,5},{5,4},{6,7},{7,6},{8,9},{9,8},{10,11... | collective-permute-start | bytes 1572872 | tf_op jit(solution)/shard_map/ppermute | solution.py:317
  29.8 8.2 %collective-permute-start.9 = (f32[512,128]{1,0:T(8,128)S(1)}, f32[512,128]{1,0:T(8,128)S(1)}, u32[]{:S(2)}, u32[]{:S(2)}) collective-permute-start(f32[512,128]{1,0:T(8,128)S(1)} %collective-permute-done.refs_0_), channel_id=1, source_target_pairs={{0,16},{1,17},{2,18},{3,19},{4,20},{5,21},{6,22},{7,23},{8,24},{9,... | collective-permute-start | bytes 786440 | tf_op jit(solution)/shard_map/ppermute | solution.py:317
  30.4 12.6 %collective-permute-start.1 = (f32[512,128]{1,0:T(8,128)S(1)}, f32[512,128]{1,0:T(8,128)S(1)}, u32[]{:S(2)}, u32[]{:S(2)}) collective-permute-start(f32[512,128]{1,0:T(8,128)S(1)} %collective-permute-done.refs_0_), channel_id=1, source_target_pairs={{0,2},{1,3},{2,0},{3,1},{4,6},{5,7},{6,4},{7,5},{8,10},{9,11},{10,... | collective-permute-start | bytes 786440 | tf_op jit(solution)/shard_map/ppermute | solution.py:317
  38.0 8.3 %collective-permute-start.2 = (f32[512,128]{1,0:T(8,128)S(1)}, f32[512,128]{1,0:T(8,128)S(1)}, u32[]{:S(2)}, u32[]{:S(2)}) collective-permute-start(f32[512,128]{1,0:T(8,128)S(1)} %collective-permute-done.refs_0_), channel_id=1, source_target_pairs={{0,18},{1,19},{2,16},{3,17},{4,22},{5,23},{6,20},{7,21},{8,26},{9,... | collective-permute-start | bytes 786440 | tf_op jit(solution)/shard_map/ppermute | solution.py:317
  40.5 5.9 %collective-permute-start.11 = (f32[1,1024,128]{2,1,0:T(8,128)S(1)}, f32[1,1024,128]{2,1,0:T(8,128)S(1)}, u32[]{:S(2)}, u32[]{:S(2)}) collective-permute-start(f32[1,1024,128]{2,1,0:T(8,128)S(1)} %shard_map.123.refs_3_), channel_id=1, source_target_pairs={{0,1},{1,0},{2,3},{3,2},{4,5},{5,4},{6,7},{7,6},{8,9},{9,8},{10,11... | collective-permute-start | bytes 1572872 | tf_op jit(solution)/shard_map/ppermute | solution.py:317
  40.6 5.8 %collective-permute-start.12 = (f32[1,1024,128]{2,1,0:T(8,128)S(1)}, f32[1,1024,128]{2,1,0:T(8,128)S(1)}, u32[]{:S(2)}, u32[]{:S(2)}) collective-permute-start(f32[1,1024,128]{2,1,0:T(8,128)S(1)} %collective-permute-done.8.refs_2_), channel_id=1, source_target_pairs={{0,1},{1,0},{2,3},{3,2},{4,5},{5,4},{6,7},{7,6},{8,9},{9,8},{10,11... | collective-permute-start | bytes 1572872 | tf_op jit(solution)/shard_map/ppermute | solution.py:317
  46.3 2.2 %collective-permute-start.10 = (f32[1,1024,128]{2,1,0:T(8,128)S(1)}, f32[1,1024,128]{2,1,0:T(8,128)S(1)}, u32[]{:S(2)}, u32[]{:S(2)}) collective-permute-start(f32[1,1024,128]{2,1,0:T(8,128)S(1)} %shard_map.125.refs_2_), channel_id=1, source_target_pairs={{0,1},{1,0},{2,3},{3,2},{4,5},{5,4},{6,7},{7,6},{8,9},{9,8},{10,11... | collective-permute-start | bytes 1572872 | tf_op jit(solution)/shard_map/ppermute | solution.py:317
  49.8 8.2 %collective-permute-start.13 = (f32[512,128]{1,0:T(8,128)S(1)}, f32[512,128]{1,0:T(8,128)S(1)}, u32[]{:S(2)}, u32[]{:S(2)}) collective-permute-start(f32[512,128]{1,0:T(8,128)S(1)} %get-tuple-element.17), channel_id=1, source_target_pairs={{0,16},{1,17},{2,18},{3,19},{4,20},{5,21},{6,22},{7,23},{8,24},{9,... | collective-permute-start | bytes 786440 | tf_op jit(solution)/shard_map/ppermute | solution.py:317
  59.7 1.4 %collective-permute-start.14 = (f32[136,256]{1,0:T(8,128)S(1)}, f32[136,256]{1,0:T(8,128)S(1)}, u32[]{:S(2)}, u32[]{:S(2)}) collective-permute-start(f32[136,256]{1,0:T(8,128)S(1)} %get-tuple-element.20), channel_id=1, source_target_pairs={{0,1},{1,0},{2,3},{3,2},{4,5},{5,4},{6,7},{7,6},{8,9},{9,8},{10,11... | collective-permute-start | bytes 417800 | tf_op jit(solution)/shard_map/ppermute | solution.py:317
  61.1 5.8 %collective-permute-start.15 = (f32[136,256]{1,0:T(8,128)S(1)}, f32[136,256]{1,0:T(8,128)S(1)}, u32[]{:S(2)}, u32[]{:S(2)}) collective-permute-start(f32[136,256]{1,0:T(8,128)S(1)} %add.15), channel_id=1, source_target_pairs={{0,16},{1,17},{2,18},{3,19},{4,20},{5,21},{6,22},{7,23},{8,24},{9,... | collective-permute-start | bytes 417800 | tf_op jit(solution)/shard_map/ppermute | solution.py:317
  66.9 5.1 %collective-permute-start.16 = (f32[136,256]{1,0:T(8,128)S(1)}, f32[136,256]{1,0:T(8,128)S(1)}, u32[]{:S(2)}, u32[]{:S(2)}) collective-permute-start(f32[136,256]{1,0:T(8,128)S(1)} %add.16), channel_id=1, source_target_pairs={{0,2},{1,3},{2,0},{3,1},{4,6},{5,7},{6,4},{7,5},{8,10},{9,11},{10,... | collective-permute-start | bytes 417800 | tf_op jit(solution)/shard_map/ppermute | solution.py:317
  72.1 5.1 %collective-permute-start.17 = (f32[136,256]{1,0:T(8,128)S(1)}, f32[136,256]{1,0:T(8,128)S(1)}, u32[]{:S(2)}, u32[]{:S(2)}) collective-permute-start(f32[136,256]{1,0:T(8,128)S(1)} %add.17), channel_id=1, source_target_pairs={{0,4},{1,5},{2,6},{3,7},{4,0},{5,1},{6,2},{7,3},{8,12},{9,13},{10,... | collective-permute-start | bytes 417800 | tf_op jit(solution)/shard_map/ppermute | solution.py:317
  77.2 7.5 %collective-permute-start.18 = (f32[136,256]{1,0:T(8,128)S(1)}, f32[136,256]{1,0:T(8,128)S(1)}, u32[]{:S(2)}, u32[]{:S(2)}) collective-permute-start(f32[136,256]{1,0:T(8,128)S(1)} %add.18), channel_id=1, source_target_pairs={{0,8},{1,9},{2,10},{3,11},{4,12},{5,13},{6,14},{7,15},{8,0},{9,1},... | collective-permute-start | bytes 417800 | tf_op jit(solution)/shard_map/ppermute | solution.py:317
  84.7 1.4 %collective-permute-start.19 = (f32[136,256]{1,0:T(8,128)S(1)}, f32[136,256]{1,0:T(8,128)S(1)}, u32[]{:S(2)}, u32[]{:S(2)}) collective-permute-start(f32[136,256]{1,0:T(8,128)S(1)} %add.19.total), channel_id=1, source_target_pairs={{0,1},{1,0},{2,3},{3,2},{4,5},{5,4},{6,7},{7,6},{8,9},{9,8},{10,11... | collective-permute-start | bytes 417800 | tf_op jit(solution)/shard_map/ppermute | solution.py:317
  (10 other events, 52.2 us)

commit v4 on v3

--- a/solution.py
+++ b/solution.py
@@ -54,10 +54,10 @@
     row = lax.axis_index("row")
     col = lax.axis_index("col")
     across = lax.axis_size("col")
-    if not has_acc:
+    if has_acc:
+        acc[...] = acc_in[...]
+    else:
         acc[...] = jnp.zeros_like(acc)
-    elif finish:
-        acc[...] = acc_in[...]
     width = acc.shape[1]
     side = tiles.shape[1]
     for goal, block in zip(goals, blocks):
@@ -124,7 +124,6 @@
         + ([spec(VMEM)] if acc is not None else []),
         out_specs=(spec(VMEM),) * 2 if finish else spec(VMEM),
         scratch_shapes=scratch,
-        input_output_aliases={} if finish or acc is None else {len(flat) + 4: 0},
         compiler_params=pltpu.CompilerParams(vmem_limit_bytes=LIMIT),
         cost_estimate=pl.CostEstimate(
             flops=n * slots * side * side * width * cost,

time: 87.3 us -> 87.2 us (level)
  no operation moved by 1% of the time
where the time goes in v4:
time: 87.2 us; the launch traced here: 86.7 us
  waiting for transfers between devices  49.2 us (56%)
  starting transfers between devices  21 us (24%)
  Pallas kernels  10.6 us (12%)
  local copies, waits for them, and re-layouts  4.96 us (6%)
    ppermute x20, waiting for transfers between devices, send(): return lax.ppermute(value, ('row', 'col'), pairs)  49.2 us
    ppermute x20, starting transfers between devices, send(): return lax.ppermute(value, ('row', 'col'), pairs)  21 us
    pallas_call x5, Pallas kernels, add_products(): pl.pallas_call(body, out_shape=(part, part) if finish else whole, in_spec...  8.03 us
    unnamed x28, local copies, waits for them, and re-layouts  4.96 us
  transfers between devices with their start and end apart: 20, of which 11 were waited for; matrix products, arithmetic and copies ran while one was open for 0% of the time, Pallas kernels for 8%

profile of v4, /device:TPU:0, one launch (start us, length us, event | category | flops | bytes accessed | tf_op | source)
XLA Modules:
  0.0 86.7 jit_solution(15228687007590292826)
XLA Ops:
  1.1 2.6 %collective-permute-start.3 = (f32[1,1024,128]{2,1,0:T(8,128)}, f32[1,1024,128]{2,1,0:T(8,128)S(1)}, u32[]{:S(2)}, u32[]{:S(2)}) collective-permute-start(f32[1,1024,128]{2,1,0:T(8,128)} %block.3), channel_id=1, source_target_pairs={{0,4},{1,5},{2,6},{3,7},{4,8},{5,9},{6,10},{7,11},{8,12},{9,13},{1... | collective-permute-start | bytes 1572872 | tf_op jit(solution)/shard_map/ppermute | solution.py:316
  3.8 3.4 %collective-permute-start.6 = (f32[1,1024,128]{2,1,0:T(8,128)}, f32[1,1024,128]{2,1,0:T(8,128)S(1)}, u32[]{:S(2)}, u32[]{:S(2)}) collective-permute-start(f32[1,1024,128]{2,1,0:T(8,128)} %block.3), channel_id=1, source_target_pairs={{0,2},{1,3},{4,6},{5,7},{8,10},{9,11},{12,14},{13,15},{18,16},{19,... | collective-permute-start | bytes 1572872 | tf_op jit(solution)/shard_map/ppermute | solution.py:316
  8.3 2.7 %collective-permute-start = (f32[512,128]{1,0:T(8,128)S(1)}, f32[512,128]{1,0:T(8,128)S(1)}, u32[]{:S(2)}, u32[]{:S(2)}) collective-permute-start(f32[512,128]{1,0:T(8,128)S(1)} %shard_map.120), channel_id=1, source_target_pairs={{0,8},{1,9},{2,10},{3,11},{4,12},{5,13},{6,14},{7,15},{8,0},{9,1},... | collective-permute-start | bytes 786440 | tf_op jit(solution)/shard_map/ppermute | solution.py:316
  11.0 1.9 %copy-done = bf16[1,1,96,128,128]{4,3,2,1,0:T(8,128)(2,1)S(1)} copy-done((bf16[1,1,96,128,128]{4,3,2,1,0:T(8,128)(2,1)S(1)}, bf16[1,1,96,128,128]{4,3,2,1,0:T(8,128)(2,1)}, u32[]{:S(2)}) %copy-start) | copy-done | bytes 3145752
  14.9 1.4 %shard_map.121.refs_3_ = f32[1024,128]{1,0:T(8,128)S(1)} custom-call(s32[1,1,96]{2,1,0:T(1,128)S(1)} %copy-done.7, s32[1,1,96]{2,1,0:T(1,128)S(1)} %copy-done.9, s32[1,1,8]{2,1,0:T(1,128)S(1)} %copy-done.11, f32[1,1024,128]{2,1,0:T(8,128)S(1)} %copy-done.2, f32[1,1024,128]{2,1,0:T(8,128)S(1)} %collective-permute-done.4.refs_1_, bf16[96,128,128]{2,1,0:T(8,128)(2,1)S(1)} %bitcast.1), custom_call_target="tpu_custom_call" | custom-call | flops 503316480 | bytes 786432 | tf_op jit(solution)/shard_map/pallas_call | solution.py:119
  16.3 2.7 %collective-permute-done.3.refs_0_ = f32[1,1024,128]{2,1,0:T(8,128)S(1)} collective-permute-done((f32[1,1024,128]{2,1,0:T(8,128)}, f32[1,1024,128]{2,1,0:T(8,128)S(1)}, u32[]{:S(2)}, u32[]{:S(2)}) %collective-permute-start.3) | collective-permute-done | bytes 524320 | tf_op jit(solution)/shard_map/ppermute | solution.py:316
  18.9 1.7 %collective-permute-start.8 = (f32[1,1024,128]{2,1,0:T(8,128)S(1)}, f32[1,1024,128]{2,1,0:T(8,128)S(1)}, u32[]{:S(2)}, u32[]{:S(2)}) collective-permute-start(f32[1,1024,128]{2,1,0:T(8,128)S(1)} %collective-permute-done.3.refs_0_), channel_id=1, source_target_pairs={{0,2},{1,3},{2,0},{3,1},{4,6},{5,7},{6,4},{7,5},{8,10},{9,11},{10,... | collective-permute-start | bytes 1572872 | tf_op jit(solution)/shard_map/ppermute | solution.py:316
  21.1 8.7 %collective-permute-done.refs_0_ = f32[512,128]{1,0:T(8,128)S(1)} collective-permute-done((f32[512,128]{1,0:T(8,128)S(1)}, f32[512,128]{1,0:T(8,128)S(1)}, u32[]{:S(2)}, u32[]{:S(2)}) %collective-permute-start) | collective-permute-done | bytes 262176 | tf_op jit(solution)/shard_map/ppermute | solution.py:316
  30.4 1.5 %collective-permute-start.1 = (f32[512,128]{1,0:T(8,128)S(1)}, f32[512,128]{1,0:T(8,128)S(1)}, u32[]{:S(2)}, u32[]{:S(2)}) collective-permute-start(f32[512,128]{1,0:T(8,128)S(1)} %collective-permute-done.refs_0_), channel_id=1, source_target_pairs={{0,2},{1,3},{2,0},{3,1},{4,6},{5,7},{6,4},{7,5},{8,10},{9,11},{10,... | collective-permute-start | bytes 786440 | tf_op jit(solution)/shard_map/ppermute | solution.py:316
  32.0 6.1 %collective-permute-done.9.refs_1_ = f32[512,128]{1,0:T(8,128)S(1)} collective-permute-done((f32[512,128]{1,0:T(8,128)S(1)}, f32[512,128]{1,0:T(8,128)S(1)}, u32[]{:S(2)}, u32[]{:S(2)}) %collective-permute-start.9) | collective-permute-done | bytes 262176 | tf_op jit(solution)/shard_map/ppermute | solution.py:316
  39.3 1.4 %shard_map.122.refs_2_.refs_5_ = f32[1024,128]{1,0:T(8,128)S(1)} custom-call(s32[1,1,96]{2,1,0:T(1,128)S(1)} %copy-done.8, s32[1,1,96]{2,1,0:T(1,128)S(1)} %copy-done.10, s32[1,1,8]{2,1,0:T(1,128)S(1)} %copy-done.12, f32[1,1024,128]{2,1,0:T(8,128)S(1)} %collective-permute-done.3.refs_0_, f32[1,1024,128]{2,1,0:T(8,128)S(1)} %collective-permute-done.6.refs_1_, ...), custom_call_target="tpu_custom_call" | custom-call | flops 503316480 | bytes 786432 | tf_op jit(solution)/shard_map/pallas_call | solution.py:119
  41.3 1.7 %shard_map.124.refs_2_.refs_4_ = f32[1024,128]{1,0:T(8,128)S(1)} custom-call(s32[1,1,96]{2,1,0:T(1,128)S(1)} %copy-done.8, s32[1,1,96]{2,1,0:T(1,128)S(1)} %copy-done.10, s32[1,1,8]{2,1,0:T(1,128)S(1)} %copy-done.12, f32[1,1024,128]{2,1,0:T(8,128)S(1)} %collective-permute-done.5.refs_0_, f32[1,1024,128]{2,1,0:T(8,128)S(1)} %collective-permute-done.7.refs_1_, ...), custom_call_target="tpu_custom_call" | custom-call | flops 1006632960 | bytes 1572864 | tf_op jit(solution)/shard_map/pallas_call | solution.py:119
  43.1 3.2 %collective-permute-done.2.refs_1_ = f32[512,128]{1,0:T(8,128)S(1)} collective-permute-done((f32[512,128]{1,0:T(8,128)S(1)}, f32[512,128]{1,0:T(8,128)S(1)}, u32[]{:S(2)}, u32[]{:S(2)}) %collective-permute-start.2) | collective-permute-done | bytes 262176 | tf_op jit(solution)/shard_map/ppermute | solution.py:316
  46.4 2.3 %shard_map.126.refs_2_ = f32[1024,128]{1,0:T(8,128)S(1)} custom-call(s32[1,1,96]{2,1,0:T(1,128)S(1)} %copy-done.8, s32[1,1,96]{2,1,0:T(1,128)S(1)} %copy-done.10, s32[1,1,8]{2,1,0:T(1,128)S(1)} %copy-done.12, f32[1,1024,128]{2,1,0:T(8,128)S(1)} %collective-permute-done.11.refs_0_, f32[1,1024,128]{2,1,0:T(8,128)S(1)} %collective-permute-done.12.refs_1_, ...), custom_call_target="tpu_custom_call" | custom-call | flops 754974720 | bytes 1179648 | tf_op jit(solution)/shard_map/pallas_call | solution.py:119
  50.1 7.7 %collective-permute-done.13.got = f32[512,128]{1,0:T(8,128)S(1)} collective-permute-done((f32[512,128]{1,0:T(8,128)S(1)}, f32[512,128]{1,0:T(8,128)S(1)}, u32[]{:S(2)}, u32[]{:S(2)}) %collective-permute-start.13) | collective-permute-done | bytes 262176 | tf_op jit(solution)/shard_map/ppermute | solution.py:316
  57.8 1.7 %shard_map.128 = (f32[1,512,256]{2,1,0:T(8,128)}, f32[136,256]{1,0:T(8,128)S(1)}, f32[136,256]{1,0:T(8,128)S(1)}) custom-call(f32[1,1024,128]{2,1,0:T(8,128)S(1)} %copy-done.3, f32[512,128]{1,0:T(8,128)S(1)} %get-tuple-element.16.kept, f32[512,128]{1,0:T(8,128)S(1)} %collective-permute-done.13.got, f32[128,256]{1,0:T(8,128)S(1)} %copy-done.5, ...), custom_call_target="tpu_custom_call" | custom-call | flops 402653184 | bytes 1572864 | tf_op jit(solution)/shard_map/pallas_call | solution.py:223
  59.5 1.4 %collective-permute-done.14 = f32[136,256]{1,0:T(8,128)S(1)} collective-permute-done((f32[136,256]{1,0:T(8,128)S(1)}, f32[136,256]{1,0:T(8,128)S(1)}, u32[]{:S(2)}, u32[]{:S(2)}) %collective-permute-start.14) | collective-permute-done | bytes 139296 | tf_op jit(solution)/shard_map/ppermute | solution.py:316
  61.5 5.2 %collective-permute-done.15 = f32[136,256]{1,0:T(8,128)S(1)} collective-permute-done((f32[136,256]{1,0:T(8,128)S(1)}, f32[136,256]{1,0:T(8,128)S(1)}, u32[]{:S(2)}, u32[]{:S(2)}) %collective-permute-start.15) | collective-permute-done | bytes 139296 | tf_op jit(solution)/shard_map/ppermute | solution.py:316
  67.9 3.9 %collective-permute-done.16 = f32[136,256]{1,0:T(8,128)S(1)} collective-permute-done((f32[136,256]{1,0:T(8,128)S(1)}, f32[136,256]{1,0:T(8,128)S(1)}, u32[]{:S(2)}, u32[]{:S(2)}) %collective-permute-start.16) | collective-permute-done | bytes 139296 | tf_op jit(solution)/shard_map/ppermute | solution.py:316
  71.9 1.3 %collective-permute-start.17 = (f32[136,256]{1,0:T(8,128)S(1)}, f32[136,256]{1,0:T(8,128)S(1)}, u32[]{:S(2)}, u32[]{:S(2)}) collective-permute-start(f32[136,256]{1,0:T(8,128)S(1)} %add.17), channel_id=1, source_target_pairs={{0,4},{1,5},{2,6},{3,7},{4,0},{5,1},{6,2},{7,3},{8,12},{9,13},{10,... | collective-permute-start | bytes 417800 | tf_op jit(solution)/shard_map/ppermute | solution.py:316
  73.2 3.8 %collective-permute-done.17 = f32[136,256]{1,0:T(8,128)S(1)} collective-permute-done((f32[136,256]{1,0:T(8,128)S(1)}, f32[136,256]{1,0:T(8,128)S(1)}, u32[]{:S(2)}, u32[]{:S(2)}) %collective-permute-start.17) | collective-permute-done | bytes 139296 | tf_op jit(solution)/shard_map/ppermute | solution.py:316
  77.0 2.3 %collective-permute-start.18 = (f32[136,256]{1,0:T(8,128)S(1)}, f32[136,256]{1,0:T(8,128)S(1)}, u32[]{:S(2)}, u32[]{:S(2)}) collective-permute-start(f32[136,256]{1,0:T(8,128)S(1)} %add.18), channel_id=1, source_target_pairs={{0,8},{1,9},{2,10},{3,11},{4,12},{5,13},{6,14},{7,15},{8,0},{9,1},... | collective-permute-start | bytes 417800 | tf_op jit(solution)/shard_map/ppermute | solution.py:316
  79.3 5.2 %collective-permute-done.18 = f32[136,256]{1,0:T(8,128)S(1)} collective-permute-done((f32[136,256]{1,0:T(8,128)S(1)}, f32[136,256]{1,0:T(8,128)S(1)}, u32[]{:S(2)}, u32[]{:S(2)}) %collective-permute-start.18) | collective-permute-done | bytes 139296 | tf_op jit(solution)/shard_map/ppermute | solution.py:316
  84.6 1.3 %collective-permute-done.19.other = f32[136,256]{1,0:T(8,128)S(1)} collective-permute-done((f32[136,256]{1,0:T(8,128)S(1)}, f32[136,256]{1,0:T(8,128)S(1)}, u32[]{:S(2)}, u32[]{:S(2)}) %collective-permute-start.19) | collective-permute-done | bytes 139296 | tf_op jit(solution)/shard_map/ppermute | solution.py:316
  (59 shorter events, 10.7 us)
Async XLA Ops:
  0.6 10.4 %collective-permute-start.4 = (f32[1,1024,128]{2,1,0:T(8,128)}, f32[1,1024,128]{2,1,0:T(8,128)S(1)}, u32[]{:S(2)}, u32[]{:S(2)}) collective-permute-start(f32[1,1024,128]{2,1,0:T(8,128)} %block.3), channel_id=1, source_target_pairs={{0,1},{1,0},{2,3},{3,2},{4,5},{5,4},{6,7},{7,6},{8,9},{9,8},{10,11... | collective-permute-start | bytes 1572872 | tf_op jit(solution)/shard_map/ppermute | solution.py:316
  1.1 17.8 %collective-permute-start.3 = (f32[1,1024,128]{2,1,0:T(8,128)}, f32[1,1024,128]{2,1,0:T(8,128)S(1)}, u32[]{:S(2)}, u32[]{:S(2)}) collective-permute-start(f32[1,1024,128]{2,1,0:T(8,128)} %block.3), channel_id=1, source_target_pairs={{0,4},{1,5},{2,6},{3,7},{4,8},{5,9},{6,10},{7,11},{8,12},{9,13},{1... | collective-permute-start | bytes 1572872 | tf_op jit(solution)/shard_map/ppermute | solution.py:316
  3.8 16.8 %collective-permute-start.6 = (f32[1,1024,128]{2,1,0:T(8,128)}, f32[1,1024,128]{2,1,0:T(8,128)S(1)}, u32[]{:S(2)}, u32[]{:S(2)}) collective-permute-start(f32[1,1024,128]{2,1,0:T(8,128)} %block.3), channel_id=1, source_target_pairs={{0,2},{1,3},{4,6},{5,7},{8,10},{9,11},{12,14},{13,15},{18,16},{19,... | collective-permute-start | bytes 1572872 | tf_op jit(solution)/shard_map/ppermute | solution.py:316
  8.3 31.0 %copy-start.8 = (s32[1,1,96]{2,1,0:T(1,128)S(1)}, s32[1,1,96]{2,1,0:T(1,128)}, u32[]{:S(2)}) copy-start(s32[1,1,96]{2,1,0:T(1,128)} %rows.9) | copy-start | bytes 1156
  8.3 31.0 %copy-start.10 = (s32[1,1,96]{2,1,0:T(1,128)S(1)}, s32[1,1,96]{2,1,0:T(1,128)}, u32[]{:S(2)}) copy-start(s32[1,1,96]{2,1,0:T(1,128)} %cols.9) | copy-start | bytes 1156
  8.3 31.0 %copy-start.12 = (s32[1,1,8]{2,1,0:T(1,128)S(1)}, s32[1,1,8]{2,1,0:T(1,128)}, u32[]{:S(2)}) copy-start(s32[1,1,8]{2,1,0:T(1,128)} %counts.9) | copy-start | bytes 100
  8.3 21.5 %collective-permute-start = (f32[512,128]{1,0:T(8,128)S(1)}, f32[512,128]{1,0:T(8,128)S(1)}, u32[]{:S(2)}, u32[]{:S(2)}) collective-permute-start(f32[512,128]{1,0:T(8,128)S(1)} %shard_map.120), channel_id=1, source_target_pairs={{0,8},{1,9},{2,10},{3,11},{4,12},{5,13},{6,14},{7,15},{8,0},{9,1},... | collective-permute-start | bytes 786440 | tf_op jit(solution)/shard_map/ppermute | solution.py:316
  14.8 24.4 %copy-start.1 = (bf16[1,1,96,128,128]{4,3,2,1,0:T(8,128)(2,1)S(1)}, bf16[1,1,96,128,128]{4,3,2,1,0:T(8,128)(2,1)}, u32[]{:S(2)}) copy-start(bf16[1,1,96,128,128]{4,3,2,1,0:T(8,128)(2,1)} %param.13) | copy-start | bytes 9437188
  18.9 21.8 %collective-permute-start.8 = (f32[1,1024,128]{2,1,0:T(8,128)S(1)}, f32[1,1024,128]{2,1,0:T(8,128)S(1)}, u32[]{:S(2)}, u32[]{:S(2)}) collective-permute-start(f32[1,1024,128]{2,1,0:T(8,128)S(1)} %collective-permute-done.3.refs_0_), channel_id=1, source_target_pairs={{0,2},{1,3},{2,0},{3,1},{4,6},{5,7},{6,4},{7,5},{8,10},{9,11},{10,... | collective-permute-start | bytes 1572872 | tf_op jit(solution)/shard_map/ppermute | solution.py:316
  20.6 20.3 %collective-permute-start.5 = (f32[1,1024,128]{2,1,0:T(8,128)S(1)}, f32[1,1024,128]{2,1,0:T(8,128)S(1)}, u32[]{:S(2)}, u32[]{:S(2)}) collective-permute-start(f32[1,1024,128]{2,1,0:T(8,128)S(1)} %collective-permute-done.3.refs_0_), channel_id=1, source_target_pairs={{0,1},{1,0},{2,3},{3,2},{4,5},{5,4},{6,7},{7,6},{8,9},{9,8},{10,11... | collective-permute-start | bytes 1572872 | tf_op jit(solution)/shard_map/ppermute | solution.py:316
  20.6 20.8 %collective-permute-start.7 = (f32[1,1024,128]{2,1,0:T(8,128)S(1)}, f32[1,1024,128]{2,1,0:T(8,128)S(1)}, u32[]{:S(2)}, u32[]{:S(2)}) collective-permute-start(f32[1,1024,128]{2,1,0:T(8,128)S(1)} %collective-permute-done.6.refs_1_), channel_id=1, source_target_pairs={{0,1},{1,0},{2,3},{3,2},{4,5},{5,4},{6,7},{7,6},{8,9},{9,8},{10,11... | collective-permute-start | bytes 1572872 | tf_op jit(solution)/shard_map/ppermute | solution.py:316
  29.8 8.2 %collective-permute-start.9 = (f32[512,128]{1,0:T(8,128)S(1)}, f32[512,128]{1,0:T(8,128)S(1)}, u32[]{:S(2)}, u32[]{:S(2)}) collective-permute-start(f32[512,128]{1,0:T(8,128)S(1)} %collective-permute-done.refs_0_), channel_id=1, source_target_pairs={{0,16},{1,17},{2,18},{3,19},{4,20},{5,21},{6,22},{7,23},{8,24},{9,... | collective-permute-start | bytes 786440 | tf_op jit(solution)/shard_map/ppermute | solution.py:316
  30.4 12.7 %collective-permute-start.1 = (f32[512,128]{1,0:T(8,128)S(1)}, f32[512,128]{1,0:T(8,128)S(1)}, u32[]{:S(2)}, u32[]{:S(2)}) collective-permute-start(f32[512,128]{1,0:T(8,128)S(1)} %collective-permute-done.refs_0_), channel_id=1, source_target_pairs={{0,2},{1,3},{2,0},{3,1},{4,6},{5,7},{6,4},{7,5},{8,10},{9,11},{10,... | collective-permute-start | bytes 786440 | tf_op jit(solution)/shard_map/ppermute | solution.py:316
  38.0 8.3 %collective-permute-start.2 = (f32[512,128]{1,0:T(8,128)S(1)}, f32[512,128]{1,0:T(8,128)S(1)}, u32[]{:S(2)}, u32[]{:S(2)}) collective-permute-start(f32[512,128]{1,0:T(8,128)S(1)} %collective-permute-done.refs_0_), channel_id=1, source_target_pairs={{0,18},{1,19},{2,16},{3,17},{4,22},{5,23},{6,20},{7,21},{8,26},{9,... | collective-permute-start | bytes 786440 | tf_op jit(solution)/shard_map/ppermute | solution.py:316
  40.8 5.7 %collective-permute-start.11 = (f32[1,1024,128]{2,1,0:T(8,128)S(1)}, f32[1,1024,128]{2,1,0:T(8,128)S(1)}, u32[]{:S(2)}, u32[]{:S(2)}) collective-permute-start(f32[1,1024,128]{2,1,0:T(8,128)S(1)} %shard_map.123.refs_3_), channel_id=1, source_target_pairs={{0,1},{1,0},{2,3},{3,2},{4,5},{5,4},{6,7},{7,6},{8,9},{9,8},{10,11... | collective-permute-start | bytes 1572872 | tf_op jit(solution)/shard_map/ppermute | solution.py:316
  40.8 5.6 %collective-permute-start.12 = (f32[1,1024,128]{2,1,0:T(8,128)S(1)}, f32[1,1024,128]{2,1,0:T(8,128)S(1)}, u32[]{:S(2)}, u32[]{:S(2)}) collective-permute-start(f32[1,1024,128]{2,1,0:T(8,128)S(1)} %collective-permute-done.8.refs_2_), channel_id=1, source_target_pairs={{0,1},{1,0},{2,3},{3,2},{4,5},{5,4},{6,7},{7,6},{8,9},{9,8},{10,11... | collective-permute-start | bytes 1572872 | tf_op jit(solution)/shard_map/ppermute | solution.py:316
  46.3 2.5 %collective-permute-start.10 = (f32[1,1024,128]{2,1,0:T(8,128)S(1)}, f32[1,1024,128]{2,1,0:T(8,128)S(1)}, u32[]{:S(2)}, u32[]{:S(2)}) collective-permute-start(f32[1,1024,128]{2,1,0:T(8,128)S(1)} %shard_map.125.refs_2_), channel_id=1, source_target_pairs={{0,1},{1,0},{2,3},{3,2},{4,5},{5,4},{6,7},{7,6},{8,9},{9,8},{10,11... | collective-permute-start | bytes 1572872 | tf_op jit(solution)/shard_map/ppermute | solution.py:316
  50.0 7.7 %collective-permute-start.13 = (f32[512,128]{1,0:T(8,128)S(1)}, f32[512,128]{1,0:T(8,128)S(1)}, u32[]{:S(2)}, u32[]{:S(2)}) collective-permute-start(f32[512,128]{1,0:T(8,128)S(1)} %get-tuple-element.17), channel_id=1, source_target_pairs={{0,16},{1,17},{2,18},{3,19},{4,20},{5,21},{6,22},{7,23},{8,24},{9,... | collective-permute-start | bytes 786440 | tf_op jit(solution)/shard_map/ppermute | solution.py:316
  59.5 1.4 %collective-permute-start.14 = (f32[136,256]{1,0:T(8,128)S(1)}, f32[136,256]{1,0:T(8,128)S(1)}, u32[]{:S(2)}, u32[]{:S(2)}) collective-permute-start(f32[136,256]{1,0:T(8,128)S(1)} %get-tuple-element.20), channel_id=1, source_target_pairs={{0,1},{1,0},{2,3},{3,2},{4,5},{5,4},{6,7},{7,6},{8,9},{9,8},{10,11... | collective-permute-start | bytes 417800 | tf_op jit(solution)/shard_map/ppermute | solution.py:316
  60.9 5.8 %collective-permute-start.15 = (f32[136,256]{1,0:T(8,128)S(1)}, f32[136,256]{1,0:T(8,128)S(1)}, u32[]{:S(2)}, u32[]{:S(2)}) collective-permute-start(f32[136,256]{1,0:T(8,128)S(1)} %add.15), channel_id=1, source_target_pairs={{0,16},{1,17},{2,18},{3,19},{4,20},{5,21},{6,22},{7,23},{8,24},{9,... | collective-permute-start | bytes 417800 | tf_op jit(solution)/shard_map/ppermute | solution.py:316
  66.7 5.1 %collective-permute-start.16 = (f32[136,256]{1,0:T(8,128)S(1)}, f32[136,256]{1,0:T(8,128)S(1)}, u32[]{:S(2)}, u32[]{:S(2)}) collective-permute-start(f32[136,256]{1,0:T(8,128)S(1)} %add.16), channel_id=1, source_target_pairs={{0,2},{1,3},{2,0},{3,1},{4,6},{5,7},{6,4},{7,5},{8,10},{9,11},{10,... | collective-permute-start | bytes 417800 | tf_op jit(solution)/shard_map/ppermute | solution.py:316
  71.9 5.1 %collective-permute-start.17 = (f32[136,256]{1,0:T(8,128)S(1)}, f32[136,256]{1,0:T(8,128)S(1)}, u32[]{:S(2)}, u32[]{:S(2)}) collective-permute-start(f32[136,256]{1,0:T(8,128)S(1)} %add.17), channel_id=1, source_target_pairs={{0,4},{1,5},{2,6},{3,7},{4,0},{5,1},{6,2},{7,3},{8,12},{9,13},{10,... | collective-permute-start | bytes 417800 | tf_op jit(solution)/shard_map/ppermute | solution.py:316
  77.0 7.5 %collective-permute-start.18 = (f32[136,256]{1,0:T(8,128)S(1)}, f32[136,256]{1,0:T(8,128)S(1)}, u32[]{:S(2)}, u32[]{:S(2)}) collective-permute-start(f32[136,256]{1,0:T(8,128)S(1)} %add.18), channel_id=1, source_target_pairs={{0,8},{1,9},{2,10},{3,11},{4,12},{5,13},{6,14},{7,15},{8,0},{9,1},... | collective-permute-start | bytes 417800 | tf_op jit(solution)/shard_map/ppermute | solution.py:316
  84.5 1.4 %collective-permute-start.19 = (f32[136,256]{1,0:T(8,128)S(1)}, f32[136,256]{1,0:T(8,128)S(1)}, u32[]{:S(2)}, u32[]{:S(2)}) collective-permute-start(f32[136,256]{1,0:T(8,128)S(1)} %add.19.total), channel_id=1, source_target_pairs={{0,1},{1,0},{2,3},{3,2},{4,5},{5,4},{6,7},{7,6},{8,9},{9,8},{10,11... | collective-permute-start | bytes 417800 | tf_op jit(solution)/shard_map/ppermute | solution.py:316
  (10 other events, 49.9 us)

commit v5 on v4

--- a/solution.py
+++ b/solution.py
@@ -181,17 +181,26 @@
     )(*[piece for piece, _ in pieces], *after)
 
 
+def own_kernel(block, self_weight, bias, out):
+    nodes, units = out.shape
+    own = block[0, pl.ds(pl.multiple_of(lax.axis_index("row") * nodes, nodes), nodes), :]
+    out[...] = dot3(split(own), split(self_weight[...]), ((1,), (0,))) + bias[
+        ...
+    ].reshape(1, units)
+
+
 def layer_kernel(
-    block, kept, got, self_weight, neigh_weight, bias, cotangent, output, keep, send
+    block, kept, got, from_own, neigh_weight, cotangent, output, keep, send
 ):
-    depth = self_weight.shape[0]
-    units = self_weight.shape[1]
+    depth = neigh_weight.shape[0]
+    units = neigh_weight.shape[1]
     nodes = kept.shape[0]
     own = block[0, pl.ds(pl.multiple_of(lax.axis_index("row") * nodes, nodes), nodes), :]
-    both = jnp.concatenate([own, kept[...] + got[...]], axis=1)
-    inputs = split(both)
-    weights = split(jnp.concatenate([self_weight[...], neigh_weight[...]], axis=0))
-    pre = dot3(inputs, weights, ((1,), (0,))) + bias[...].reshape(1, units)
+    aggregate = split(kept[...] + got[...])
+    inputs = [
+        jnp.concatenate(parts, axis=1) for parts in zip(split(own), aggregate)
+    ]
+    pre = from_own[...] + dot3(aggregate, split(neigh_weight[...]), ((1,), (0,)))
     root = 0.7978845608028654
     square = pre * pre
     bend = jnp.tanh(root * (pre + 0.044715 * (square * pre)))
@@ -220,10 +229,22 @@
     nodes, depth = kept.shape
     units = self_weight.shape[1]
     part = jax.ShapeDtypeStruct((depth + 8, units), F32)
+    from_own = pl.pallas_call(
+        own_kernel,
+        out_shape=jax.ShapeDtypeStruct((nodes, units), F32),
+        in_specs=[spec(VMEM)] * 3,
+        out_specs=spec(VMEM),
+        compiler_params=pltpu.CompilerParams(vmem_limit_bytes=LIMIT),
+        cost_estimate=pl.CostEstimate(
+            flops=6 * nodes * depth * units,
+            bytes_accessed=nodes * units * 4,
+            transcendentals=0,
+        ),
+    )(block, self_weight, bias)
     return pl.pallas_call(
         layer_kernel,
         out_shape=(jax.ShapeDtypeStruct((1, nodes, units), F32), part, part),
-        in_specs=[spec(VMEM)] * 7,
+        in_specs=[spec(VMEM)] * 6,
         out_specs=(spec(VMEM),) * 3,
         compiler_params=pltpu.CompilerParams(vmem_limit_bytes=LIMIT),
         cost_estimate=pl.CostEstimate(
@@ -231,7 +252,7 @@
             bytes_accessed=nodes * units * 12,
             transcendentals=nodes * units,
         ),
-    )(block, kept, got, self_weight, neigh_weight, bias, cotangent)
+    )(block, kept, got, from_own, neigh_weight, cotangent)
 
 
 def grads_kernel(total, other, grad_self, grad_neigh, grad_bias):

time: 87.2 us -> 87 us (level)
  no operation moved by 1% of the time
where the time goes in v5:
time: 87 us; the launch traced here: 86.6 us
  waiting for transfers between devices  49.1 us (56%)
  starting transfers between devices  21.1 us (24%)
  Pallas kernels  10.4 us (12%)
  local copies, waits for them, and re-layouts  4.96 us (6%)
  between operations  0.89 us (1%)
    ppermute x20, waiting for transfers between devices, send(): return lax.ppermute(value, ('row', 'col'), pairs)  49.1 us
    ppermute x20, starting transfers between devices, send(): return lax.ppermute(value, ('row', 'col'), pairs)  21.1 us
    pallas_call x5, Pallas kernels, add_products(): pl.pallas_call(body, out_shape=(part, part) if finish else whole, in_spec...  7.59 us
    unnamed x28, local copies, waits for them, and re-layouts  4.96 us
  transfers between devices with their start and end apart: 20, of which 11 were waited for; matrix products, arithmetic and copies ran while one was open for 0% of the time, Pallas kernels for 8%

profile of v5, /device:TPU:0, one launch (start us, length us, event | category | flops | bytes accessed | tf_op | source)
XLA Modules:
  0.0 86.6 jit_solution(2050381900361725898)
XLA Ops:
  1.1 2.6 %collective-permute-start.3 = (f32[1,1024,128]{2,1,0:T(8,128)}, f32[1,1024,128]{2,1,0:T(8,128)S(1)}, u32[]{:S(2)}, u32[]{:S(2)}) collective-permute-start(f32[1,1024,128]{2,1,0:T(8,128)} %block.5), channel_id=1, source_target_pairs={{0,4},{1,5},{2,6},{3,7},{4,8},{5,9},{6,10},{7,11},{8,12},{9,13},{1... | collective-permute-start | bytes 1572872 | tf_op jit(solution)/shard_map/ppermute | solution.py:337
  3.8 3.4 %collective-permute-start.6 = (f32[1,1024,128]{2,1,0:T(8,128)}, f32[1,1024,128]{2,1,0:T(8,128)S(1)}, u32[]{:S(2)}, u32[]{:S(2)}) collective-permute-start(f32[1,1024,128]{2,1,0:T(8,128)} %block.5), channel_id=1, source_target_pairs={{0,2},{1,3},{4,6},{5,7},{8,10},{9,11},{12,14},{13,15},{18,16},{19,... | collective-permute-start | bytes 1572872 | tf_op jit(solution)/shard_map/ppermute | solution.py:337
  8.3 2.7 %collective-permute-start = (f32[512,128]{1,0:T(8,128)S(1)}, f32[512,128]{1,0:T(8,128)S(1)}, u32[]{:S(2)}, u32[]{:S(2)}) collective-permute-start(f32[512,128]{1,0:T(8,128)S(1)} %shard_map.120), channel_id=1, source_target_pairs={{0,8},{1,9},{2,10},{3,11},{4,12},{5,13},{6,14},{7,15},{8,0},{9,1},... | collective-permute-start | bytes 786440 | tf_op jit(solution)/shard_map/ppermute | solution.py:337
  11.0 1.9 %copy-done = bf16[1,1,96,128,128]{4,3,2,1,0:T(8,128)(2,1)S(1)} copy-done((bf16[1,1,96,128,128]{4,3,2,1,0:T(8,128)(2,1)S(1)}, bf16[1,1,96,128,128]{4,3,2,1,0:T(8,128)(2,1)}, u32[]{:S(2)}) %copy-start) | copy-done | bytes 3145752
  14.9 1.4 %shard_map.121.refs_3_ = f32[1024,128]{1,0:T(8,128)S(1)} custom-call(s32[1,1,96]{2,1,0:T(1,128)S(1)} %copy-done.7, s32[1,1,96]{2,1,0:T(1,128)S(1)} %copy-done.9, s32[1,1,8]{2,1,0:T(1,128)S(1)} %copy-done.11, f32[1,1024,128]{2,1,0:T(8,128)S(1)} %copy-done.2, f32[1,1024,128]{2,1,0:T(8,128)S(1)} %collective-permute-done.4.refs_1_, bf16[96,128,128]{2,1,0:T(8,128)(2,1)S(1)} %bitcast.1), custom_call_target="tpu_custom_call" | custom-call | flops 503316480 | bytes 786432 | tf_op jit(solution)/shard_map/pallas_call | solution.py:119
  16.2 2.7 %collective-permute-done.3.refs_0_ = f32[1,1024,128]{2,1,0:T(8,128)S(1)} collective-permute-done((f32[1,1024,128]{2,1,0:T(8,128)}, f32[1,1024,128]{2,1,0:T(8,128)S(1)}, u32[]{:S(2)}, u32[]{:S(2)}) %collective-permute-start.3) | collective-permute-done | bytes 524320 | tf_op jit(solution)/shard_map/ppermute | solution.py:337
  18.9 1.7 %collective-permute-start.8 = (f32[1,1024,128]{2,1,0:T(8,128)S(1)}, f32[1,1024,128]{2,1,0:T(8,128)S(1)}, u32[]{:S(2)}, u32[]{:S(2)}) collective-permute-start(f32[1,1024,128]{2,1,0:T(8,128)S(1)} %collective-permute-done.3.refs_0_), channel_id=1, source_target_pairs={{0,2},{1,3},{2,0},{3,1},{4,6},{5,7},{6,4},{7,5},{8,10},{9,11},{10,... | collective-permute-start | bytes 1572872 | tf_op jit(solution)/shard_map/ppermute | solution.py:337
  21.1 8.7 %collective-permute-done.refs_0_ = f32[512,128]{1,0:T(8,128)S(1)} collective-permute-done((f32[512,128]{1,0:T(8,128)S(1)}, f32[512,128]{1,0:T(8,128)S(1)}, u32[]{:S(2)}, u32[]{:S(2)}) %collective-permute-start) | collective-permute-done | bytes 262176 | tf_op jit(solution)/shard_map/ppermute | solution.py:337
  30.4 1.5 %collective-permute-start.1 = (f32[512,128]{1,0:T(8,128)S(1)}, f32[512,128]{1,0:T(8,128)S(1)}, u32[]{:S(2)}, u32[]{:S(2)}) collective-permute-start(f32[512,128]{1,0:T(8,128)S(1)} %collective-permute-done.refs_0_), channel_id=1, source_target_pairs={{0,2},{1,3},{2,0},{3,1},{4,6},{5,7},{6,4},{7,5},{8,10},{9,11},{10,... | collective-permute-start | bytes 786440 | tf_op jit(solution)/shard_map/ppermute | solution.py:337
  32.0 6.1 %collective-permute-done.9.refs_1_ = f32[512,128]{1,0:T(8,128)S(1)} collective-permute-done((f32[512,128]{1,0:T(8,128)S(1)}, f32[512,128]{1,0:T(8,128)S(1)}, u32[]{:S(2)}, u32[]{:S(2)}) %collective-permute-start.9) | collective-permute-done | bytes 262176 | tf_op jit(solution)/shard_map/ppermute | solution.py:337
  39.3 1.4 %shard_map.122.refs_2_.refs_5_ = f32[1024,128]{1,0:T(8,128)S(1)} custom-call(s32[1,1,96]{2,1,0:T(1,128)S(1)} %copy-done.8, s32[1,1,96]{2,1,0:T(1,128)S(1)} %copy-done.10, s32[1,1,8]{2,1,0:T(1,128)S(1)} %copy-done.12, f32[1,1024,128]{2,1,0:T(8,128)S(1)} %collective-permute-done.3.refs_0_, f32[1,1024,128]{2,1,0:T(8,128)S(1)} %collective-permute-done.6.refs_1_, ...), custom_call_target="tpu_custom_call" | custom-call | flops 503316480 | bytes 786432 | tf_op jit(solution)/shard_map/pallas_call | solution.py:119
  41.3 1.5 %shard_map.124.refs_2_.refs_4_ = f32[1024,128]{1,0:T(8,128)S(1)} custom-call(s32[1,1,96]{2,1,0:T(1,128)S(1)} %copy-done.8, s32[1,1,96]{2,1,0:T(1,128)S(1)} %copy-done.10, s32[1,1,8]{2,1,0:T(1,128)S(1)} %copy-done.12, f32[1,1024,128]{2,1,0:T(8,128)S(1)} %collective-permute-done.5.refs_0_, f32[1,1024,128]{2,1,0:T(8,128)S(1)} %collective-permute-done.7.refs_1_, ...), custom_call_target="tpu_custom_call" | custom-call | flops 1006632960 | bytes 1572864 | tf_op jit(solution)/shard_map/pallas_call | solution.py:119
  42.9 3.4 %collective-permute-done.2.refs_1_ = f32[512,128]{1,0:T(8,128)S(1)} collective-permute-done((f32[512,128]{1,0:T(8,128)S(1)}, f32[512,128]{1,0:T(8,128)S(1)}, u32[]{:S(2)}, u32[]{:S(2)}) %collective-permute-start.2) | collective-permute-done | bytes 262176 | tf_op jit(solution)/shard_map/ppermute | solution.py:337
  46.4 1.9 %shard_map.126.refs_2_ = f32[1024,128]{1,0:T(8,128)S(1)} custom-call(s32[1,1,96]{2,1,0:T(1,128)S(1)} %copy-done.8, s32[1,1,96]{2,1,0:T(1,128)S(1)} %copy-done.10, s32[1,1,8]{2,1,0:T(1,128)S(1)} %copy-done.12, f32[1,1024,128]{2,1,0:T(8,128)S(1)} %collective-permute-done.11.refs_0_, f32[1,1024,128]{2,1,0:T(8,128)S(1)} %collective-permute-done.12.refs_1_, ...), custom_call_target="tpu_custom_call" | custom-call | flops 754974720 | bytes 1179648 | tf_op jit(solution)/shard_map/pallas_call | solution.py:119
  48.4 1.4 %shard_map.127 = (f32[512,128]{1,0:T(8,128)S(1)}, f32[512,128]{1,0:T(8,128)S(1)}) custom-call(s32[1,1,96]{2,1,0:T(1,128)S(1)} %copy-done.8, s32[1,1,96]{2,1,0:T(1,128)S(1)} %copy-done.10, s32[1,1,8]{2,1,0:T(1,128)S(1)} %copy-done.12, f32[1,1024,128]{2,1,0:T(8,128)S(1)} %collective-permute-done.10.refs_0_, bf16[96,128,128]{2,1,0:T(8,128)(2,1)S(1)} %bitcast.5, ...), custom_call_target="tpu_custom_call" | custom-call | flops 251658240 | bytes 393216 | tf_op jit(solution)/shard_map/pallas_call | solution.py:119
  50.3 7.5 %collective-permute-done.13.got = f32[512,128]{1,0:T(8,128)S(1)} collective-permute-done((f32[512,128]{1,0:T(8,128)S(1)}, f32[512,128]{1,0:T(8,128)S(1)}, u32[]{:S(2)}, u32[]{:S(2)}) %collective-permute-start.13) | collective-permute-done | bytes 262176 | tf_op jit(solution)/shard_map/ppermute | solution.py:337
  57.8 1.7 %shard_map.129 = (f32[1,512,256]{2,1,0:T(8,128)}, f32[136,256]{1,0:T(8,128)S(1)}, f32[136,256]{1,0:T(8,128)S(1)}) custom-call(f32[1,1024,128]{2,1,0:T(8,128)S(1)} %copy-done.3, f32[512,128]{1,0:T(8,128)S(1)} %get-tuple-element.16.kept, f32[512,128]{1,0:T(8,128)S(1)} %collective-permute-done.13.got, f32[512,256]{1,0:T(8,128)S(1)} %shard_map.128.from_own, ...), custom_call_target="tpu_custom_call" | custom-call | flops 402653184 | bytes 1572864 | tf_op jit(solution)/shard_map/pallas_call | solution.py:244
  59.4 1.4 %collective-permute-done.14 = f32[136,256]{1,0:T(8,128)S(1)} collective-permute-done((f32[136,256]{1,0:T(8,128)S(1)}, f32[136,256]{1,0:T(8,128)S(1)}, u32[]{:S(2)}, u32[]{:S(2)}) %collective-permute-start.14) | collective-permute-done | bytes 139296 | tf_op jit(solution)/shard_map/ppermute | solution.py:337
  61.2 5.4 %collective-permute-done.15 = f32[136,256]{1,0:T(8,128)S(1)} collective-permute-done((f32[136,256]{1,0:T(8,128)S(1)}, f32[136,256]{1,0:T(8,128)S(1)}, u32[]{:S(2)}, u32[]{:S(2)}) %collective-permute-start.15) | collective-permute-done | bytes 139296 | tf_op jit(solution)/shard_map/ppermute | solution.py:337
  67.8 3.9 %collective-permute-done.16 = f32[136,256]{1,0:T(8,128)S(1)} collective-permute-done((f32[136,256]{1,0:T(8,128)S(1)}, f32[136,256]{1,0:T(8,128)S(1)}, u32[]{:S(2)}, u32[]{:S(2)}) %collective-permute-start.16) | collective-permute-done | bytes 139296 | tf_op jit(solution)/shard_map/ppermute | solution.py:337
  73.1 3.8 %collective-permute-done.17 = f32[136,256]{1,0:T(8,128)S(1)} collective-permute-done((f32[136,256]{1,0:T(8,128)S(1)}, f32[136,256]{1,0:T(8,128)S(1)}, u32[]{:S(2)}, u32[]{:S(2)}) %collective-permute-start.17) | collective-permute-done | bytes 139296 | tf_op jit(solution)/shard_map/ppermute | solution.py:337
  76.9 2.6 %collective-permute-start.18 = (f32[136,256]{1,0:T(8,128)S(1)}, f32[136,256]{1,0:T(8,128)S(1)}, u32[]{:S(2)}, u32[]{:S(2)}) collective-permute-start(f32[136,256]{1,0:T(8,128)S(1)} %add.18), channel_id=1, source_target_pairs={{0,8},{1,9},{2,10},{3,11},{4,12},{5,13},{6,14},{7,15},{8,0},{9,1},... | collective-permute-start | bytes 417800 | tf_op jit(solution)/shard_map/ppermute | solution.py:337
  79.5 4.9 %collective-permute-done.18 = f32[136,256]{1,0:T(8,128)S(1)} collective-permute-done((f32[136,256]{1,0:T(8,128)S(1)}, f32[136,256]{1,0:T(8,128)S(1)}, u32[]{:S(2)}, u32[]{:S(2)}) %collective-permute-start.18) | collective-permute-done | bytes 139296 | tf_op jit(solution)/shard_map/ppermute | solution.py:337
  84.5 1.3 %collective-permute-done.19.other = f32[136,256]{1,0:T(8,128)S(1)} collective-permute-done((f32[136,256]{1,0:T(8,128)S(1)}, f32[136,256]{1,0:T(8,128)S(1)}, u32[]{:S(2)}, u32[]{:S(2)}) %collective-permute-start.19) | collective-permute-done | bytes 139296 | tf_op jit(solution)/shard_map/ppermute | solution.py:337
  (60 shorter events, 11.0 us)
Async XLA Ops:
  0.6 10.4 %collective-permute-start.4 = (f32[1,1024,128]{2,1,0:T(8,128)}, f32[1,1024,128]{2,1,0:T(8,128)S(1)}, u32[]{:S(2)}, u32[]{:S(2)}) collective-permute-start(f32[1,1024,128]{2,1,0:T(8,128)} %block.5), channel_id=1, source_target_pairs={{0,1},{1,0},{2,3},{3,2},{4,5},{5,4},{6,7},{7,6},{8,9},{9,8},{10,11... | collective-permute-start | bytes 1572872 | tf_op jit(solution)/shard_map/ppermute | solution.py:337
  1.1 17.8 %collective-permute-start.3 = (f32[1,1024,128]{2,1,0:T(8,128)}, f32[1,1024,128]{2,1,0:T(8,128)S(1)}, u32[]{:S(2)}, u32[]{:S(2)}) collective-permute-start(f32[1,1024,128]{2,1,0:T(8,128)} %block.5), channel_id=1, source_target_pairs={{0,4},{1,5},{2,6},{3,7},{4,8},{5,9},{6,10},{7,11},{8,12},{9,13},{1... | collective-permute-start | bytes 1572872 | tf_op jit(solution)/shard_map/ppermute | solution.py:337
  3.8 16.8 %collective-permute-start.6 = (f32[1,1024,128]{2,1,0:T(8,128)}, f32[1,1024,128]{2,1,0:T(8,128)S(1)}, u32[]{:S(2)}, u32[]{:S(2)}) collective-permute-start(f32[1,1024,128]{2,1,0:T(8,128)} %block.5), channel_id=1, source_target_pairs={{0,2},{1,3},{4,6},{5,7},{8,10},{9,11},{12,14},{13,15},{18,16},{19,... | collective-permute-start | bytes 1572872 | tf_op jit(solution)/shard_map/ppermute | solution.py:337
  8.3 31.0 %copy-start.8 = (s32[1,1,96]{2,1,0:T(1,128)S(1)}, s32[1,1,96]{2,1,0:T(1,128)}, u32[]{:S(2)}) copy-start(s32[1,1,96]{2,1,0:T(1,128)} %rows.9) | copy-start | bytes 1156
  8.3 31.0 %copy-start.10 = (s32[1,1,96]{2,1,0:T(1,128)S(1)}, s32[1,1,96]{2,1,0:T(1,128)}, u32[]{:S(2)}) copy-start(s32[1,1,96]{2,1,0:T(1,128)} %cols.9) | copy-start | bytes 1156
  8.3 31.0 %copy-start.12 = (s32[1,1,8]{2,1,0:T(1,128)S(1)}, s32[1,1,8]{2,1,0:T(1,128)}, u32[]{:S(2)}) copy-start(s32[1,1,8]{2,1,0:T(1,128)} %counts.9) | copy-start | bytes 100
  8.3 21.5 %collective-permute-start = (f32[512,128]{1,0:T(8,128)S(1)}, f32[512,128]{1,0:T(8,128)S(1)}, u32[]{:S(2)}, u32[]{:S(2)}) collective-permute-start(f32[512,128]{1,0:T(8,128)S(1)} %shard_map.120), channel_id=1, source_target_pairs={{0,8},{1,9},{2,10},{3,11},{4,12},{5,13},{6,14},{7,15},{8,0},{9,1},... | collective-permute-start | bytes 786440 | tf_op jit(solution)/shard_map/ppermute | solution.py:337
  14.8 24.4 %copy-start.1 = (bf16[1,1,96,128,128]{4,3,2,1,0:T(8,128)(2,1)S(1)}, bf16[1,1,96,128,128]{4,3,2,1,0:T(8,128)(2,1)}, u32[]{:S(2)}) copy-start(bf16[1,1,96,128,128]{4,3,2,1,0:T(8,128)(2,1)} %param.13) | copy-start | bytes 9437188
  18.9 21.8 %collective-permute-start.8 = (f32[1,1024,128]{2,1,0:T(8,128)S(1)}, f32[1,1024,128]{2,1,0:T(8,128)S(1)}, u32[]{:S(2)}, u32[]{:S(2)}) collective-permute-start(f32[1,1024,128]{2,1,0:T(8,128)S(1)} %collective-permute-done.3.refs_0_), channel_id=1, source_target_pairs={{0,2},{1,3},{2,0},{3,1},{4,6},{5,7},{6,4},{7,5},{8,10},{9,11},{10,... | collective-permute-start | bytes 1572872 | tf_op jit(solution)/shard_map/ppermute | solution.py:337
  20.6 20.3 %collective-permute-start.5 = (f32[1,1024,128]{2,1,0:T(8,128)S(1)}, f32[1,1024,128]{2,1,0:T(8,128)S(1)}, u32[]{:S(2)}, u32[]{:S(2)}) collective-permute-start(f32[1,1024,128]{2,1,0:T(8,128)S(1)} %collective-permute-done.3.refs_0_), channel_id=1, source_target_pairs={{0,1},{1,0},{2,3},{3,2},{4,5},{5,4},{6,7},{7,6},{8,9},{9,8},{10,11... | collective-permute-start | bytes 1572872 | tf_op jit(solution)/shard_map/ppermute | solution.py:337
  20.6 20.8 %collective-permute-start.7 = (f32[1,1024,128]{2,1,0:T(8,128)S(1)}, f32[1,1024,128]{2,1,0:T(8,128)S(1)}, u32[]{:S(2)}, u32[]{:S(2)}) collective-permute-start(f32[1,1024,128]{2,1,0:T(8,128)S(1)} %collective-permute-done.6.refs_1_), channel_id=1, source_target_pairs={{0,1},{1,0},{2,3},{3,2},{4,5},{5,4},{6,7},{7,6},{8,9},{9,8},{10,11... | collective-permute-start | bytes 1572872 | tf_op jit(solution)/shard_map/ppermute | solution.py:337
  29.8 8.2 %collective-permute-start.9 = (f32[512,128]{1,0:T(8,128)S(1)}, f32[512,128]{1,0:T(8,128)S(1)}, u32[]{:S(2)}, u32[]{:S(2)}) collective-permute-start(f32[512,128]{1,0:T(8,128)S(1)} %collective-permute-done.refs_0_), channel_id=1, source_target_pairs={{0,16},{1,17},{2,18},{3,19},{4,20},{5,21},{6,22},{7,23},{8,24},{9,... | collective-permute-start | bytes 786440 | tf_op jit(solution)/shard_map/ppermute | solution.py:337
  30.4 12.4 %collective-permute-start.1 = (f32[512,128]{1,0:T(8,128)S(1)}, f32[512,128]{1,0:T(8,128)S(1)}, u32[]{:S(2)}, u32[]{:S(2)}) collective-permute-start(f32[512,128]{1,0:T(8,128)S(1)} %collective-permute-done.refs_0_), channel_id=1, source_target_pairs={{0,2},{1,3},{2,0},{3,1},{4,6},{5,7},{6,4},{7,5},{8,10},{9,11},{10,... | collective-permute-start | bytes 786440 | tf_op jit(solution)/shard_map/ppermute | solution.py:337
  38.0 8.3 %collective-permute-start.2 = (f32[512,128]{1,0:T(8,128)S(1)}, f32[512,128]{1,0:T(8,128)S(1)}, u32[]{:S(2)}, u32[]{:S(2)}) collective-permute-start(f32[512,128]{1,0:T(8,128)S(1)} %collective-permute-done.refs_0_), channel_id=1, source_target_pairs={{0,18},{1,19},{2,16},{3,17},{4,22},{5,23},{6,20},{7,21},{8,26},{9,... | collective-permute-start | bytes 786440 | tf_op jit(solution)/shard_map/ppermute | solution.py:337
  40.8 5.7 %collective-permute-start.11 = (f32[1,1024,128]{2,1,0:T(8,128)S(1)}, f32[1,1024,128]{2,1,0:T(8,128)S(1)}, u32[]{:S(2)}, u32[]{:S(2)}) collective-permute-start(f32[1,1024,128]{2,1,0:T(8,128)S(1)} %shard_map.123.refs_3_), channel_id=1, source_target_pairs={{0,1},{1,0},{2,3},{3,2},{4,5},{5,4},{6,7},{7,6},{8,9},{9,8},{10,11... | collective-permute-start | bytes 1572872 | tf_op jit(solution)/shard_map/ppermute | solution.py:337
  40.8 5.6 %collective-permute-start.12 = (f32[1,1024,128]{2,1,0:T(8,128)S(1)}, f32[1,1024,128]{2,1,0:T(8,128)S(1)}, u32[]{:S(2)}, u32[]{:S(2)}) collective-permute-start(f32[1,1024,128]{2,1,0:T(8,128)S(1)} %collective-permute-done.8.refs_2_), channel_id=1, source_target_pairs={{0,1},{1,0},{2,3},{3,2},{4,5},{5,4},{6,7},{7,6},{8,9},{9,8},{10,11... | collective-permute-start | bytes 1572872 | tf_op jit(solution)/shard_map/ppermute | solution.py:337
  46.3 2.0 %collective-permute-start.10 = (f32[1,1024,128]{2,1,0:T(8,128)S(1)}, f32[1,1024,128]{2,1,0:T(8,128)S(1)}, u32[]{:S(2)}, u32[]{:S(2)}) collective-permute-start(f32[1,1024,128]{2,1,0:T(8,128)S(1)} %shard_map.125.refs_2_), channel_id=1, source_target_pairs={{0,1},{1,0},{2,3},{3,2},{4,5},{5,4},{6,7},{7,6},{8,9},{9,8},{10,11... | collective-permute-start | bytes 1572872 | tf_op jit(solution)/shard_map/ppermute | solution.py:337
  49.8 8.0 %collective-permute-start.13 = (f32[512,128]{1,0:T(8,128)S(1)}, f32[512,128]{1,0:T(8,128)S(1)}, u32[]{:S(2)}, u32[]{:S(2)}) collective-permute-start(f32[512,128]{1,0:T(8,128)S(1)} %get-tuple-element.17), channel_id=1, source_target_pairs={{0,16},{1,17},{2,18},{3,19},{4,20},{5,21},{6,22},{7,23},{8,24},{9,... | collective-permute-start | bytes 786440 | tf_op jit(solution)/shard_map/ppermute | solution.py:337
  59.4 1.4 %collective-permute-start.14 = (f32[136,256]{1,0:T(8,128)S(1)}, f32[136,256]{1,0:T(8,128)S(1)}, u32[]{:S(2)}, u32[]{:S(2)}) collective-permute-start(f32[136,256]{1,0:T(8,128)S(1)} %get-tuple-element.20), channel_id=1, source_target_pairs={{0,1},{1,0},{2,3},{3,2},{4,5},{5,4},{6,7},{7,6},{8,9},{9,8},{10,11... | collective-permute-start | bytes 417800 | tf_op jit(solution)/shard_map/ppermute | solution.py:337
  60.8 5.8 %collective-permute-start.15 = (f32[136,256]{1,0:T(8,128)S(1)}, f32[136,256]{1,0:T(8,128)S(1)}, u32[]{:S(2)}, u32[]{:S(2)}) collective-permute-start(f32[136,256]{1,0:T(8,128)S(1)} %add.15), channel_id=1, source_target_pairs={{0,16},{1,17},{2,18},{3,19},{4,20},{5,21},{6,22},{7,23},{8,24},{9,... | collective-permute-start | bytes 417800 | tf_op jit(solution)/shard_map/ppermute | solution.py:337
  66.6 5.1 %collective-permute-start.16 = (f32[136,256]{1,0:T(8,128)S(1)}, f32[136,256]{1,0:T(8,128)S(1)}, u32[]{:S(2)}, u32[]{:S(2)}) collective-permute-start(f32[136,256]{1,0:T(8,128)S(1)} %add.16), channel_id=1, source_target_pairs={{0,2},{1,3},{2,0},{3,1},{4,6},{5,7},{6,4},{7,5},{8,10},{9,11},{10,... | collective-permute-start | bytes 417800 | tf_op jit(solution)/shard_map/ppermute | solution.py:337
  71.8 5.1 %collective-permute-start.17 = (f32[136,256]{1,0:T(8,128)S(1)}, f32[136,256]{1,0:T(8,128)S(1)}, u32[]{:S(2)}, u32[]{:S(2)}) collective-permute-start(f32[136,256]{1,0:T(8,128)S(1)} %add.17), channel_id=1, source_target_pairs={{0,4},{1,5},{2,6},{3,7},{4,0},{5,1},{6,2},{7,3},{8,12},{9,13},{10,... | collective-permute-start | bytes 417800 | tf_op jit(solution)/shard_map/ppermute | solution.py:337
  76.9 7.5 %collective-permute-start.18 = (f32[136,256]{1,0:T(8,128)S(1)}, f32[136,256]{1,0:T(8,128)S(1)}, u32[]{:S(2)}, u32[]{:S(2)}) collective-permute-start(f32[136,256]{1,0:T(8,128)S(1)} %add.18), channel_id=1, source_target_pairs={{0,8},{1,9},{2,10},{3,11},{4,12},{5,13},{6,14},{7,15},{8,0},{9,1},... | collective-permute-start | bytes 417800 | tf_op jit(solution)/shard_map/ppermute | solution.py:337
  84.5 1.4 %collective-permute-start.19 = (f32[136,256]{1,0:T(8,128)S(1)}, f32[136,256]{1,0:T(8,128)S(1)}, u32[]{:S(2)}, u32[]{:S(2)}) collective-permute-start(f32[136,256]{1,0:T(8,128)S(1)} %add.19.total), channel_id=1, source_target_pairs={{0,1},{1,0},{2,3},{3,2},{4,5},{5,4},{6,7},{7,6},{8,9},{9,8},{10,11... | collective-permute-start | bytes 417800 | tf_op jit(solution)/shard_map/ppermute | solution.py:337
  (10 other events, 28.5 us)
